TPU v7x, 128 devices: a whole 4x4x4 slice. The times are simulated.
128 devices in a mesh: lat: 8 (over y, core), lon: 16 (over x, z).
Axes of the slice: x: 4, y: 4, z: 4, core: 2. Of those that a mesh axis runs over, the one named last changes fastest.
Arguments:
- fields: bfloat16 [80, 512, 2048], P(None, 'lat', 'lon'), may hold values from -6 to 6
- depart_lists: int32 [128, 16, 2], P('lat', 'lon'), may hold values from 0 to 2047, as said below
- stencil_offsets: int32 [512, 2048], P('lat', 'lon'), may hold values from 0 to 4
- interp_weights: float32 [4, 512, 2048], P(None, 'lat', 'lon'), may hold values from -0.07 to 1
- diag_coef: float32 [512, 2048], P('lat', 'lon'), may hold values from 0.05 to 2
- level_scale: float32 [16], replicated, may hold values from 0.5 to 4
Outputs:
- advected: bfloat16 [64, 512, 2048], P(None, 'lat', 'lon')
- pressure: float32 [16, 512, 2048], P(None, 'lat', 'lon')
- residual: float32 [16, 512, 2048], P(None, 'lat', 'lon')
Inputs may be any that keep to these rules, and one draw needn't show every extreme that they name: `depart_lists`: the entries of a reader device name tiles of its own band or the bands next to it, and of its own sector, the two sectors next to it (periodic in longitude), or, for devices of the first and last band only, the sector across the pole (own sector + 8, counted round); every such polar device names that sector at least once. Among the 32 entries of one device, exactly 16 name tiles of one sector, and each other sector is named fewer than 16 times.
All inputs are finite; a program needn't handle non-finite values.
Results may differ from a plain program's by a relative error of at most 0.0004.
Values may be sent and summed in bfloat16 or wider, within the bound.
No kernel may reach another device: no remote copies, remote signals or barrier semaphores. Data moves between devices by JAX's collectives and lax.ppermute only.
A program may use at most 128 MiB of HBM per device.

v0:
```python
import jax
import jax.numpy as jnp
from jax import lax
from jax.sharding import PartitionSpec as P

TILE_ROWS = 4
SOURCES = 2
ITERS = 2


def padded(block, sides, width, periodic):
    for axis, dim in sides:
        count = lax.axis_size(axis)
        forward = [(i, i + 1) for i in range(count - 1)]
        if periodic:
            forward.append((count - 1, 0))
        backward = [(target, source) for source, target in forward]
        low = lax.ppermute(
            lax.slice_in_dim(block, block.shape[dim] - width, None, axis=dim), axis, forward
        )
        high = lax.ppermute(lax.slice_in_dim(block, 0, width, axis=dim), axis, backward)
        block = jnp.concatenate([low, block, high], axis=dim)
    return block


def level_inner(first, second):
    return jnp.sum(first * second, axis=(1, 2))


def operate(field, coef):
    rim_rows = padded(field, (("lat", 1),), 1, False)
    rim_cols = padded(field, (("lon", 2),), 1, True)
    beside = rim_rows[:, 2:, :] + rim_rows[:, :-2, :]
    beside = beside + rim_cols[:, :, 2:] + rim_cols[:, :, :-2]
    return coef * field - beside


def norm_sum(residual, smoothed):
    return lax.psum(level_inner(residual, smoothed), ("lat", "lon"))


def on_device(fields, depart_lists, stencil_offsets, interp_weights, diag_coef, level_scale):
    field_count, row_count, col_count = fields.shape
    tile_count = row_count // TILE_ROWS
    level_count = level_scale.shape[0]
    lon_count = lax.axis_size("lon")
    most = tile_count * SOURCES // 2
    band_here = lax.axis_index("lat")
    wanted = depart_lists[:, 0, :].reshape(-1)
    owner = wanted // tile_count
    owner_band = owner // lon_count
    owner_sector = owner % lon_count
    ext_ids = (owner_band - band_here + 1) * tile_count + wanted % tile_count
    band = padded(fields, (("lat", 1),), row_count, False)
    span = SOURCES * TILE_ROWS
    member = (owner_sector[:, None] == jnp.arange(lon_count, dtype=jnp.int32)[None, :]).astype(
        jnp.int32
    )
    earlier = jnp.cumsum(member, axis=0) - member
    places = owner_sector * most + jnp.sum(earlier * member, axis=1)
    request = jnp.zeros((lon_count * most,), jnp.int32).at[places].set(ext_ids)
    asked = lax.all_to_all(request, "lon", split_axis=0, concat_axis=0, tiled=True)
    blocks = band.reshape(field_count, 3 * tile_count, TILE_ROWS * col_count)
    packed = jnp.take(blocks, asked, axis=1)
    arrived = lax.all_to_all(packed, "lon", split_axis=1, concat_axis=1, tiled=True)
    source = jnp.take(arrived, places, axis=1).reshape(field_count, tile_count, span, col_count)
    offsets = stencil_offsets.reshape(tile_count, TILE_ROWS, col_count)
    weights = interp_weights.reshape(4, tile_count, TILE_ROWS, col_count)
    summed = jnp.zeros((field_count, tile_count, TILE_ROWS, col_count), jnp.float32)
    for source_row in range(span):
        coeff = jnp.zeros((tile_count, TILE_ROWS, col_count), jnp.float32)
        for point in range(4):
            coeff = coeff + jnp.where(offsets + point == source_row, weights[point], 0.0)
        row_values = source[:, :, source_row, :].astype(jnp.float32)
        summed = summed + coeff[None] * row_values[:, :, None, :]
    interp = summed.reshape(field_count, row_count, col_count)
    advected = interp[: 4 * level_count].astype(jnp.bfloat16)
    rhs = interp[4 * level_count :] + 0.5 * interp[2 * level_count : 3 * level_count]
    coef = 4.0 + diag_coef[None, :, :] * level_scale[:, None, None]
    pressure = jnp.zeros_like(rhs)
    residual = rhs
    smoothed = residual / coef
    direction = smoothed
    norm_now = norm_sum(residual, smoothed)
    for sweep in range(ITERS):
        image = operate(direction, coef)
        curvature = lax.psum(level_inner(direction, image), ("lat", "lon"))
        step_size = norm_now / curvature
        pressure = pressure + step_size[:, None, None] * direction
        residual = residual - step_size[:, None, None] * image
        if sweep + 1 < ITERS:
            smoothed = residual / coef
            norm_next = norm_sum(residual, smoothed)
            direction = smoothed + (norm_next / norm_now)[:, None, None] * direction
            norm_now = norm_next
    return (advected, pressure, residual)


def solution(mesh):
    placed = (
        P(None, "lat", "lon"),
        P("lat", "lon", None),
        P("lat", "lon"),
        P(None, "lat", "lon"),
        P("lat", "lon"),
        P(),
    )
    return jax.shard_map(
        on_device,
        mesh=mesh,
        in_specs=placed,
        out_specs=(P(None, "lat", "lon"), P(None, "lat", "lon"), P(None, "lat", "lon")),
        check_vma=False,
    )
```

profile of v0, /device:TPU:1, one launch (start us, length us, event | category | flops | bytes accessed | tf_op | source)
XLA Modules:
  0.0 718.9 jit_solution(4394746860073545904)
XLA Ops:
  0.6 3.3 collective-permute-start.1
  4.0 3.2 collective-permute-start
  7.2 0.8 copy.22
  8.5 0.7 scatter_custom_fusion
  9.2 13.8 %all_to_all.20 = s32[16,16,1]{1,2,0:T(1,128)S(1)} all-to-all(s32[16,16,1]{1,2,0:T(1,128)S(1)} %bitcast.137), channel_id=1, replica_groups=mesh['lat'=8,'lon'=16] {'lon'}, dimensions={0} | all-to-all | bytes 2048 | tf_op jit(solution)/shard_map/all_to_all | solution.py:62
  24.5 3.2 pad_maximum_fusion
  27.6 7.2 reshape.587
  34.8 6.2 copy.27
  41.0 12.4 %gather_fusion = bf16[256,80,512]{2,1,0:T(8,128)(2,1)} fusion(bf16[80,48,512]{2,0,1:T(8,128)(2,1)} %copy.27, s32[1024]{0:T(1024)S(1)} %pad_clamp_fusion.1), kind=kCustom, calls=%fused_computation | custom fusion | bytes 41944064 | tf_op jit(solution)/shard_map/jit(_take)/gather | solution.py:64
  53.4 17.7 %select_bitcast_fusion = bf16[80,256,512]{2,0,1:T(8,128)(2,1)} fusion(bf16[256,80,512]{2,1,0:T(8,128)(2,1)} %gather_fusion, pred[256]{0:T(512)(128)(4,1)S(1)} %compare_and_fusion), kind=kLoop, calls=%fused_computation.3 | loop fusion | flops 10485760 | bytes 41943296 | tf_op jit(solution)/shard_map/jit(_take)/select_n | solution.py:64
  71.1 5.7 all-to-all-start.1
  77.6 374.3 %all-to-all-done.1 = bf16[80,256,512]{2,0,1:T(8,128)(2,1)} async-done(((bf16[80,256,512]{2,0,1:T(8,128)(2,1)}), bf16[80,256,512]{2,0,1:T(8,128)(2,1)}, u32[]{:S(2)}, u32[]{:S(2)}) %all-to-all-start.1) | async-done | bytes 20971552 | tf_op jit(solution)/shard_map/all_to_all | solution.py:65
  451.9 7.7 %gather_fusion.1 = bf16[32,80,512]{2,1,0:T(8,128)(2,1)S(1)} fusion(bf16[80,256,512]{2,0,1:T(8,128)(2,1)} %all-to-all-done.1, s32[1024]{0:T(1024)S(1)} %pad_clamp_fusion), kind=kCustom, calls=%fused_computation.1 | custom fusion | bytes 5243008 | tf_op jit(solution)/shard_map/jit(_take)/gather | solution.py:66
  459.6 3.0 copy.28
  462.6 4.1 gather.12
  467.0 3.9 slice_convert_fusion.8
  470.9 2.9 multiply_add_fusion
  474.5 1.9 collective-permute-start.3
  476.5 2.8 collective-permute-start.2
  479.5 3.0 collective-permute-start.5
  482.5 1.9 collective-permute-start.4
  484.4 12.2 %collective-permute-done.5 = f32[16,64,1]{2,1,0:T(8,128)S(1)} collective-permute-done((f32[16,64,1]{2,1,0:T(8,128)S(1)}, f32[16,64,1]{2,1,0:T(8,128)S(1)}, u32[]{:S(2)}, u32[]{:S(2)}) %collective-permute-start.5) | collective-permute-done | bytes 4128 | tf_op jit(solution)/shard_map/ppermute | solution.py:18
  497.2 64.7 %all-reduce = (f32[16]{0:T(128)S(1)}, f32[16]{0:T(128)S(1)}) all-reduce(f32[16]{0:T(128)S(1)} %get-tuple-element.7, f32[16]{0:T(128)S(1)} %multiply_reduce_fusion.2), channel_id=1, replica_groups=mesh['lat'=8,'lon'=16] {'lat','lon'}, use_global_device_ids=true, to_apply=%region_4.5 | all-reduce | flops 32 | bytes 256 | tf_op jit(solution)/shard_map/psum | solution.py:39
  561.9 0.7 multiply_reduce_fusion.1
  562.6 64.2 %psum.30 = f32[16]{0:T(128)S(1)} all-reduce(f32[16]{0:T(128)S(1)} %get-tuple-element.5), channel_id=1, replica_groups=mesh['lat'=8,'lon'=16] {'lat','lon'}, use_global_device_ids=true, to_apply=%region_8.9 | all-reduce | flops 16 | bytes 128 | tf_op jit(solution)/shard_map/psum | solution.py:39
  627.1 1.9 collective-permute-start.7
  629.0 2.4 collective-permute-start.6
  631.9 4.5 collective-permute-start.8
  636.5 12.2 %collective-permute-done.9 = f32[16,64,1]{2,1,0:T(8,128)S(1)} collective-permute-done((f32[16,64,1]{2,1,0:T(8,128)S(1)}, f32[16,64,1]{2,1,0:T(8,128)S(1)}, u32[]{:S(2)}, u32[]{:S(2)}) %collective-permute-start.9) | collective-permute-done | bytes 4128 | tf_op jit(solution)/shard_map/ppermute | solution.py:18
  649.3 3.0 slice.204
  652.3 65.1 %psum.31 = f32[16]{0:T(128)S(1)} all-reduce(f32[16]{0:T(128)S(1)} %multiply_reduce_fusion), channel_id=1, replica_groups=mesh['lat'=8,'lon'=16] {'lat','lon'}, use_global_device_ids=true, to_apply=%region_10.11 | all-reduce | flops 16 | bytes 128 | tf_op jit(solution)/shard_map/psum | solution.py:87
  717.4 1.5 multiply_subtract_fusion
  (61 shorter events, 6.1 us)
Async XLA Ops:
  0.6 23.8 %collective-permute-start.1 = (bf16[80,64,128]{2,1,0:T(8,128)(2,1)}, bf16[80,64,128]{2,1,0:T(8,128)(2,1)S(1)}, u32[]{:S(2)}, u32[]{:S(2)}) collective-permute-start(bf16[80,64,128]{2,1,0:T(8,128)(2,1)} %param.6), channel_id=1, source_target_pairs={{16,0},{32,16},{48,32},{64,48},{80,64},{96,80},{112,96},{17,1},{33... | collective-permute-start | bytes 3932168 | tf_op jit(solution)/shard_map/ppermute | solution.py:21
  4.0 20.5 %collective-permute-start = (bf16[80,64,128]{2,1,0:T(8,128)(2,1)}, bf16[80,64,128]{2,1,0:T(8,128)(2,1)S(1)}, u32[]{:S(2)}, u32[]{:S(2)}) collective-permute-start(bf16[80,64,128]{2,1,0:T(8,128)(2,1)} %param.6), channel_id=1, source_target_pairs={{0,16},{16,32},{32,48},{48,64},{64,80},{80,96},{96,112},{1,17},{17... | collective-permute-start | bytes 3932168 | tf_op jit(solution)/shard_map/ppermute | solution.py:18
  71.1 5.8 copy-start.5
  71.1 6.0 copy-start.2
  71.1 6.0 copy-start.3
  71.1 380.9 %all-to-all-start.1 = ((bf16[80,256,512]{2,0,1:T(8,128)(2,1)}), bf16[80,256,512]{2,0,1:T(8,128)(2,1)}, u32[]{:S(2)}, u32[]{:S(2)}) async-start(bf16[80,256,512]{2,0,1:T(8,128)(2,1)} %select_bitcast_fusion), calls=%async_computation.1 | async-start | bytes 41943040 | tf_op jit(solution)/shard_map/all_to_all | solution.py:65
  470.9 3.0 copy-start.1
  470.9 3.0 copy-start.4
  473.9 23.3 %copy-start = (f32[80,16,4,128]{3,2,1,0:T(4,128)}, f32[80,16,4,128]{3,2,1,0:T(4,128)S(1)}, u32[]{:S(2)}) copy-start(f32[80,16,4,128]{3,2,1,0:T(4,128)S(1)} %multiply_add_fusion) | copy-start | bytes 7864324
  474.5 22.0 %collective-permute-start.3 = (f32[16,1,128]{2,1,0:T(1,128)S(1)}, f32[16,1,128]{2,1,0:T(1,128)S(1)}, u32[]{:S(2)}, u32[]{:S(2)}) collective-permute-start(f32[16,1,128]{2,1,0:T(1,128)S(1)} %get-tuple-element.26), channel_id=1, source_target_pairs={{0,16},{16,32},{32,48},{48,64},{64,80},{80,96},{96,112},{1,17},{17... | collective-permute-start | bytes 24584 | tf_op jit(solution)/shard_map/ppermute | solution.py:18
  476.5 20.0 %collective-permute-start.2 = (f32[16,1,128]{2,1,0:T(1,128)S(1)}, f32[16,1,128]{2,1,0:T(1,128)S(1)}, u32[]{:S(2)}, u32[]{:S(2)}) collective-permute-start(f32[16,1,128]{2,1,0:T(1,128)S(1)} %get-tuple-element.25), channel_id=1, source_target_pairs={{16,0},{32,16},{48,32},{64,48},{80,64},{96,80},{112,96},{17,1},{33... | collective-permute-start | bytes 24584 | tf_op jit(solution)/shard_map/ppermute | solution.py:21
  479.5 17.0 %collective-permute-start.5 = (f32[16,64,1]{2,1,0:T(8,128)S(1)}, f32[16,64,1]{2,1,0:T(8,128)S(1)}, u32[]{:S(2)}, u32[]{:S(2)}) collective-permute-start(f32[16,64,1]{2,1,0:T(8,128)S(1)} %get-tuple-element.28), channel_id=1, source_target_pairs={{0,1},{1,2},{2,3},{3,4},{4,5},{5,6},{6,7},{7,8},{8,9},{9,10},{10,1... | collective-permute-start | bytes 12296 | tf_op jit(solution)/shard_map/ppermute | solution.py:18
  482.5 14.1 %collective-permute-start.4 = (f32[16,64,1]{2,1,0:T(8,128)S(1)}, f32[16,64,1]{2,1,0:T(8,128)S(1)}, u32[]{:S(2)}, u32[]{:S(2)}) collective-permute-start(f32[16,64,1]{2,1,0:T(8,128)S(1)} %get-tuple-element.27), channel_id=1, source_target_pairs={{1,0},{2,1},{3,2},{4,3},{5,4},{6,5},{7,6},{8,7},{9,8},{10,9},{11,1... | collective-permute-start | bytes 12296 | tf_op jit(solution)/shard_map/ppermute | solution.py:21
  627.1 21.6 %collective-permute-start.7 = (f32[16,1,128]{2,1,0:T(1,128)S(1)}, f32[16,1,128]{2,1,0:T(1,128)S(1)}, u32[]{:S(2)}, u32[]{:S(2)}) collective-permute-start(f32[16,1,128]{2,1,0:T(1,128)S(1)} %get-tuple-element.22), channel_id=1, source_target_pairs={{0,16},{16,32},{32,48},{48,64},{64,80},{80,96},{96,112},{1,17},{17... | collective-permute-start | bytes 24584 | tf_op jit(solution)/shard_map/ppermute | solution.py:18
  629.0 19.6 %collective-permute-start.6 = (f32[16,1,128]{2,1,0:T(1,128)S(1)}, f32[16,1,128]{2,1,0:T(1,128)S(1)}, u32[]{:S(2)}, u32[]{:S(2)}) collective-permute-start(f32[16,1,128]{2,1,0:T(1,128)S(1)} %get-tuple-element.21), channel_id=1, source_target_pairs={{16,0},{32,16},{48,32},{64,48},{80,64},{96,80},{112,96},{17,1},{33... | collective-permute-start | bytes 24584 | tf_op jit(solution)/shard_map/ppermute | solution.py:21
  631.6 17.0 %collective-permute-start.9 = (f32[16,64,1]{2,1,0:T(8,128)S(1)}, f32[16,64,1]{2,1,0:T(8,128)S(1)}, u32[]{:S(2)}, u32[]{:S(2)}) collective-permute-start(f32[16,64,1]{2,1,0:T(8,128)S(1)} %get-tuple-element.24), channel_id=1, source_target_pairs={{0,1},{1,2},{2,3},{3,4},{4,5},{5,6},{6,7},{7,8},{8,9},{9,10},{10,1... | collective-permute-start | bytes 12296 | tf_op jit(solution)/shard_map/ppermute | solution.py:18
  631.9 16.7 %collective-permute-start.8 = (f32[16,64,1]{2,1,0:T(8,128)S(1)}, f32[16,64,1]{2,1,0:T(8,128)S(1)}, u32[]{:S(2)}, u32[]{:S(2)}) collective-permute-start(f32[16,64,1]{2,1,0:T(8,128)S(1)} %get-tuple-element.23), channel_id=1, source_target_pairs={{1,0},{2,1},{3,2},{4,3},{5,4},{6,5},{7,6},{8,7},{9,8},{10,9},{11,1... | collective-permute-start | bytes 12296 | tf_op jit(solution)/shard_map/ppermute | solution.py:21
where the time goes:
time: 720 us; the launch traced here: 719 us
  waiting for transfers between devices  399 us (55%)
  blocking collectives  208 us (29%)
  local copies, waits for them, and re-layouts  46.6 us (6%)
  other arithmetic  33.9 us (5%)
  starting transfers between devices  30.9 us (4%)
    all_to_all x1, waiting for transfers between devices, on_device(): lax.all_to_all(packed, 'lon', split_axis=1, concat_axis=1, tiled=True)  374 us
    psum x2, blocking collectives, norm_sum(): return lax.psum(level_inner(residual, smoothed), ('lat', 'lon'))  129 us
    psum x1, blocking collectives, on_device(): curvature = lax.psum(level_inner(direction, image), ('lat', 'lon'))  65.1 us
    ppermute x5, waiting for transfers between devices, padded(): lax.ppermute(lax.slice_in_dim(block, block.shape[dim] - width, None, axis...  24.3 us
    select_n x2, other arithmetic, on_device(): packed = jnp.take(blocks, asked, axis=1)  17.7 us
    ppermute x5, starting transfers between devices, padded(): lax.ppermute(lax.slice_in_dim(block, 0, width, axis=dim), axis, backward)  15 us
    gather x3, local copies, waits for them, and re-layouts, on_device(): jnp.take(arrived, places, axis=1)  14.7 us
  transfers between devices with their start and end apart: 11, of which 3 were waited for; matrix products, arithmetic and copies ran while one was open for 1% of the time, Pallas kernels for 0%

commit v1 on v0

v1 whole, which is shorter than its diff:
```python
import functools

import jax
import jax.numpy as jnp
from jax import lax
from jax.experimental import pallas as pl
from jax.experimental.pallas import tpu as pltpu
from jax.sharding import PartitionSpec as P

ROWS = 4
LANES = 128
SPAN = 64
F32 = jnp.float32
BF16 = jnp.bfloat16


def iota(shape, dim):
    return lax.broadcasted_iota(jnp.int32, shape, dim)


def ring(axis, step):
    count = lax.axis_size(axis)
    return [(i, (i + step) % count) for i in range(count)]


def line(axis, step):
    count = lax.axis_size(axis)
    return [(i, i + step) for i in range(count) if 0 <= i + step < count]


def across_pole():
    bands, sectors = lax.axis_size("lat"), lax.axis_size("lon")
    return [
        (band * sectors + s, band * sectors + (s + sectors // 2) % sectors)
        for band in (0, bands - 1)
        for s in range(sectors)
    ]


def to_lat(block, step):
    return lax.ppermute(block, "lat", line("lat", step))


def to_lon(block, step):
    return lax.ppermute(block, "lon", ring("lon", step))


def to_far(block):
    return lax.ppermute(block, ("lat", "lon"), across_pole())


def coded(depart_lists, tiles):
    sectors = lax.axis_size("lon")
    wanted = depart_lists.reshape(1, -1)
    owner = wanted // tiles
    turn = (owner % sectors - lax.axis_index("lon") + sectors) % sectors
    tile = (owner // sectors - lax.axis_index("lat") + 1) * tiles + wanted % tiles
    code = turn * SPAN + tile
    return jnp.pad(code, ((0, 0), (0, LANES - code.shape[1])), constant_values=2 * SPAN)


def ranks(member):
    before = (iota((LANES, LANES), 0) < iota((LANES, LANES), 1)).astype(BF16)
    ones = jnp.where(member, 1.0, 0.0).astype(BF16)
    return jnp.dot(ones, before, preferred_element_type=F32)


def pack_kernel(sectors, left, right, far, low, own, high, out_left, out_right, out_far, pick):
    @pl.when(pl.program_id(0) == 0)
    def _():
        sub = iota((8, LANES), 0)
        codes = jnp.where(sub == 0, left[...], jnp.where(sub == 1, right[...], far[...]))
        want = jnp.where(sub == 0, 1, jnp.where(sub == 1, sectors - 1, sectors // 2))
        member = (codes >> 6) == want
        rank = jnp.where(member, ranks(member), -1.0)
        tile = ((codes & (SPAN - 1)) + 1).astype(F32)
        slot = (iota((64, LANES), 0) >> 2).astype(F32)
        row = (iota((64, 192), 0) & 3).astype(F32)
        col = iota((64, 192), 1).astype(F32)
        for d in range(3):
            hit = rank[d : d + 1] == slot
            held = jnp.sum(jnp.where(hit, tile[d : d + 1], 0.0), axis=1, keepdims=True) - 1.0
            pick[d * 64 : (d + 1) * 64, :] = jnp.where(col == held * 4.0 + row, 1.0, 0.0).astype(BF16)

    def pair(g, carry):
        pool = jnp.concatenate(
            [jnp.concatenate([low[f], own[f], high[f]], axis=0) for f in (2 * g, 2 * g + 1)], axis=1
        )
        got = jnp.dot(pick[...], pool, preferred_element_type=F32).astype(BF16)
        for d, out in enumerate((out_left, out_right, out_far)):
            for half in range(2):
                out[2 * g + half] = got[d * 64 : (d + 1) * 64, half * LANES : (half + 1) * LANES]
        return carry

    lax.fori_loop(0, own.shape[0] // 2, pair, 0, unroll=4)


def pack(lists, bands, step):
    levels = bands[0].shape[0]
    sectors = lax.axis_size("lon")
    block = pl.BlockSpec((step, 64, LANES), lambda g: (g, 0, 0))
    row = pl.BlockSpec((1, LANES), lambda g: (0, 0))
    return pl.pallas_call(
        functools.partial(pack_kernel, sectors),
        grid=(levels // step,),
        in_specs=[row] * 3 + [block] * 3,
        out_specs=[block] * 3,
        out_shape=[jax.ShapeDtypeStruct((levels, 64, LANES), BF16)] * 3,
        scratch_shapes=[pltpu.VMEM((192, 192), BF16)],
        compiler_params=pltpu.CompilerParams(vmem_limit_bytes=32 << 20),
        cost_estimate=pl.CostEstimate(
            flops=levels * 2 * 192 * 192 * LANES, bytes_accessed=levels * 6 * 64 * LANES * 2, transcendentals=0
        ),
        name="pack",
    )(*lists, *bands)


def set_gather(sectors, codes_ref, gather):
    codes = jnp.broadcast_to(codes_ref[...], (8, LANES))
    turn = codes >> 6
    sub = iota((8, LANES), 0)
    group = jnp.where(sub == 1, sectors - 1, jnp.where(sub == 2, 1, jnp.where(sub == 3, sectors // 2, 0)))
    rank = ranks(turn == group)
    turn = turn[:1]
    place = jnp.where(turn == 0, (codes[:1] & (SPAN - 1)).astype(F32), -1.0)
    place = jnp.where(turn == sectors - 1, 48.0 + rank[1:2], place)
    place = jnp.where(turn == 1, 64.0 + rank[2:3], place)
    place = jnp.where(turn == sectors // 2, 80.0 + rank[3:4], place)
    row = iota((LANES, LANES), 0)
    mine = iota((LANES, LANES), 1) == 2 * (row & 15) + (row >> 6)
    place = jnp.sum(jnp.where(mine, place, 0.0), axis=1, keepdims=True)
    within = ((iota((LANES, 384), 0) >> 4) & 3).astype(F32)
    col = iota((LANES, 384), 1).astype(F32)
    gather[...] = jnp.where(col == place * 4.0 + within, 1.0, 0.0).astype(BF16)


def every_fourth(q):
    return pl.ds(q, 16, stride=4)


def set_weights(offsets, weights, coef):
    for q in range(4):
        offset = offsets[every_fourth(q), :]
        points = [weights[m, every_fourth(q), :] for m in range(4)]
        for r in range(8):
            value = jnp.zeros((16, LANES), F32)
            for m in range(4):
                if 0 <= r - m <= 4:
                    value = jnp.where(offset == r - m, points[m], value)
            coef[q * 8 + r] = value


def interpolate(gather, coef, pools, first, second):
    pool = jnp.concatenate(
        [jnp.concatenate([ref[f] for ref in pools], axis=0) for f in (first, second)], axis=1
    )
    rows = jnp.dot(gather[...], pool, preferred_element_type=F32)
    out = []
    for q in range(4):
        sums = [None, None]
        for r in range(8):
            weight = coef[q * 8 + r]
            for h in range(2):
                term = weight * rows[r * 16 : (r + 1) * 16, h * LANES : (h + 1) * LANES]
                sums[h] = term if r == 0 else sums[h] + term
        out.append(sums)
    return out


def first_kernel(
    sectors, scale, codes, offsets, weights, diag, low, own, high, left, right, far,
    adv, rhs, z, cols, up, down, gather, coef, tmp,
):
    set_gather(sectors, codes, gather)
    set_weights(offsets, weights, coef)
    pools = (low, own, high, left, right, far)

    def level(l, carry):
        values = interpolate(gather, coef, pools, l, 16 + l)
        for q in range(4):
            tmp[l, every_fourth(q), :] = values[q][0]
            rhs[l, every_fourth(q), :] = values[q][1] + 0.5 * values[q][0]
        return carry

    lax.fori_loop(0, 16, level, 0, unroll=2)
    group = iota((64, LANES), 1) >> 2
    packed = jnp.where(group == 16, pltpu.roll(diag[...], 65, 1), 0.0)
    for l in range(16):
        adv[l] = tmp[l].astype(BF16)
        value = rhs[l] / (4.0 + diag[...] * scale[l])
        z[l] = value
        packed = jnp.where(group == l, pltpu.roll(value, 2 + 4 * l, 1), packed)
        up[l : l + 1, :] = value[0:1]
        up[16 + l : 17 + l, :] = value[1:2]
        down[l : l + 1, :] = value[63:64]
        down[16 + l : 17 + l, :] = value[62:63]
    cols[...] = packed
    up[32:33, :] = diag[0:1, :]
    down[32:33, :] = diag[63:64, :]
    up[33:40, :] = jnp.ones((7, LANES), F32)
    down[33:40, :] = jnp.ones((7, LANES), F32)


SMEM = pl.BlockSpec(memory_space=pltpu.SMEM)
VMEM = pl.BlockSpec(memory_space=pltpu.VMEM)


def first_levels(scale, codes, offsets, weights, diag, pools):
    slab = jax.ShapeDtypeStruct((16, 64, LANES), F32)
    edge = jax.ShapeDtypeStruct((40, LANES), F32)
    whole = pl.BlockSpec((16, 64, LANES), lambda g: (0, 0, 0))
    flat = lambda rows: pl.BlockSpec((rows, LANES), lambda g: (0, 0))
    return pl.pallas_call(
        functools.partial(first_kernel, lax.axis_size("lon")),
        grid=(1,),
        in_specs=[SMEM] + [VMEM] * 10,
        out_specs=[
            pl.BlockSpec((16, 64, LANES), lambda g: (2, 0, 0)), whole, whole, flat(64), flat(40), flat(40)
        ],
        out_shape=[
            jax.ShapeDtypeStruct((64, 64, LANES), BF16), slab, slab,
            jax.ShapeDtypeStruct((64, LANES), F32), edge, edge,
        ],
        scratch_shapes=[
            pltpu.VMEM((LANES, 384), BF16), pltpu.VMEM((32, 16, LANES), F32), pltpu.VMEM((16, 64, LANES), F32)
        ],
        compiler_params=pltpu.CompilerParams(vmem_limit_bytes=32 << 20),
        cost_estimate=pl.CostEstimate(flops=32 * 2 * 128 * 384 * 128, bytes_accessed=6 << 20, transcendentals=0),
        name="first_levels",
    )(scale, codes, offsets, weights, diag, *pools)


def other_kernel(
    sectors, codes, offsets, weights, low, own, high, left, right, far, start, adv, gather, coef, tmp
):
    @pl.when(pl.program_id(0) == 0)
    def _():
        set_gather(sectors, codes, gather)
        set_weights(offsets, weights, coef)

    pools = (low, own, high, left, right, far)

    def pair(g, carry):
        values = interpolate(gather, coef, pools, 2 * g, 2 * g + 1)
        for h in range(2):
            for q in range(4):
                tmp[2 * g + h, every_fourth(q), :] = values[q][h]
        return carry

    count = own.shape[0]
    lax.fori_loop(0, count // 2, pair, 0, unroll=2)
    for f in range(count):
        adv[f] = tmp[f].astype(BF16)


def other_levels(codes, offsets, weights, pools, start):
    block = pl.BlockSpec((16, 64, LANES), lambda g: (g, 0, 0))
    flat = lambda rows: pl.BlockSpec((rows, LANES), lambda g: (0, 0))
    return pl.pallas_call(
        functools.partial(other_kernel, lax.axis_size("lon")),
        grid=(3,),
        in_specs=[flat(1), flat(64), pl.BlockSpec((4, 64, LANES), lambda g: (0, 0, 0))]
        + [block] * 6
        + [pl.BlockSpec(memory_space=pl.ANY)],
        out_specs=pl.BlockSpec((16, 64, LANES), lambda g: (g + g // 2, 0, 0)),
        out_shape=jax.ShapeDtypeStruct(start.shape, start.dtype),
        scratch_shapes=[
            pltpu.VMEM((LANES, 384), BF16), pltpu.VMEM((32, 16, LANES), F32), pltpu.VMEM((16, 64, LANES), F32)
        ],
        input_output_aliases={9: 0},
        compiler_params=pltpu.CompilerParams(vmem_limit_bytes=32 << 20),
        cost_estimate=pl.CostEstimate(flops=48 * 2 * 128 * 384 * 128, bytes_accessed=6 << 20, transcendentals=0),
        name="other_levels",
    )(codes, offsets, weights, *pools, start)


def sum_kernel(scale, z, rhs, diag, cols, left, right, above, below, n0, n1, sums, rowsums):
    lane = iota((64, LANES), 1)
    spread = jnp.zeros((1, LANES), F32)
    column = jnp.zeros((16, LANES), F32)
    for l in range(16):
        spread = jnp.where((lane[:1] >> 2) == l, scale[l], spread)
        column = jnp.where(iota((16, LANES), 0) == l, scale[l], column)
    row16, lane16 = iota((16, LANES), 0), lane[:16]

    def corner(row, which):
        return jnp.sum(jnp.where(lane16 == 4 * row16 + which, row, 0.0), axis=1, keepdims=True)

    def rim_row(edge, inner):
        near, second, flag = edge[0:16, :], edge[16:32, :], edge[33:34, :]
        west, east = corner(edge[34:35, :], 1), corner(edge[35:36, :], 2)
        beside = jnp.where(lane16 == 0, west, pltpu.roll(near, 1, 1))
        beside = beside + jnp.where(lane16 == LANES - 1, east, pltpu.roll(near, LANES - 1, 1))
        return flag * (second + inner + beside) / (4.0 + edge[32:33, :] * column)

    top_in = jnp.concatenate([z[l, 0:1, :] for l in range(16)], axis=0)
    low_in = jnp.concatenate([z[l, 63:64, :] for l in range(16)], axis=0)
    top, bottom = rim_row(above, top_in), rim_row(below, low_in)

    def rim_col(edge, first, last, toward, diag_lane):
        values = edge[...]
        up = jnp.concatenate([first, values[:-1]], axis=0)
        down = jnp.concatenate([values[1:], last], axis=0)
        outer = pltpu.roll(values, toward % LANES, 1)
        inner = pltpu.roll(cols[...], -toward % LANES, 1)
        coef = 4.0 + values[:, diag_lane : diag_lane + 1] * spread
        return (up + down + outer + inner) / coef

    west = rim_col(left, above[34:35, :], below[34:35, :], 1, 64)
    east = rim_col(right, above[35:36, :], below[35:36, :], -1, 65)

    def beside(value, west_col, east_col, upper, lower):
        total = jnp.where(lane == 0, west_col, pltpu.roll(value, 1, 1))
        total = total + jnp.where(lane == LANES - 1, east_col, pltpu.roll(value, LANES - 1, 1))
        total = total + jnp.concatenate([upper, value[:-1]], axis=0)
        return total + jnp.concatenate([value[1:], lower], axis=0)

    for l in range(16):
        value, start = z[l], rhs[l]
        inverse = 1.0 / (4.0 + diag[...] * scale[l])
        around = beside(
            value, left[:, 4 * l + 1 : 4 * l + 2], right[:, 4 * l + 2 : 4 * l + 3], above[l : l + 1, :], below[l : l + 1, :]
        )
        n0[l] = around
        again = around * inverse
        second = beside(
            again, west[:, 4 * l + 1 : 4 * l + 2], east[:, 4 * l + 2 : 4 * l + 3], top[l : l + 1], bottom[l : l + 1]
        )
        n1[l] = second
        for k, term in enumerate((start * value, start * again, around * again, second * again)):
            part = term[0:8]
            for j in range(1, 8):
                part = part + term[8 * j : 8 * j + 8]
            rowsums[k * 16 + l : k * 16 + l + 1, :] = jnp.sum(part, axis=0, keepdims=True)
    total = jnp.sum(rowsums[...], axis=1, keepdims=True)
    packed = jnp.zeros((8, LANES), F32)
    for j in range(8):
        packed = jnp.where(lane[:8] == j, total[8 * j : 8 * j + 8], packed)
    for j in range(sums.shape[0]):
        sums[j] = packed


def level_sums(scale, z, rhs, diag, cols, left, right, above, below):
    slab = jax.ShapeDtypeStruct((16, 64, LANES), F32)
    return pl.pallas_call(
        sum_kernel,
        in_specs=[SMEM] + [VMEM] * 8,
        out_specs=[VMEM] * 3,
        out_shape=[slab, slab, jax.ShapeDtypeStruct((lax.axis_size("lat"), 8, LANES), F32)],
        scratch_shapes=[pltpu.VMEM((64, LANES), F32)],
        compiler_params=pltpu.CompilerParams(vmem_limit_bytes=32 << 20),
        cost_estimate=pl.CostEstimate(flops=1 << 22, bytes_accessed=2 << 20, transcendentals=0),
        name="level_sums",
    )(scale, z, rhs, diag, cols, left, right, above, below)


def last_kernel(scale, parts, rhs, diag, n0, n1, pressure, residual):
    total = parts[0]
    for j in range(1, parts.shape[0]):
        total = total + parts[j]
    lane = iota((8, LANES), 1)

    def of(k, half):
        return jnp.sum(jnp.where(lane == 2 * k + half, total, 0.0), axis=1, keepdims=True)

    for half in range(2):
        s0, s1, s2, s3 = (of(k, half) for k in range(4))
        curve = s0 - s1
        step = s0 / curve
        keep = -s1 / curve
        norm = keep * keep * s0 + 2.0 * keep * step * s1 + step * step * s2
        ratio = norm / s0
        bend = norm - (keep * keep * s1 + 2.0 * keep * step * s2 + step * step * s3)
        other = norm / (bend - ratio * ratio * curve)
        along = other * (keep + ratio)
        across = other * step
        fit_z, fit_p = step + along, across
        fit_r, fit_n0, fit_n1 = keep - along, step + along - across, across
        for s in range(8):
            l = 8 * half + s
            at = lambda column: column[s : s + 1]
            inverse = 1.0 / (4.0 + diag[...] * scale[l])
            start, around = rhs[l], n0[l]
            pressure[l] = (at(fit_z) * start + at(fit_p) * around) * inverse
            residual[l] = at(fit_r) * start + at(fit_n0) * around + at(fit_n1) * n1[l]


def last_step(scale, parts, rhs, diag, n0, n1):
    slab = jax.ShapeDtypeStruct((16, 64, LANES), F32)
    return pl.pallas_call(
        last_kernel,
        in_specs=[SMEM] + [VMEM] * 5,
        out_specs=[VMEM] * 2,
        out_shape=[slab, slab],
        compiler_params=pltpu.CompilerParams(vmem_limit_bytes=32 << 20),
        cost_estimate=pl.CostEstimate(flops=1 << 21, bytes_accessed=3 << 20, transcendentals=0),
        name="last_step",
    )(scale, parts, rhs, diag, n0, n1)


def exchange(parts, axis):
    return lax.all_to_all(parts, axis, split_axis=0, concat_axis=0, tiled=True)


def on_device(fields, depart_lists, stencil_offsets, interp_weights, diag_coef, level_scale):
    tiles = depart_lists.shape[0]
    codes = coded(depart_lists, tiles)
    lists = (to_lon(codes, 1), to_lon(codes, -1), to_far(codes))
    first = jnp.concatenate([fields[32:48], fields[64:80]], axis=0)
    other = jnp.concatenate([fields[0:32], fields[48:64]], axis=0)

    def banded(block):
        return (to_lat(block, 1), block, to_lat(block, -1))

    def fetched(bands):
        to_left, to_right, far = pack(lists, bands, 16)
        return bands + (to_lon(to_right, 1), to_lon(to_left, -1), to_far(far))

    pools = fetched(banded(first))
    adv, rhs, z, cols, up, down = first_levels(
        level_scale, codes, stencil_offsets, interp_weights, diag_coef, pools
    )
    left, right = to_lon(cols, 1), to_lon(cols, -1)
    rim = lambda edge, row: jnp.concatenate([edge[:34], left[row : row + 1], right[row : row + 1], edge[36:]], axis=0)
    below = to_lat(rim(up, 0), -1)
    above = to_lat(rim(down, 63), 1)
    n0, n1, parts = level_sums(level_scale, z, rhs, diag_coef, cols, left, right, above, below)
    parts = jnp.sum(exchange(parts, "lat"), axis=0)
    parts = exchange(jnp.broadcast_to(parts[None], (lax.axis_size("lon"),) + parts.shape), "lon")
    pressure, residual = last_step(level_scale, parts, rhs, diag_coef, n0, n1)
    adv = other_levels(codes, stencil_offsets, interp_weights, fetched(banded(other)), adv)
    return (adv, pressure, residual)


def solution(mesh):
    placed = (
        P(None, "lat", "lon"),
        P("lat", "lon", None),
        P("lat", "lon"),
        P(None, "lat", "lon"),
        P("lat", "lon"),
        P(),
    )
    return jax.shard_map(
        on_device,
        mesh=mesh,
        in_specs=placed,
        out_specs=(P(None, "lat", "lon"), P(None, "lat", "lon"), P(None, "lat", "lon")),
        check_vma=False,
    )
```

time: 720 us -> 141 us (0.20)
  waiting for transfers between devices: 399 us -> 22 us
  blocking collectives: 208 us -> 26.5 us
  local copies, waits for them, and re-layouts: 46.6 us -> 5.05 us
  other arithmetic: 33.9 us -> 0.94 us
  starting transfers between devices: 30.9 us -> 63.7 us
  Pallas kernels: 0 us -> 20.4 us
    all_to_all x1 -> x0, waiting for transfers between devices: 374 us -> none  [on_device(): lax.all_to_all(packed, 'lon', split_axis=1, concat_axis=1, tiled=True)]
    psum x3 -> x0, blocking collectives: 194 us -> none  [the longest x2 129 us: norm_sum(): return lax.psum(level_inner(residual, smoothed), ('lat', 'lon'))]
    ppermute x10 -> x17, starting transfers between devices: 25.3 us -> 63.7 us  [the longest x6 40.4 us: to_lat(): return lax.ppermute(block, 'lat', line('lat', step))]
    gather x4 -> x0, local copies, waits for them, and re-layouts: 27.1 us -> none  [the longest x3 14.7 us: on_device(): jnp.take(arrived, places, axis=1)]
    pallas_call x0 -> x6, Pallas kernels: none -> 20.4 us  [the longest x2 5.59 us: pack(): pl.pallas_call(functools.partial(pack_kernel, sectors), grid=(levels // s...]
    select_n x5 -> x0, other arithmetic: 18 us -> none  [the longest x2 17.7 us: on_device(): packed = jnp.take(blocks, asked, axis=1)]
    reshape x2 -> x1, local copies, waits for them, and re-layouts: 13.4 us -> 0.09 us  [coded(): wanted = depart_lists.reshape(1, -1)]
    all_to_all x1 -> x2, blocking collectives: 13.8 us -> 26.5 us  [exchange(): return lax.all_to_all(parts, axis, split_axis=0, concat_axis=0, tiled=True)]
  transfers between devices with their start and end apart: 11 -> 17, of which waited for: 3 -> 5; matrix products, arithmetic and copies ran while one was open for 1% -> 1% of each run, Pallas kernels for 0% -> 11%
where the time goes in v1:
time: 141 us; the launch traced here: 140 us
  starting transfers between devices  63.7 us (45%)
  blocking collectives  26.5 us (19%)
  waiting for transfers between devices  22 us (16%)
  Pallas kernels  20.4 us (14%)
  local copies, waits for them, and re-layouts  5.05 us (4%)
    ppermute x6, starting transfers between devices, to_lat(): return lax.ppermute(block, 'lat', line('lat', step))  40.4 us
    all_to_all x2, blocking collectives, exchange(): return lax.all_to_all(parts, axis, split_axis=0, concat_axis=0, tiled=True)  26.5 us
    ppermute x8, waiting for transfers between devices, to_lon(): return lax.ppermute(block, 'lon', ring('lon', step))  20.9 us
    ppermute x8, starting transfers between devices, to_lon(): return lax.ppermute(block, 'lon', ring('lon', step))  20.4 us
    pallas_call x2, Pallas kernels, pack(): pl.pallas_call(functools.partial(pack_kernel, sectors), grid=(levels // s...  5.59 us
    pallas_call x1, Pallas kernels, other_levels(): pl.pallas_call(functools.partial(other_kernel, lax.axis_size('lon')), gri...  5.51 us
    pallas_call x1, Pallas kernels, first_levels(): pl.pallas_call(functools.partial(first_kernel, lax.axis_size('lon')), gri...  4.37 us
    unnamed x23, local copies, waits for them, and re-layouts  3.76 us
  transfers between devices with their start and end apart: 17, of which 5 were waited for; matrix products, arithmetic and copies ran while one was open for 1% of the time, Pallas kernels for 11%

profile of v1, /device:TPU:1, one launch (start us, length us, event | category | flops | bytes accessed | tf_op | source)
XLA Modules:
  0.0 139.6 jit_solution(520026158803060899)
XLA Ops:
  0.6 1.2 fusion.6
  1.9 3.5 %collective-permute-start.9 = (bf16[32,64,128]{2,1,0:T(8,128)(2,1)S(1)}, bf16[32,64,128]{2,1,0:T(8,128)(2,1)S(1)}, u32[]{:S(2)}, u32[]{:S(2)}) collective-permute-start(bf16[32,64,128]{2,1,0:T(8,128)(2,1)S(1)} %pad_maximum_fusion.1.own), channel_id=1, source_target_pairs={{16,0},{32,16},{48,32},{64,48},{80,64},{96,80},{112,96},{17,1},{33... | collective-permute-start | bytes 1572872 | tf_op jit(solution)/shard_map/ppermute | solution.py:41
  5.4 3.2 %collective-permute-start.8 = (bf16[32,64,128]{2,1,0:T(8,128)(2,1)S(1)}, bf16[32,64,128]{2,1,0:T(8,128)(2,1)}, u32[]{:S(2)}, u32[]{:S(2)}) collective-permute-start(bf16[32,64,128]{2,1,0:T(8,128)(2,1)S(1)} %pad_maximum_fusion.1.own), channel_id=1, source_target_pairs={{0,16},{16,32},{32,48},{48,64},{64,80},{80,96},{96,112},{1,17},{17... | collective-permute-start | bytes 1572872 | tf_op jit(solution)/shard_map/ppermute | solution.py:41
  8.7 1.9 %collective-permute-start.1 = (bf16[48,64,128]{2,1,0:T(8,128)(2,1)S(1)}, bf16[48,64,128]{2,1,0:T(8,128)(2,1)S(1)}, u32[]{:S(2)}, u32[]{:S(2)}) collective-permute-start(bf16[48,64,128]{2,1,0:T(8,128)(2,1)S(1)} %pad_maximum_fusion.own), channel_id=1, source_target_pairs={{16,0},{32,16},{48,32},{64,48},{80,64},{96,80},{112,96},{17,1},{33... | collective-permute-start | bytes 2359304 | tf_op jit(solution)/shard_map/ppermute | solution.py:41
  10.6 3.6 %collective-permute-start = (bf16[48,64,128]{2,1,0:T(8,128)(2,1)S(1)}, bf16[48,64,128]{2,1,0:T(8,128)(2,1)S(1)}, u32[]{:S(2)}, u32[]{:S(2)}) collective-permute-start(bf16[48,64,128]{2,1,0:T(8,128)(2,1)S(1)} %pad_maximum_fusion.own), channel_id=1, source_target_pairs={{0,16},{16,32},{32,48},{48,64},{64,80},{80,96},{96,112},{1,17},{17... | collective-permute-start | bytes 2359304 | tf_op jit(solution)/shard_map/ppermute | solution.py:41
  14.5 0.7 collective-permute-start.4
  15.2 6.0 %collective-permute-start.3 = (s32[1,128]{1,0:T(1,128)S(1)}, s32[1,128]{1,0:T(1,128)S(1)}, u32[]{:S(2)}, u32[]{:S(2)}) collective-permute-start(s32[1,128]{1,0:T(1,128)S(1)} %pad.4.codes), channel_id=1, source_target_pairs={{0,15},{1,0},{2,1},{3,2},{4,3},{5,4},{6,5},{7,6},{8,7},{9,8},{10,9... | collective-permute-start | bytes 1544 | tf_op jit(solution)/shard_map/ppermute | solution.py:45
  21.2 0.7 collective-permute-done.3.right
  21.9 5.9 %collective-permute-done.2.left = s32[1,128]{1,0:T(1,128)S(1)} collective-permute-done((s32[1,128]{1,0:T(1,128)S(1)}, s32[1,128]{1,0:T(1,128)S(1)}, u32[]{:S(2)}, u32[]{:S(2)}) %collective-permute-start.2) | collective-permute-done | bytes 544 | tf_op jit(solution)/shard_map/ppermute | solution.py:45
  27.9 2.5 %pack.3 = (bf16[32,64,128]{2,1,0:T(8,128)(2,1)S(1)}, bf16[32,64,128]{2,1,0:T(8,128)(2,1)S(1)}, bf16[32,64,128]{2,1,0:T(8,128)(2,1)S(1)}) custom-call(s32[1,128]{1,0:T(1,128)S(1)} %collective-permute-done.2.left, s32[1,128]{1,0:T(1,128)S(1)} %collective-permute-done.3.right, s32[1,128]{1,0:T(1,128)S(1)} %collective-permute-done.4.far, ...), custom_call_target="tpu_custom_call" | custom-call | flops 301989888 | bytes 3145728 | tf_op jit(solution)/shard_map/pack/pallas_call | solution.py:103
  30.4 4.8 %collective-permute-start.11 = (bf16[32,64,128]{2,1,0:T(8,128)(2,1)S(1)}, bf16[32,64,128]{2,1,0:T(8,128)(2,1)S(1)}, u32[]{:S(2)}, u32[]{:S(2)}) collective-permute-start(bf16[32,64,128]{2,1,0:T(8,128)(2,1)S(1)} %get-tuple-element.24), channel_id=1, source_target_pairs={{0,15},{1,0},{2,1},{3,2},{4,3},{5,4},{6,5},{7,6},{8,7},{9,8},{10,9... | collective-permute-start | bytes 1572872 | tf_op jit(solution)/shard_map/ppermute | solution.py:45
  35.2 0.7 collective-permute-start.12
  35.9 5.9 %collective-permute-done.10.left = bf16[32,64,128]{2,1,0:T(8,128)(2,1)S(1)} collective-permute-done((bf16[32,64,128]{2,1,0:T(8,128)(2,1)S(1)}, bf16[32,64,128]{2,1,0:T(8,128)(2,1)S(1)}, u32[]{:S(2)}, u32[]{:S(2)}) %collective-permute-start.10) | collective-permute-done | bytes 524320 | tf_op jit(solution)/shard_map/ppermute | solution.py:45
  41.8 1.0 copy-done.1
  42.9 4.4 %first_levels.1 = (bf16[64,64,128]{2,1,0:T(8,128)(2,1)}, f32[16,64,128]{2,1,0:T(8,128)S(1)}, f32[16,64,128]{2,1,0:T(8,128)S(1)}, f32[64,128]{1,0:T(8,128)S(1)}, ...) custom-call(f32[16]{0:T(128)S(1)} %copy-done.9, s32[1,128]{1,0:T(1,128)S(1)} %pad.4.codes, s32[64,128]{1,0:T(8,128)S(1)} %copy-done.7, ...), custom_call_target="tpu_custom_call" | custom-call | flops 402653184 | bytes 6291456 | tf_op jit(solution)/shard_map/first_levels/pallas_call | solution.py:213
  47.2 4.8 %collective-permute-start.14 = (f32[64,128]{1,0:T(8,128)S(1)}, f32[64,128]{1,0:T(8,128)S(1)}, u32[]{:S(2)}, u32[]{:S(2)}) collective-permute-start(f32[64,128]{1,0:T(8,128)S(1)} %get-tuple-element.29.cols), channel_id=1, source_target_pairs={{0,15},{1,0},{2,1},{3,2},{4,3},{5,4},{6,5},{7,6},{8,7},{9,8},{10,9... | collective-permute-start | bytes 98312 | tf_op jit(solution)/shard_map/ppermute | solution.py:45
  52.0 3.1 %pack.2 = (bf16[48,64,128]{2,1,0:T(8,128)(2,1)}, bf16[48,64,128]{2,1,0:T(8,128)(2,1)}, bf16[48,64,128]{2,1,0:T(8,128)(2,1)}) custom-call(s32[1,128]{1,0:T(1,128)S(1)} %collective-permute-done.2.left, s32[1,128]{1,0:T(1,128)S(1)} %collective-permute-done.3.right, s32[1,128]{1,0:T(1,128)S(1)} %collective-permute-done.4.far, ...), custom_call_target="tpu_custom_call" | custom-call | flops 452984832 | bytes 4718592 | tf_op jit(solution)/shard_map/pack/pallas_call | solution.py:103
  55.1 4.8 %collective-permute-start.6 = (bf16[48,64,128]{2,1,0:T(8,128)(2,1)}, bf16[48,64,128]{2,1,0:T(8,128)(2,1)}, u32[]{:S(2)}, u32[]{:S(2)}) collective-permute-start(bf16[48,64,128]{2,1,0:T(8,128)(2,1)} %get-tuple-element.21), channel_id=1, source_target_pairs={{0,15},{1,0},{2,1},{3,2},{4,3},{5,4},{6,5},{7,6},{8,7},{9,8},{10,9... | collective-permute-start | bytes 2359304 | tf_op jit(solution)/shard_map/ppermute | solution.py:45
  59.9 1.6 %collective-permute-start.7 = (bf16[48,64,128]{2,1,0:T(8,128)(2,1)}, bf16[48,64,128]{2,1,0:T(8,128)(2,1)}, u32[]{:S(2)}, u32[]{:S(2)}) collective-permute-start(bf16[48,64,128]{2,1,0:T(8,128)(2,1)} %get-tuple-element.22), channel_id=1, source_target_pairs={{0,8},{1,9},{2,10},{3,11},{4,12},{5,13},{6,14},{7,15},{8,0},{9,1},... | collective-permute-start | bytes 2359304 | tf_op jit(solution)/shard_map/ppermute | solution.py:49
  61.5 8.3 %collective-permute-done.13.left = f32[64,128]{1,0:T(8,128)S(1)} collective-permute-done((f32[64,128]{1,0:T(8,128)S(1)}, f32[64,128]{1,0:T(8,128)S(1)}, u32[]{:S(2)}, u32[]{:S(2)}) %collective-permute-start.13) | collective-permute-done | bytes 32800 | tf_op jit(solution)/shard_map/ppermute | solution.py:45
  69.9 26.2 %collective-permute-start.16 = (f32[40,128]{1,0:T(8,128)S(1)}, f32[40,128]{1,0:T(8,128)S(1)}, u32[]{:S(2)}, u32[]{:S(2)}) collective-permute-start(f32[40,128]{1,0:T(8,128)S(1)} %pad_maximum_fusion.3), channel_id=1, source_target_pairs={{16,0},{32,16},{48,32},{64,48},{80,64},{96,80},{112,96},{17,1},{33... | collective-permute-start | bytes 61448 | tf_op jit(solution)/shard_map/ppermute | solution.py:41
  96.1 1.9 %collective-permute-start.15 = (f32[40,128]{1,0:T(8,128)S(1)}, f32[40,128]{1,0:T(8,128)S(1)}, u32[]{:S(2)}, u32[]{:S(2)}) collective-permute-start(f32[40,128]{1,0:T(8,128)S(1)} %pad_maximum_fusion.2), channel_id=1, source_target_pairs={{0,16},{16,32},{32,48},{48,64},{64,80},{80,96},{96,112},{1,17},{17... | collective-permute-start | bytes 61448 | tf_op jit(solution)/shard_map/ppermute | solution.py:41
  98.1 1.1 collective-permute-done.15.above
  99.2 3.1 %level_sums.1 = (f32[16,64,128]{2,1,0:T(8,128)S(1)}, f32[16,64,128]{2,1,0:T(8,128)S(1)}, f32[8,8,128]{2,1,0:T(8,128)S(1)}) custom-call(f32[16]{0:T(128)S(1)} %copy-done.9, f32[16,64,128]{2,1,0:T(8,128)S(1)} %get-tuple-element.27.z, f32[16,64,128]{2,1,0:T(8,128)S(1)} %get-tuple-element.28.rhs, f32[64,128]{1,0:T(8,128)S(1)} %copy-done.5, ...), custom_call_target="tpu_custom_call" | custom-call | flops 4194304 | bytes 2097152 | tf_op jit(solution)/shard_map/level_sums/pallas_call | solution.py:345
  102.3 0.8 copy-done.3
  103.1 17.5 %all_to_all.10 = f32[8,8,128]{2,1,0:T(8,128)} all-to-all(f32[8,8,128]{2,1,0:T(8,128)S(1)} %get-tuple-element.32), channel_id=1, replica_groups=mesh['lat'=8,'lon'=16] {'lat'}, dimensions={0} | all-to-all | bytes 65536 | tf_op jit(solution)/shard_map/all_to_all | solution.py:402
  120.6 0.8 reduce_sum.9
  121.3 9.1 %all_to_all.11.parts = f32[16,8,128]{2,1,0:T(8,128)S(1)} all-to-all(f32[16,8,128]{2,1,0:T(8,128)S(1)} %broadcast_in_dim.2), channel_id=1, replica_groups=mesh['lat'=8,'lon'=16] {'lon'}, dimensions={0} | all-to-all | bytes 131072 | tf_op jit(solution)/shard_map/all_to_all | solution.py:402
  130.4 1.0 copy-done.4
  131.5 0.8 copy-done.6
  132.2 1.8 %last_step.1 = (f32[16,64,128]{2,1,0:T(8,128)}, f32[16,64,128]{2,1,0:T(8,128)}) custom-call(f32[16]{0:T(128)S(1)} %copy-done.9, f32[16,8,128]{2,1,0:T(8,128)S(1)} %all_to_all.11.parts, f32[16,64,128]{2,1,0:T(8,128)S(1)} %get-tuple-element.28.rhs, f32[64,128]{1,0:T(8,128)S(1)} %copy-done.6, f32[16,64,128]{2,1,0:T(8,128)S(1)} %get-tuple-element.33.n0, ...), custom_call_target="tpu_custom_call" | custom-call | flops 2097152 | bytes 3145728 | tf_op jit(solution)/shard_map/last_step/pallas_call | solution.py:390
  134.1 5.5 %other_levels.1 = bf16[64,64,128]{2,1,0:T(8,128)(2,1)} custom-call(s32[1,128]{1,0:T(1,128)S(1)} %pad.4.codes, s32[64,128]{1,0:T(8,128)S(1)} %copy-done.8, f32[4,64,128]{2,1,0:T(8,128)S(1)} %copy-done.2, bf16[48,64,128]{2,1,0:T(8,128)(2,1)S(1)} %collective-permute-done.low, ...), custom_call_target="tpu_custom_call", output_to_operand_aliasing={{}: (9, {})} | custom-call | flops 603979776 | bytes 6291456 | tf_op jit(solution)/shard_map/other_levels/pallas_call | solution.py:259
  (49 shorter events, 0.5 us)
Async XLA Ops:
  1.8 6.7 %slice-start = ((bf16[80,64,128]{2,1,0:T(8,128)(2,1)}), bf16[32,64,128]{2,1,0:T(8,128)(2,1)S(1)}, s32[]{:S(2)}) async-start(bf16[80,64,128]{2,1,0:T(8,128)(2,1)} %param.6), calls=%async_computation.2 | async-start | bytes 1048576 | tf_op jit(solution)/shard_map/slice | solution.py:410
  1.9 12.4 %copy-start.10 = (s32[16,1,2]{0,2,1:T(2,128)S(1)}, s32[16,1,2]{0,2,1:T(2,128)}, u32[]{:S(2)}) copy-start(s32[16,1,2]{0,2,1:T(2,128)} %param.7) | copy-start | bytes 388
  1.9 26.0 %collective-permute-start.9 = (bf16[32,64,128]{2,1,0:T(8,128)(2,1)S(1)}, bf16[32,64,128]{2,1,0:T(8,128)(2,1)S(1)}, u32[]{:S(2)}, u32[]{:S(2)}) collective-permute-start(bf16[32,64,128]{2,1,0:T(8,128)(2,1)S(1)} %pad_maximum_fusion.1.own), channel_id=1, source_target_pairs={{16,0},{32,16},{48,32},{64,48},{80,64},{96,80},{112,96},{17,1},{33... | collective-permute-start | bytes 1572872 | tf_op jit(solution)/shard_map/ppermute | solution.py:41
  5.4 22.5 %collective-permute-start.8 = (bf16[32,64,128]{2,1,0:T(8,128)(2,1)S(1)}, bf16[32,64,128]{2,1,0:T(8,128)(2,1)}, u32[]{:S(2)}, u32[]{:S(2)}) collective-permute-start(bf16[32,64,128]{2,1,0:T(8,128)(2,1)S(1)} %pad_maximum_fusion.1.own), channel_id=1, source_target_pairs={{0,16},{16,32},{32,48},{48,64},{64,80},{80,96},{96,112},{1,17},{17... | collective-permute-start | bytes 1572872 | tf_op jit(solution)/shard_map/ppermute | solution.py:41
  8.6 33.2 %copy-start.2 = (f32[4,64,128]{2,1,0:T(8,128)S(1)}, f32[4,64,128]{2,1,0:T(8,128)}, u32[]{:S(2)}) copy-start(f32[4,64,128]{2,1,0:T(8,128)} %weights.3) | copy-start | bytes 393220
  8.6 33.2 %copy-start.9 = (f32[16]{0:T(128)S(1)}, f32[16]{0:T(128)}, u32[]{:S(2)}) copy-start(f32[16]{0:T(128)} %scale.5) | copy-start | bytes 196
  8.7 43.3 %collective-permute-start.1 = (bf16[48,64,128]{2,1,0:T(8,128)(2,1)S(1)}, bf16[48,64,128]{2,1,0:T(8,128)(2,1)S(1)}, u32[]{:S(2)}, u32[]{:S(2)}) collective-permute-start(bf16[48,64,128]{2,1,0:T(8,128)(2,1)S(1)} %pad_maximum_fusion.own), channel_id=1, source_target_pairs={{16,0},{32,16},{48,32},{64,48},{80,64},{96,80},{112,96},{17,1},{33... | collective-permute-start | bytes 2359304 | tf_op jit(solution)/shard_map/ppermute | solution.py:41
  10.6 41.4 %collective-permute-start = (bf16[48,64,128]{2,1,0:T(8,128)(2,1)S(1)}, bf16[48,64,128]{2,1,0:T(8,128)(2,1)S(1)}, u32[]{:S(2)}, u32[]{:S(2)}) collective-permute-start(bf16[48,64,128]{2,1,0:T(8,128)(2,1)S(1)} %pad_maximum_fusion.own), channel_id=1, source_target_pairs={{0,16},{16,32},{32,48},{48,64},{64,80},{80,96},{96,112},{1,17},{17... | collective-permute-start | bytes 2359304 | tf_op jit(solution)/shard_map/ppermute | solution.py:41
  14.4 27.4 %copy-start.5 = (f32[64,128]{1,0:T(8,128)S(1)}, f32[64,128]{1,0:T(8,128)}, u32[]{:S(2)}) copy-start(f32[64,128]{1,0:T(8,128)} %diag.5) | copy-start | bytes 98308
  14.4 27.4 %copy-start.7 = (s32[64,128]{1,0:T(8,128)S(1)}, s32[64,128]{1,0:T(8,128)}, u32[]{:S(2)}) copy-start(s32[64,128]{1,0:T(8,128)} %offsets.3) | copy-start | bytes 98308
  14.5 0.7 collective-permute-start.4
  15.2 6.7 %collective-permute-start.3 = (s32[1,128]{1,0:T(1,128)S(1)}, s32[1,128]{1,0:T(1,128)S(1)}, u32[]{:S(2)}, u32[]{:S(2)}) collective-permute-start(s32[1,128]{1,0:T(1,128)S(1)} %pad.4.codes), channel_id=1, source_target_pairs={{0,15},{1,0},{2,1},{3,2},{4,3},{5,4},{6,5},{7,6},{8,7},{9,8},{10,9... | collective-permute-start | bytes 1544 | tf_op jit(solution)/shard_map/ppermute | solution.py:45
  21.9 5.9 %collective-permute-start.2 = (s32[1,128]{1,0:T(1,128)S(1)}, s32[1,128]{1,0:T(1,128)S(1)}, u32[]{:S(2)}, u32[]{:S(2)}) collective-permute-start(s32[1,128]{1,0:T(1,128)S(1)} %pad.4.codes), channel_id=1, source_target_pairs={{0,1},{1,2},{2,3},{3,4},{4,5},{5,6},{6,7},{7,8},{8,9},{9,10},{10,1... | collective-permute-start | bytes 1544 | tf_op jit(solution)/shard_map/ppermute | solution.py:45
  27.8 13.9 %copy-start = (bf16[32,64,128]{2,1,0:T(8,128)(2,1)}, bf16[32,64,128]{2,1,0:T(8,128)(2,1)S(1)}, u32[]{:S(2)}) copy-start(bf16[32,64,128]{2,1,0:T(8,128)(2,1)S(1)} %collective-permute-done.9.high) | copy-start | bytes 1572868
  30.3 11.4 %collective-permute-start.10 = (bf16[32,64,128]{2,1,0:T(8,128)(2,1)S(1)}, bf16[32,64,128]{2,1,0:T(8,128)(2,1)S(1)}, u32[]{:S(2)}, u32[]{:S(2)}) collective-permute-start(bf16[32,64,128]{2,1,0:T(8,128)(2,1)S(1)} %get-tuple-element.23), channel_id=1, source_target_pairs={{0,1},{1,2},{2,3},{3,4},{4,5},{5,6},{6,7},{7,8},{8,9},{9,10},{10,1... | collective-permute-start | bytes 1572872 | tf_op jit(solution)/shard_map/ppermute | solution.py:45
  30.4 11.3 %collective-permute-start.11 = (bf16[32,64,128]{2,1,0:T(8,128)(2,1)S(1)}, bf16[32,64,128]{2,1,0:T(8,128)(2,1)S(1)}, u32[]{:S(2)}, u32[]{:S(2)}) collective-permute-start(bf16[32,64,128]{2,1,0:T(8,128)(2,1)S(1)} %get-tuple-element.24), channel_id=1, source_target_pairs={{0,15},{1,0},{2,1},{3,2},{4,3},{5,4},{6,5},{7,6},{8,7},{9,8},{10,9... | collective-permute-start | bytes 1572872 | tf_op jit(solution)/shard_map/ppermute | solution.py:45
  35.2 6.6 %collective-permute-start.12 = (bf16[32,64,128]{2,1,0:T(8,128)(2,1)S(1)}, bf16[32,64,128]{2,1,0:T(8,128)(2,1)S(1)}, u32[]{:S(2)}, u32[]{:S(2)}) collective-permute-start(bf16[32,64,128]{2,1,0:T(8,128)(2,1)S(1)} %get-tuple-element.25), channel_id=1, source_target_pairs={{0,8},{1,9},{2,10},{3,11},{4,12},{5,13},{6,14},{7,15},{8,0},{9,1},... | collective-permute-start | bytes 1572872 | tf_op jit(solution)/shard_map/ppermute | solution.py:49
  41.8 1.0 copy-start.1
  47.2 14.2 %collective-permute-start.14 = (f32[64,128]{1,0:T(8,128)S(1)}, f32[64,128]{1,0:T(8,128)S(1)}, u32[]{:S(2)}, u32[]{:S(2)}) collective-permute-start(f32[64,128]{1,0:T(8,128)S(1)} %get-tuple-element.29.cols), channel_id=1, source_target_pairs={{0,15},{1,0},{2,1},{3,2},{4,3},{5,4},{6,5},{7,6},{8,7},{9,8},{10,9... | collective-permute-start | bytes 98312 | tf_op jit(solution)/shard_map/ppermute | solution.py:45
  55.1 78.9 %collective-permute-start.5 = (bf16[48,64,128]{2,1,0:T(8,128)(2,1)}, bf16[48,64,128]{2,1,0:T(8,128)(2,1)}, u32[]{:S(2)}, u32[]{:S(2)}) collective-permute-start(bf16[48,64,128]{2,1,0:T(8,128)(2,1)} %get-tuple-element.20), channel_id=1, source_target_pairs={{0,1},{1,2},{2,3},{3,4},{4,5},{5,6},{6,7},{7,8},{8,9},{9,10},{10,1... | collective-permute-start | bytes 2359304 | tf_op jit(solution)/shard_map/ppermute | solution.py:45
  55.1 78.9 %collective-permute-start.6 = (bf16[48,64,128]{2,1,0:T(8,128)(2,1)}, bf16[48,64,128]{2,1,0:T(8,128)(2,1)}, u32[]{:S(2)}, u32[]{:S(2)}) collective-permute-start(bf16[48,64,128]{2,1,0:T(8,128)(2,1)} %get-tuple-element.21), channel_id=1, source_target_pairs={{0,15},{1,0},{2,1},{3,2},{4,3},{5,4},{6,5},{7,6},{8,7},{9,8},{10,9... | collective-permute-start | bytes 2359304 | tf_op jit(solution)/shard_map/ppermute | solution.py:45
  59.9 74.2 %collective-permute-start.7 = (bf16[48,64,128]{2,1,0:T(8,128)(2,1)}, bf16[48,64,128]{2,1,0:T(8,128)(2,1)}, u32[]{:S(2)}, u32[]{:S(2)}) collective-permute-start(bf16[48,64,128]{2,1,0:T(8,128)(2,1)} %get-tuple-element.22), channel_id=1, source_target_pairs={{0,8},{1,9},{2,10},{3,11},{4,12},{5,13},{6,14},{7,15},{8,0},{9,1},... | collective-permute-start | bytes 2359304 | tf_op jit(solution)/shard_map/ppermute | solution.py:49
  61.5 8.4 %collective-permute-start.13 = (f32[64,128]{1,0:T(8,128)S(1)}, f32[64,128]{1,0:T(8,128)S(1)}, u32[]{:S(2)}, u32[]{:S(2)}) collective-permute-start(f32[64,128]{1,0:T(8,128)S(1)} %get-tuple-element.29.cols), channel_id=1, source_target_pairs={{0,1},{1,2},{2,3},{3,4},{4,5},{5,6},{6,7},{7,8},{8,9},{9,10},{10,1... | collective-permute-start | bytes 98312 | tf_op jit(solution)/shard_map/ppermute | solution.py:45
  69.9 28.2 %collective-permute-start.16 = (f32[40,128]{1,0:T(8,128)S(1)}, f32[40,128]{1,0:T(8,128)S(1)}, u32[]{:S(2)}, u32[]{:S(2)}) collective-permute-start(f32[40,128]{1,0:T(8,128)S(1)} %pad_maximum_fusion.3), channel_id=1, source_target_pairs={{16,0},{32,16},{48,32},{64,48},{80,64},{96,80},{112,96},{17,1},{33... | collective-permute-start | bytes 61448 | tf_op jit(solution)/shard_map/ppermute | solution.py:41
  96.1 3.1 %collective-permute-start.15 = (f32[40,128]{1,0:T(8,128)S(1)}, f32[40,128]{1,0:T(8,128)S(1)}, u32[]{:S(2)}, u32[]{:S(2)}) collective-permute-start(f32[40,128]{1,0:T(8,128)S(1)} %pad_maximum_fusion.2), channel_id=1, source_target_pairs={{0,16},{16,32},{32,48},{48,64},{64,80},{80,96},{96,112},{1,17},{17... | collective-permute-start | bytes 61448 | tf_op jit(solution)/shard_map/ppermute | solution.py:41
  102.3 0.8 copy-start.3
  121.3 12.7 %copy-start.8 = (s32[64,128]{1,0:T(8,128)S(1)}, s32[64,128]{1,0:T(8,128)}, u32[]{:S(2)}) copy-start(s32[64,128]{1,0:T(8,128)} %offsets.3) | copy-start | bytes 98308
  130.4 1.0 copy-start.4
  131.5 0.8 copy-start.6

commit v2 on v1

v2 whole, which is shorter than its diff:
```python
import functools

import jax
import jax.numpy as jnp
from jax import lax
from jax.experimental import pallas as pl
from jax.experimental.pallas import tpu as pltpu
from jax.sharding import PartitionSpec as P

ROWS = 4
LANES = 128
SPAN = 64
F32 = jnp.float32
BF16 = jnp.bfloat16


def iota(shape, dim):
    return lax.broadcasted_iota(jnp.int32, shape, dim)


def swap(block, axis, odd):
    count = lax.axis_size(axis)
    ends = [(i, i + 1) for i in range(odd, count - 1, 2)]
    if odd and axis == "lon":
        ends.append((count - 1, 0))
    return lax.ppermute(block, axis, ends + [(b, a) for a, b in ends])


def swaps(even_block, odd_block, axis):
    return swap(even_block, axis, 0), swap(odd_block, axis, 1)


def from_pole(block, ends):
    sectors = lax.axis_size("lon")
    pairs = [
        (source * sectors + s, band * sectors + (s + sectors // 2) % sectors)
        for source, band in ends
        for s in range(sectors)
    ]
    return lax.ppermute(block, ("lat", "lon"), pairs)


def from_far(block):
    last = lax.axis_size("lat") - 1
    return from_pole(block, ((0, 0), (last, last)))


def from_far_next(block):
    last = lax.axis_size("lat") - 1
    return from_pole(block, ((1, 0), (last - 1, last)))


def after(block, *others):
    return lax.optimization_barrier((block,) + others)[0]


def coded(depart_lists, tiles):
    bands, sectors = lax.axis_size("lat"), lax.axis_size("lon")
    band, sector = lax.axis_index("lat"), lax.axis_index("lon")
    wanted = depart_lists.reshape(1, -1)
    owner = wanted // tiles
    theirs = owner % sectors
    turn = jnp.where(theirs == (sector ^ 1), 1, 2)
    turn = jnp.where(theirs == (sector + sectors // 2) % sectors, 3, turn)
    turn = jnp.where(theirs == sector, 0, turn)
    source = owner // sectors
    place = jnp.where(source == band, 0, jnp.where(source == (band ^ 1), 1, 2))
    code = turn * SPAN + place * tiles + wanted % tiles
    return jnp.pad(code, ((0, 0), (0, LANES - code.shape[1])), constant_values=4 * SPAN)


def flat(rows):
    return pl.BlockSpec((rows, LANES), lambda g: (0, 0))


def ranks(member):
    before = (iota((LANES, LANES), 0) < iota((LANES, LANES), 1)).astype(BF16)
    ones = jnp.where(member, 1.0, 0.0).astype(BF16)
    return jnp.dot(ones, before, preferred_element_type=F32)


def pack_kernel(count, *refs):
    lists, (own, next_even, next_odd), outs, pick = refs[:count], refs[count : count + 3], refs[count + 3 : -1], refs[-1]

    @pl.when(pl.program_id(0) == 0)
    def _():
        sub = iota((8, LANES), 0)
        codes = jnp.where(sub == 0, lists[0][...], lists[1][...])
        if count > 2:
            far_codes = lists[2][0].astype(F32)[:8].astype(jnp.int32)
            codes = jnp.where(sub == 2, far_codes, codes)
        member = (codes >> 6) == sub + 1
        rank = jnp.where(member, ranks(member), -1.0)
        tile = ((codes & (SPAN - 1)) + 1).astype(F32)
        slot = (iota((64, LANES), 0) >> 2).astype(F32)
        row = (iota((64, 192), 0) & 3).astype(F32)
        col = iota((64, 192), 1).astype(F32)
        for d in range(count):
            hit = rank[d : d + 1] == slot
            held = jnp.sum(jnp.where(hit, tile[d : d + 1], 0.0), axis=1, keepdims=True) - 1.0
            pick[d * 64 : (d + 1) * 64, :] = jnp.where(col == held * 4.0 + row, 1.0, 0.0).astype(BF16)

    def pair(g, carry):
        pool = jnp.concatenate(
            [jnp.concatenate([ref[f] for ref in (own, next_even, next_odd)], axis=0) for f in (2 * g, 2 * g + 1)],
            axis=1,
        )
        got = jnp.dot(pick[...], pool, preferred_element_type=F32).astype(BF16)
        for d, out in enumerate(outs):
            for half in range(2):
                out[2 * g + half] = got[d * 64 : (d + 1) * 64, half * LANES : (half + 1) * LANES]
        return carry

    lax.fori_loop(0, 8, pair, 0, unroll=8)


def pack(lists, bands, blocks, of):
    levels, count = 16 * blocks, len(lists)
    source = pl.BlockSpec((16, 64, LANES), lambda g: (of(g), 0, 0))
    block = pl.BlockSpec((16, 64, LANES), lambda g: (g, 0, 0))
    rows = [flat(1)] * 2 + [pl.BlockSpec((1, 64, LANES), lambda g: (32, 0, 0))] * (count - 2)
    return pl.pallas_call(
        functools.partial(pack_kernel, count),
        grid=(blocks,),
        in_specs=rows + [source] * 3,
        out_specs=[block] * count,
        out_shape=[jax.ShapeDtypeStruct((levels, 64, LANES), BF16)] * count,
        scratch_shapes=[pltpu.VMEM((count * 64, 192), BF16)],
        compiler_params=pltpu.CompilerParams(vmem_limit_bytes=32 << 20),
        cost_estimate=pl.CostEstimate(
            flops=levels * 2 * 192 * 192 * LANES, bytes_accessed=levels * 5 * 64 * LANES * 2, transcendentals=0
        ),
        name="pack",
    )(*lists, *bands)


def set_gather(codes_ref, gather, far_slots):
    codes = jnp.broadcast_to(codes_ref[...], (8, LANES))
    turn = codes >> 6
    sub = iota((8, LANES), 0)
    rank = ranks(turn == sub)
    turn, tile = turn[:1], codes[:1] & (SPAN - 1)
    place = jnp.where(turn == 0, tile.astype(F32), -1.0)
    place = jnp.where(turn == 1, 48.0 + rank[1:2], place)
    place = jnp.where(turn == 2, 64.0 + rank[2:3], place)
    if far_slots:
        across = 80.0 + rank[3:4]
    else:
        across = ((tile & 15) + jnp.where(tile < 16, 80, 96)).astype(F32)
    place = jnp.where(turn == 3, across, place)
    row = iota((LANES, LANES), 0)
    mine = iota((LANES, LANES), 1) == 2 * (row & 15) + (row >> 6)
    place = jnp.sum(jnp.where(mine, place, 0.0), axis=1, keepdims=True)
    within = ((iota(gather.shape, 0) >> 4) & 3).astype(F32)
    col = iota(gather.shape, 1).astype(F32)
    gather[...] = jnp.where(col == place * 4.0 + within, 1.0, 0.0).astype(BF16)


def every_fourth(q):
    return pl.ds(q, 16, stride=4)


def set_weights(offsets, weights, coef):
    for q in range(4):
        offset = offsets[every_fourth(q), :]
        points = [weights[m, every_fourth(q), :] for m in range(4)]
        for r in range(8):
            value = jnp.zeros((16, LANES), F32)
            for m in range(4):
                if 0 <= r - m <= 4:
                    value = jnp.where(offset == r - m, points[m], value)
            coef[q * 8 + r] = value


def interpolate(gather, coef, first_pools, second_pools, first, second=None):
    second = first if second is None else second
    pool = jnp.concatenate(
        [
            jnp.concatenate([ref[f] for ref in pools], axis=0)
            for pools, f in ((first_pools, first), (second_pools, second))
        ],
        axis=1,
    )
    rows = jnp.dot(gather[...], pool, preferred_element_type=F32)
    out = []
    for q in range(4):
        sums = [None, None]
        for r in range(8):
            weight = coef[q * 8 + r]
            for h in range(2):
                term = weight * rows[r * 16 : (r + 1) * 16, h * LANES : (h + 1) * LANES]
                sums[h] = term if r == 0 else sums[h] + term
        out.append(sums)
    return out


def levels_block(of):
    return pl.BlockSpec((16, 64, LANES), lambda g: (of(g), 0, 0))


SMEM = pl.BlockSpec(memory_space=pltpu.SMEM)
VMEM = pl.BlockSpec(memory_space=pltpu.VMEM)
WEIGHTS = pl.BlockSpec((4, 64, LANES), lambda g: (0, 0, 0))


def scratch(pool):
    return [
        pltpu.VMEM((LANES, 64 * pool), BF16), pltpu.VMEM((32, 16, LANES), F32), pltpu.VMEM((16, 64, LANES), F32)
    ]


def first_kernel(scale, codes, offsets, weights, diag, *refs):
    middle, top = refs[0:7], refs[7:14]
    adv, rhs, cols, edge_even, edge_odd, own_up, own_down, gather, coef, tmp = refs[14:]
    set_gather(codes, gather, False)
    set_weights(offsets, weights, coef)

    def level(l, carry):
        values = interpolate(gather, coef, middle, top, l)
        for q in range(4):
            tmp[l, every_fourth(q), :] = values[q][0]
            rhs[l, every_fourth(q), :] = values[q][1] + 0.5 * values[q][0]
        return carry

    lax.fori_loop(0, 16, level, 0, unroll=8)
    group = iota((64, LANES), 1) >> 2
    packed = jnp.where(group == 16, pltpu.roll(diag[...], 65, 1), 0.0)
    for l in range(16):
        adv[l] = tmp[l].astype(BF16)
        value = rhs[l] / (4.0 + diag[...] * scale[l])
        for ref, ends in ((own_up, (0, 1)), (own_down, (63, 62))):
            for place, r in enumerate(ends):
                ref[16 * place + l : 16 * place + l + 1, :] = value[r : r + 1]
        packed = jnp.where(group == l, pltpu.roll(value, 2 + 4 * l, 1), packed)
    cols[...] = packed
    for ref, r in ((own_up, 0), (own_down, 63)):
        ref[32:33, :] = diag[r : r + 1, :]
        ref[33:40, :] = jnp.ones((7, LANES), F32)
    up, down = own_up[...], own_down[...]
    even_band = lax.rem(lax.axis_index("lat"), 2) == 0
    edge_even[...] = jnp.where(even_band, down, up)
    edge_odd[...] = jnp.where(even_band, up, down)


def first_levels(scale, codes, offsets, weights, diag, bands, slots, far):
    slab = jax.ShapeDtypeStruct((16, 64, LANES), F32)
    edge = jax.ShapeDtypeStruct((40, LANES), F32)
    whole = levels_block(lambda g: 0)
    pools, specs = [], []
    for half in range(2):
        pools += [*bands, *slots, *far]
        specs += [levels_block(lambda g, half=half: 2 + 2 * half)] * 3 + [levels_block(lambda g, half=half: half)] * 4
    return pl.pallas_call(
        first_kernel,
        grid=(1,),
        in_specs=[SMEM, flat(1), flat(64), WEIGHTS, flat(64)] + specs,
        out_specs=[levels_block(lambda g: 2), whole, flat(64)] + [flat(40)] * 4,
        out_shape=[
            jax.ShapeDtypeStruct((64, 64, LANES), BF16), slab, jax.ShapeDtypeStruct((64, LANES), F32)
        ] + [edge] * 4,
        scratch_shapes=scratch(7),
        compiler_params=pltpu.CompilerParams(vmem_limit_bytes=60 << 20),
        cost_estimate=pl.CostEstimate(flops=32 * 2 * 128 * 448 * 128, bytes_accessed=6 << 20, transcendentals=0),
        name="first_levels",
    )(scale, codes, offsets, weights, diag, *pools)


def other_kernel(codes, offsets, weights, *refs):
    pools, (start, adv, gather, coef, tmp) = refs[:6], refs[6:]

    @pl.when(pl.program_id(0) == 0)
    def _():
        set_gather(codes, gather, True)
        set_weights(offsets, weights, coef)

    def pair(g, carry):
        values = interpolate(gather, coef, pools, pools, 2 * g, 2 * g + 1)
        for h in range(2):
            for q in range(4):
                tmp[2 * g + h, every_fourth(q), :] = values[q][h]
        return carry

    lax.fori_loop(0, 8, pair, 0, unroll=8)
    for f in range(16):
        adv[f] = tmp[f].astype(BF16)


def other_levels(codes, offsets, weights, bands, slots, start):
    return pl.pallas_call(
        other_kernel,
        grid=(3,),
        in_specs=[flat(1), flat(64), WEIGHTS]
        + [levels_block(lambda g: g + g // 2)] * 3
        + [levels_block(lambda g: g)] * 3
        + [pl.BlockSpec(memory_space=pl.ANY)],
        out_specs=levels_block(lambda g: g + g // 2),
        out_shape=jax.ShapeDtypeStruct(start.shape, start.dtype),
        scratch_shapes=scratch(6),
        input_output_aliases={9: 0},
        compiler_params=pltpu.CompilerParams(vmem_limit_bytes=32 << 20),
        cost_estimate=pl.CostEstimate(flops=48 * 2 * 128 * 448 * 128, bytes_accessed=6 << 20, transcendentals=0),
        name="other_levels",
    )(codes, offsets, weights, *bands, *slots, start)


def sum_kernel(scale, rhs, diag, cols, own_up, own_down, cols_even, cols_odd, edge_even, edge_odd, n0, n1, sums, rowsums):
    lane = iota((64, LANES), 1)
    even_band = lax.rem(lax.axis_index("lat"), 2) == 0
    even_sector = lax.rem(lax.axis_index("lon"), 2) == 0
    even, odd = edge_even[...], edge_odd[...]
    above, below = jnp.where(even_band, odd, even), jnp.where(even_band, even, odd)
    even, odd = cols_even[...], cols_odd[...]
    left, right = jnp.where(even_sector, odd, even), jnp.where(even_sector, even, odd)
    spread = jnp.zeros((1, LANES), F32)
    column = jnp.zeros((16, LANES), F32)
    for l in range(16):
        spread = jnp.where((lane[:1] >> 2) == l, scale[l], spread)
        column = jnp.where(iota((16, LANES), 0) == l, scale[l], column)
    row16, lane16 = iota((16, LANES), 0), lane[:16]

    west_even, west_odd = left[64:80, LANES - 1 : LANES], left[80:96, LANES - 1 : LANES]
    east_even, east_odd = right[64:80, 0:1], right[80:96, 0:1]
    corners = [
        [jnp.where(even_band, west_odd, west_even), jnp.where(even_band, east_odd, east_even)],
        [jnp.where(even_band, west_even, west_odd), jnp.where(even_band, east_even, east_odd)],
    ]

    def spread_corner(column, which):
        return jnp.sum(jnp.where(lane16 == 4 * row16 + which, column, 0.0), axis=0, keepdims=True)

    def rim_row(edge, inner, west, east):
        near, second, flag = edge[0:16, :], edge[16:32, :], edge[33:34, :]
        beside = jnp.where(lane16 == 0, west, pltpu.roll(near, 1, 1))
        beside = beside + jnp.where(lane16 == LANES - 1, east, pltpu.roll(near, LANES - 1, 1))
        return flag * (second + inner + beside) / (4.0 + edge[32:33, :] * column)

    top, bottom = rim_row(above, own_up[0:16, :], *corners[0]), rim_row(below, own_down[0:16, :], *corners[1])

    def rim_col(edge, side, which, toward, diag_lane):
        values = edge[0:64]
        first, last = (spread_corner(pair[side], which) for pair in corners)
        up = jnp.concatenate([first, values[:-1]], axis=0)
        down = jnp.concatenate([values[1:], last], axis=0)
        outer = pltpu.roll(values, toward % LANES, 1)
        inner = pltpu.roll(cols[...], -toward % LANES, 1)
        coef = 4.0 + values[:, diag_lane : diag_lane + 1] * spread
        return (up + down + outer + inner) / coef

    west = rim_col(left, 0, 1, 1, 64)
    east = rim_col(right, 1, 2, -1, 65)

    def beside(value, west_col, east_col, upper, lower):
        total = jnp.where(lane == 0, west_col, pltpu.roll(value, 1, 1))
        total = total + jnp.where(lane == LANES - 1, east_col, pltpu.roll(value, LANES - 1, 1))
        total = total + jnp.concatenate([upper, value[:-1]], axis=0)
        return total + jnp.concatenate([value[1:], lower], axis=0)

    for l in range(16):
        start = rhs[l]
        inverse = 1.0 / (4.0 + diag[...] * scale[l])
        value = start * inverse
        around = beside(
            value, left[0:64, 4 * l + 1 : 4 * l + 2], right[0:64, 4 * l + 2 : 4 * l + 3], above[l : l + 1, :], below[l : l + 1, :]
        )
        n0[l] = around
        again = around * inverse
        second = beside(
            again, west[:, 4 * l + 1 : 4 * l + 2], east[:, 4 * l + 2 : 4 * l + 3], top[l : l + 1], bottom[l : l + 1]
        )
        n1[l] = second
        for k, term in enumerate((start * value, start * again, around * again, second * again)):
            part = term[0:8]
            for j in range(1, 8):
                part = part + term[8 * j : 8 * j + 8]
            rowsums[k * 16 + l : k * 16 + l + 1, :] = jnp.sum(part, axis=0, keepdims=True)
    total = jnp.sum(rowsums[...], axis=1, keepdims=True)
    packed = jnp.zeros((8, LANES), F32)
    for j in range(8):
        packed = jnp.where(lane[:8] == j, total[8 * j : 8 * j + 8], packed)
    for j in range(sums.shape[0]):
        sums[j] = packed


def level_sums(scale, rhs, diag, cols, own, cols_rim, edges):
    slab = jax.ShapeDtypeStruct((16, 64, LANES), F32)
    return pl.pallas_call(
        sum_kernel,
        in_specs=[SMEM] + [VMEM] * 9,
        out_specs=[VMEM] * 3,
        out_shape=[slab, slab, jax.ShapeDtypeStruct((lax.axis_size("lat"), 8, LANES), F32)],
        scratch_shapes=[pltpu.VMEM((64, LANES), F32)],
        compiler_params=pltpu.CompilerParams(vmem_limit_bytes=60 << 20),
        cost_estimate=pl.CostEstimate(flops=1 << 22, bytes_accessed=2 << 20, transcendentals=0),
        name="level_sums",
    )(scale, rhs, diag, cols, *own, *cols_rim, *edges)


def last_kernel(scale, parts, rhs, diag, n0, n1, pressure, residual):
    total = parts[0]
    for j in range(1, parts.shape[0]):
        total = total + parts[j]
    lane = iota((8, LANES), 1)

    def of(k, half):
        return jnp.sum(jnp.where(lane == 2 * k + half, total, 0.0), axis=1, keepdims=True)

    for half in range(2):
        s0, s1, s2, s3 = (of(k, half) for k in range(4))
        curve = s0 - s1
        step = s0 / curve
        keep = -s1 / curve
        norm = keep * keep * s0 + 2.0 * keep * step * s1 + step * step * s2
        ratio = norm / s0
        bend = norm - (keep * keep * s1 + 2.0 * keep * step * s2 + step * step * s3)
        other = norm / (bend - ratio * ratio * curve)
        along = other * (keep + ratio)
        across = other * step
        fit_z, fit_p = step + along, across
        fit_r, fit_n0, fit_n1 = keep - along, step + along - across, across
        for s in range(8):
            l = 8 * half + s
            at = lambda column: column[s : s + 1]
            inverse = 1.0 / (4.0 + diag[...] * scale[l])
            start, around = rhs[l], n0[l]
            pressure[l] = (at(fit_z) * start + at(fit_p) * around) * inverse
            residual[l] = at(fit_r) * start + at(fit_n0) * around + at(fit_n1) * n1[l]


def last_step(scale, parts, rhs, diag, n0, n1):
    slab = jax.ShapeDtypeStruct((16, 64, LANES), F32)
    return pl.pallas_call(
        last_kernel,
        in_specs=[SMEM] + [VMEM] * 5,
        out_specs=[VMEM] * 2,
        out_shape=[slab, slab],
        compiler_params=pltpu.CompilerParams(vmem_limit_bytes=60 << 20),
        cost_estimate=pl.CostEstimate(flops=1 << 21, bytes_accessed=3 << 20, transcendentals=0),
        name="last_step",
    )(scale, parts, rhs, diag, n0, n1)


def exchange(parts, axis):
    return lax.all_to_all(parts, axis, split_axis=0, concat_axis=0, tiled=True)


def on_device(fields, depart_lists, stencil_offsets, interp_weights, diag_coef, level_scale):
    tiles = depart_lists.shape[0]
    codes = coded(depart_lists, tiles)
    bands = (fields,) + swaps(fields, fields, "lat")
    lists = swaps(codes, codes, "lon")
    rows = jnp.broadcast_to(codes.astype(BF16)[None], (1, 64, LANES))
    first = after(jnp.concatenate([fields[32:48], fields[64:80], rows], axis=0), *lists)
    first_far = (from_far(first), from_far_next(first))
    first_out = pack(lists, bands, 2, lambda g: 2 + 2 * g)
    first_slots = swaps(*first_out, "lon")
    later = after(lists[0], *first_out, *first_far)
    *other_out, other_far = pack((later, lists[1], first_far[0]), bands, 3, lambda g: g + g // 2)
    other_slots = swaps(*other_out, "lon")
    first_slots = (after(first_slots[0], *other_out), first_slots[1])
    adv, rhs, cols, *edges = first_levels(
        level_scale, codes, stencil_offsets, interp_weights, diag_coef, bands, first_slots, first_far
    )
    own, edges = edges[2:], swaps(*edges[:2], "lat")
    rim = jnp.concatenate([cols, edges[0][:16], edges[1][:16]], axis=0)
    cols_rim = swaps(rim, rim, "lon")
    other_far = from_far(after(other_far, *cols_rim))
    n0, n1, parts = level_sums(level_scale, rhs, diag_coef, cols, own, cols_rim, edges)
    parts = jnp.sum(exchange(parts, "lat"), axis=0)
    parts = exchange(jnp.broadcast_to(parts[None], (lax.axis_size("lon"),) + parts.shape), "lon")
    adv = other_levels(codes, stencil_offsets, interp_weights, bands, other_slots + (other_far,), adv)
    parts = after(parts, adv)
    pressure, residual = last_step(level_scale, parts, rhs, diag_coef, n0, n1)
    return (adv, pressure, residual)


def solution(mesh):
    placed = (
        P(None, "lat", "lon"),
        P("lat", "lon", None),
        P("lat", "lon"),
        P(None, "lat", "lon"),
        P("lat", "lon"),
        P(),
    )
    return jax.shard_map(
        on_device,
        mesh=mesh,
        in_specs=placed,
        out_specs=(P(None, "lat", "lon"), P(None, "lat", "lon"), P(None, "lat", "lon")),
        check_vma=False,
    )
```

time: 141 us -> 98.3 us (0.70)
  starting transfers between devices: 63.7 us -> 36.6 us
  blocking collectives: 26.5 us -> 9.19 us
    ppermute x17 -> x15, starting transfers between devices: 63.7 us -> 32.4 us  [the longest x12 25.9 us: swap(): return lax.ppermute(block, axis, ends + [(b, a) for a, b in ends])]
    all_to_all x2 -> x1, blocking collectives: 26.5 us -> 9.19 us  [exchange(): return lax.all_to_all(parts, axis, split_axis=0, concat_axis=0, tiled=True)]
    all_to_all x0 -> x1, starting transfers between devices: none -> 4.15 us  [exchange(): return lax.all_to_all(parts, axis, split_axis=0, concat_axis=0, tiled=True)]
    ppermute x17 -> x15, waiting for transfers between devices: 22 us -> 22.9 us  [the longest x12 22.9 us: swap(): return lax.ppermute(block, axis, ends + [(b, a) for a, b in ends])]
    unnamed x23 -> x37, local copies, waits for them, and re-layouts: 3.76 us -> 3.17 us
  transfers between devices with their start and end apart: 17 -> 16, of which waited for: 5 -> 7; matrix products, arithmetic and copies ran while one was open for 1% -> 4% of each run, Pallas kernels for 11% -> 14%
where the time goes in v2:
time: 98.3 us; the launch traced here: 97.5 us
  starting transfers between devices  36.6 us (37%)
  waiting for transfers between devices  22.9 us (23%)
  Pallas kernels  21.3 us (22%)
  blocking collectives  9.19 us (9%)
  local copies, waits for them, and re-layouts  4.97 us (5%)
  other arithmetic  1.65 us (2%)
    ppermute x12, starting transfers between devices, swap(): return lax.ppermute(block, axis, ends + [(b, a) for a, b in ends])  25.9 us
    ppermute x12, waiting for transfers between devices, swap(): return lax.ppermute(block, axis, ends + [(b, a) for a, b in ends])  22.9 us
    all_to_all x1, blocking collectives, exchange(): return lax.all_to_all(parts, axis, split_axis=0, concat_axis=0, tiled=True)  9.19 us
    ppermute x3, starting transfers between devices, from_pole(): return lax.ppermute(block, ('lat', 'lon'), pairs)  6.48 us
    pallas_call x2, Pallas kernels, pack(): pl.pallas_call(functools.partial(pack_kernel, count), grid=(blocks,), in_...  5.16 us
    pallas_call x1, Pallas kernels, first_levels(): pl.pallas_call(first_kernel, grid=(1,), in_specs=[SMEM, flat(1), flat(64)...  4.58 us
    pallas_call x1, Pallas kernels, level_sums(): pl.pallas_call(sum_kernel, in_specs=[SMEM] + [VMEM] * 9, out_specs=[VMEM]...  4.56 us
    pallas_call x1, Pallas kernels, other_levels(): pl.pallas_call(other_kernel, grid=(3,), in_specs=[flat(1), flat(64), WEIG...  4.34 us
  transfers between devices with their start and end apart: 16, of which 7 were waited for; matrix products, arithmetic and copies ran while one was open for 4% of the time, Pallas kernels for 14%

profile of v2, /device:TPU:1, one launch (start us, length us, event | category | flops | bytes accessed | tf_op | source)
XLA Modules:
  0.0 97.5 jit_solution(11356128692964520677)
XLA Ops:
  0.6 4.7 %collective-permute-start.1 = (bf16[80,64,128]{2,1,0:T(8,128)(2,1)}, bf16[80,64,128]{2,1,0:T(8,128)(2,1)S(1)}, u32[]{:S(2)}, u32[]{:S(2)}) collective-permute-start(bf16[80,64,128]{2,1,0:T(8,128)(2,1)} %refs_0_.3), channel_id=1, source_target_pairs={{16,32},{48,64},{80,96},{32,16},{64,48},{96,80},{17,33},{49,65},{8... | collective-permute-start | bytes 3932168 | tf_op jit(solution)/shard_map/ppermute | solution.py:26
  5.5 0.8 copy.11
  6.4 6.0 %collective-permute-start.3 = (s32[1,128]{1,0:T(1,128)S(1)}, s32[1,128]{1,0:T(1,128)S(1)}, u32[]{:S(2)}, u32[]{:S(2)}) collective-permute-start(s32[1,128]{1,0:T(1,128)S(1)} %get-tuple-element.50.codes), channel_id=1, source_target_pairs={{1,2},{3,4},{5,6},{7,8},{9,10},{11,12},{13,14},{15,0},{2,1},{4,3},... | collective-permute-start | bytes 1544 | tf_op jit(solution)/shard_map/ppermute | solution.py:26
  12.4 1.1 %fusion.4 = (bf16[16,64,128]{2,1,0:T(8,128)(2,1)S(1)}, bf16[16,64,128]{2,1,0:T(8,128)(2,1)S(1)}) fusion(bf16[80,64,128]{2,1,0:T(8,128)(2,1)} %refs_0_.3), kind=kLoop, calls=%fused_computation.22 | loop fusion | bytes 1048576 | tf_op jit(solution)/shard_map/slice | solution.py:452
  13.6 1.2 %collective-permute-done.2.refs_0_ = s32[1,128]{1,0:T(1,128)S(1)} collective-permute-done((s32[1,128]{1,0:T(1,128)S(1)}, s32[1,128]{1,0:T(1,128)S(1)}, u32[]{:S(2)}, u32[]{:S(2)}) %collective-permute-start.2) | collective-permute-done | bytes 544 | tf_op jit(solution)/shard_map/ppermute | solution.py:26
  14.8 4.2 %collective-permute-start.5 = (bf16[33,64,128]{2,1,0:T(8,128)(2,1)S(1)}, bf16[33,64,128]{2,1,0:T(8,128)(2,1)S(1)}, u32[]{:S(2)}, u32[]{:S(2)}) collective-permute-start(bf16[33,64,128]{2,1,0:T(8,128)(2,1)S(1)} %pad_maximum_fusion), channel_id=1, source_target_pairs={{16,8},{17,9},{18,10},{19,11},{20,12},{21,13},{22,14},{23,15},{24,... | collective-permute-start | bytes 1622024 | tf_op jit(solution)/shard_map/ppermute | solution.py:40
  19.8 1.1 %collective-permute-done.1.refs_4_.refs_5_.refs_2_.refs_9_ = bf16[80,64,128]{2,1,0:T(8,128)(2,1)S(1)} collective-permute-done((bf16[80,64,128]{2,1,0:T(8,128)(2,1)}, bf16[80,64,128]{2,1,0:T(8,128)(2,1)S(1)}, u32[]{:S(2)}, u32[]{:S(2)}) %collective-permute-start.1) | collective-permute-done | bytes 1310752 | tf_op jit(solution)/shard_map/ppermute | solution.py:26
  20.9 2.0 %pack.2 = (bf16[32,64,128]{2,1,0:T(8,128)(2,1)S(1)}, bf16[32,64,128]{2,1,0:T(8,128)(2,1)S(1)}) custom-call(s32[1,128]{1,0:T(1,128)S(1)} %collective-permute-done.2.refs_0_, s32[1,128]{1,0:T(1,128)S(1)} %collective-permute-done.3.refs_1_, bf16[80,64,128]{2,1,0:T(8,128)(2,1)S(1)} %copy-done, ...), custom_call_target="tpu_custom_call" | custom-call | flops 301989888 | bytes 2621440 | tf_op jit(solution)/shard_map/pack/pallas_call | solution.py:122
  22.9 2.0 %collective-permute-start.8 = (bf16[32,64,128]{2,1,0:T(8,128)(2,1)S(1)}, bf16[32,64,128]{2,1,0:T(8,128)(2,1)S(1)}, u32[]{:S(2)}, u32[]{:S(2)}) collective-permute-start(bf16[32,64,128]{2,1,0:T(8,128)(2,1)S(1)} %get-tuple-element.25), channel_id=1, source_target_pairs={{0,1},{2,3},{4,5},{6,7},{8,9},{10,11},{12,13},{14,15},{1,0},{3,2},... | collective-permute-start | bytes 1572872 | tf_op jit(solution)/shard_map/ppermute | solution.py:26
  24.9 4.4 %collective-permute-start.9 = (bf16[32,64,128]{2,1,0:T(8,128)(2,1)S(1)}, bf16[32,64,128]{2,1,0:T(8,128)(2,1)}, u32[]{:S(2)}, u32[]{:S(2)}) collective-permute-start(bf16[32,64,128]{2,1,0:T(8,128)(2,1)S(1)} %get-tuple-element.26), channel_id=1, source_target_pairs={{1,2},{3,4},{5,6},{7,8},{9,10},{11,12},{13,14},{15,0},{2,1},{4,3},... | collective-permute-start | bytes 1572872 | tf_op jit(solution)/shard_map/ppermute | solution.py:26
  29.4 0.8 copy-done.12
  30.2 3.1 %pack.3 = (bf16[48,64,128]{2,1,0:T(8,128)(2,1)S(1)}, bf16[48,64,128]{2,1,0:T(8,128)(2,1)S(1)}, bf16[48,64,128]{2,1,0:T(8,128)(2,1)S(1)}) custom-call(s32[1,128]{1,0:T(1,128)S(1)} %collective-permute-done.2.refs_0_, s32[1,128]{1,0:T(1,128)S(1)} %collective-permute-done.3.refs_1_, bf16[33,64,128]{2,1,0:T(8,128)(2,1)S(1)} %collective-permute-done.4.refs_2_.refs_5_.refs_12_, ...), custom_call_target="tpu_custom_call" | custom-call | flops 452984832 | bytes 3932160 | tf_op jit(solution)/shard_map/pack/pallas_call | solution.py:122
  33.4 4.0 %collective-permute-done.8.refs_3_.refs_10_ = bf16[32,64,128]{2,1,0:T(8,128)(2,1)S(1)} collective-permute-done((bf16[32,64,128]{2,1,0:T(8,128)(2,1)S(1)}, bf16[32,64,128]{2,1,0:T(8,128)(2,1)S(1)}, u32[]{:S(2)}, u32[]{:S(2)}) %collective-permute-start.8) | collective-permute-done | bytes 524320 | tf_op jit(solution)/shard_map/ppermute | solution.py:26
  37.4 0.8 copy-done.13
  38.2 6.7 %collective-permute-done.9.refs_4_.refs_11_ = bf16[32,64,128]{2,1,0:T(8,128)(2,1)} collective-permute-done((bf16[32,64,128]{2,1,0:T(8,128)(2,1)S(1)}, bf16[32,64,128]{2,1,0:T(8,128)(2,1)}, u32[]{:S(2)}, u32[]{:S(2)}) %collective-permute-start.9) | collective-permute-done | bytes 524320 | tf_op jit(solution)/shard_map/ppermute | solution.py:26
  44.9 4.6 %first_levels.1 = (bf16[64,64,128]{2,1,0:T(8,128)(2,1)}, f32[16,64,128]{2,1,0:T(8,128)}, f32[64,128]{1,0:T(8,128)}, f32[40,128]{1,0:T(8,128)}, f32[40,128]{1,0:T...) custom-call(f32[16]{0:T(128)} %scale.5, s32[1,128]{1,0:T(1,128)} %copy-done.7, s32[64,128]{1,0:T(8,128)} %offsets.3, ...), custom_call_target="tpu_custom_call" | custom-call | flops 469762048 | bytes 6291456 | tf_op jit(solution)/shard_map/first_levels/pallas_call | solution.py:253
  50.0 1.9 %collective-permute-start.11 = (f32[40,128]{1,0:T(8,128)}, f32[40,128]{1,0:T(8,128)S(1)}, u32[]{:S(2)}, u32[]{:S(2)}) collective-permute-start(f32[40,128]{1,0:T(8,128)} %get-tuple-element.35), channel_id=1, source_target_pairs={{16,32},{48,64},{80,96},{32,16},{64,48},{96,80},{17,33},{49,65},{8... | collective-permute-start | bytes 61448 | tf_op jit(solution)/shard_map/ppermute | solution.py:26
  51.9 3.4 %collective-permute-done.11.edge_odd = f32[40,128]{1,0:T(8,128)S(1)} collective-permute-done((f32[40,128]{1,0:T(8,128)}, f32[40,128]{1,0:T(8,128)S(1)}, u32[]{:S(2)}, u32[]{:S(2)}) %collective-permute-start.11) | collective-permute-done | bytes 20512 | tf_op jit(solution)/shard_map/ppermute | solution.py:26
  55.3 0.8 pad_maximum_fusion.1
  56.0 3.2 %collective-permute-start.13 = (f32[96,128]{1,0:T(8,128)S(1)}, f32[96,128]{1,0:T(8,128)S(1)}, u32[]{:S(2)}, u32[]{:S(2)}) collective-permute-start(f32[96,128]{1,0:T(8,128)S(1)} %pad_maximum_fusion.1), channel_id=1, source_target_pairs={{1,2},{3,4},{5,6},{7,8},{9,10},{11,12},{13,14},{15,0},{2,1},{4,3},... | collective-permute-start | bytes 147464 | tf_op jit(solution)/shard_map/ppermute | solution.py:26
  59.2 1.5 %collective-permute-start.6 = (bf16[48,64,128]{2,1,0:T(8,128)(2,1)}, bf16[48,64,128]{2,1,0:T(8,128)(2,1)S(1)}, u32[]{:S(2)}, u32[]{:S(2)}) collective-permute-start(bf16[48,64,128]{2,1,0:T(8,128)(2,1)} %copy-done.11), channel_id=1, source_target_pairs={{0,1},{2,3},{4,5},{6,7},{8,9},{10,11},{12,13},{14,15},{1,0},{3,2},... | collective-permute-start | bytes 2359304 | tf_op jit(solution)/shard_map/ppermute | solution.py:26
  60.7 1.6 %collective-permute-start.7 = (bf16[48,64,128]{2,1,0:T(8,128)(2,1)}, bf16[48,64,128]{2,1,0:T(8,128)(2,1)}, u32[]{:S(2)}, u32[]{:S(2)}) collective-permute-start(bf16[48,64,128]{2,1,0:T(8,128)(2,1)} %copy-done.10), channel_id=1, source_target_pairs={{1,2},{3,4},{5,6},{7,8},{9,10},{11,12},{13,14},{15,0},{2,1},{4,3},... | collective-permute-start | bytes 2359304 | tf_op jit(solution)/shard_map/ppermute | solution.py:26
  62.3 0.7 collective-permute-done.12.cols_even
  63.0 1.5 %collective-permute-start.14 = (bf16[48,64,128]{2,1,0:T(8,128)(2,1)}, bf16[48,64,128]{2,1,0:T(8,128)(2,1)}, u32[]{:S(2)}, u32[]{:S(2)}) collective-permute-start(bf16[48,64,128]{2,1,0:T(8,128)(2,1)} %copy-done.9), channel_id=1, source_target_pairs={{0,8},{1,9},{2,10},{3,11},{4,12},{5,13},{6,14},{7,15},{8,0},{9,1},... | collective-permute-start | bytes 2359304 | tf_op jit(solution)/shard_map/ppermute | solution.py:40
  64.6 4.6 %level_sums.1 = (f32[16,64,128]{2,1,0:T(8,128)}, f32[16,64,128]{2,1,0:T(8,128)}, f32[8,8,128]{2,1,0:T(8,128)}) custom-call(f32[16]{0:T(128)} %scale.5, f32[16,64,128]{2,1,0:T(8,128)} %get-tuple-element.38.rhs, f32[64,128]{1,0:T(8,128)} %diag.5, f32[64,128]{1,0:T(8,128)} %get-tuple-element.33.cols, f32[40,128]{1,0:T(8,128)} %get-tuple-element.39.own_up, ...), custom_call_target="tpu_custom_call" | custom-call | flops 4194304 | bytes 2097152 | tf_op jit(solution)/shard_map/level_sums/pallas_call | solution.py:386
  69.2 9.2 %all_to_all.10 = f32[8,8,128]{2,1,0:T(8,128)} all-to-all(f32[8,8,128]{2,1,0:T(8,128)} %get-tuple-element.41), channel_id=1, replica_groups=mesh['lat'=8,'lon'=16] {'lat'}, dimensions={0} | all-to-all | bytes 65536 | tf_op jit(solution)/shard_map/all_to_all | solution.py:443
  78.4 0.8 reduce_sum.9
  79.8 4.2 %all-to-all-start.1 = ((f32[16,8,128]{2,1,0:T(8,128)}), f32[16,8,128]{2,1,0:T(8,128)}, u32[]{:S(2)}, u32[]{:S(2)}) async-start(f32[16,8,128]{2,1,0:T(8,128)} %broadcast_in_dim.32), calls=%async_computation.1 | async-start | bytes 131072 | tf_op jit(solution)/shard_map/all_to_all | solution.py:443
  83.9 5.7 %collective-permute-done.7.refs_4_ = bf16[48,64,128]{2,1,0:T(8,128)(2,1)} collective-permute-done((bf16[48,64,128]{2,1,0:T(8,128)(2,1)}, bf16[48,64,128]{2,1,0:T(8,128)(2,1)}, u32[]{:S(2)}, u32[]{:S(2)}) %collective-permute-start.7) | collective-permute-done | bytes 786464 | tf_op jit(solution)/shard_map/ppermute | solution.py:26
  89.7 0.7 copy-done.6
  90.5 4.3 %other_levels.1 = bf16[64,64,128]{2,1,0:T(8,128)(2,1)} custom-call(s32[1,128]{1,0:T(1,128)S(1)} %copy-done.8, s32[64,128]{1,0:T(8,128)S(1)} %copy-done.6, f32[4,64,128]{2,1,0:T(8,128)S(1)} %copy-done.5, bf16[80,64,128]{2,1,0:T(8,128)(2,1)S(1)} %copy-done.1, ...), custom_call_target="tpu_custom_call", output_to_operand_aliasing={{}: (9, {})} | custom-call | flops 704643072 | bytes 6291456 | tf_op jit(solution)/shard_map/other_levels/pallas_call | solution.py:289
  94.8 2.7 %last_step.1 = (f32[16,64,128]{2,1,0:T(8,128)}, f32[16,64,128]{2,1,0:T(8,128)}) custom-call(f32[16]{0:T(128)} %scale.5, f32[16,8,128]{2,1,0:T(8,128)} %all-to-all-done.1.parts, f32[16,64,128]{2,1,0:T(8,128)} %get-tuple-element.38.rhs, f32[64,128]{1,0:T(8,128)} %diag.5, f32[16,64,128]{2,1,0:T(8,128)} %get-tuple-element.43.n0, f32[16,64,128]{2,1,0:T(8,128)} %get-tuple-element.44.n1), custom_call_target="tpu_custom_call" | custom-call | flops 2097152 | bytes 3145728 | tf_op jit(solution)/shard_map/last_step/pallas_call | solution.py:431
  (55 shorter events, 2.2 us)
Async XLA Ops:
  0.6 20.2 %copy-start = (bf16[80,64,128]{2,1,0:T(8,128)(2,1)S(1)}, bf16[80,64,128]{2,1,0:T(8,128)(2,1)}, u32[]{:S(2)}) copy-start(bf16[80,64,128]{2,1,0:T(8,128)(2,1)} %refs_0_.3) | copy-start | bytes 3932164
  0.6 20.2 %collective-permute-start.1 = (bf16[80,64,128]{2,1,0:T(8,128)(2,1)}, bf16[80,64,128]{2,1,0:T(8,128)(2,1)S(1)}, u32[]{:S(2)}, u32[]{:S(2)}) collective-permute-start(bf16[80,64,128]{2,1,0:T(8,128)(2,1)} %refs_0_.3), channel_id=1, source_target_pairs={{16,32},{48,64},{80,96},{32,16},{64,48},{96,80},{17,33},{49,65},{8... | collective-permute-start | bytes 3932168 | tf_op jit(solution)/shard_map/ppermute | solution.py:26
  5.4 15.5 %collective-permute-start = (bf16[80,64,128]{2,1,0:T(8,128)(2,1)}, bf16[80,64,128]{2,1,0:T(8,128)(2,1)}, u32[]{:S(2)}, u32[]{:S(2)}) collective-permute-start(bf16[80,64,128]{2,1,0:T(8,128)(2,1)} %refs_0_.3), channel_id=1, source_target_pairs={{0,16},{32,48},{64,80},{96,112},{16,0},{48,32},{80,64},{112,96},{1... | collective-permute-start | bytes 3932168 | tf_op jit(solution)/shard_map/ppermute | solution.py:26
  6.4 16.5 %copy-start.7 = (s32[1,128]{1,0:T(1,128)}, s32[1,128]{1,0:T(1,128)S(1)}, u32[]{:S(2)}) copy-start(s32[1,128]{1,0:T(1,128)S(1)} %get-tuple-element.50.codes) | copy-start | bytes 1540
  6.4 7.2 %collective-permute-start.3 = (s32[1,128]{1,0:T(1,128)S(1)}, s32[1,128]{1,0:T(1,128)S(1)}, u32[]{:S(2)}, u32[]{:S(2)}) collective-permute-start(s32[1,128]{1,0:T(1,128)S(1)} %get-tuple-element.50.codes), channel_id=1, source_target_pairs={{1,2},{3,4},{5,6},{7,8},{9,10},{11,12},{13,14},{15,0},{2,1},{4,3},... | collective-permute-start | bytes 1544 | tf_op jit(solution)/shard_map/ppermute | solution.py:26
  12.4 2.4 %collective-permute-start.2 = (s32[1,128]{1,0:T(1,128)S(1)}, s32[1,128]{1,0:T(1,128)S(1)}, u32[]{:S(2)}, u32[]{:S(2)}) collective-permute-start(s32[1,128]{1,0:T(1,128)S(1)} %get-tuple-element.50.codes), channel_id=1, source_target_pairs={{0,1},{2,3},{4,5},{6,7},{8,9},{10,11},{12,13},{14,15},{1,0},{3,2},... | collective-permute-start | bytes 1544 | tf_op jit(solution)/shard_map/ppermute | solution.py:26
  14.8 14.6 %collective-permute-start.5 = (bf16[33,64,128]{2,1,0:T(8,128)(2,1)S(1)}, bf16[33,64,128]{2,1,0:T(8,128)(2,1)S(1)}, u32[]{:S(2)}, u32[]{:S(2)}) collective-permute-start(bf16[33,64,128]{2,1,0:T(8,128)(2,1)S(1)} %pad_maximum_fusion), channel_id=1, source_target_pairs={{16,8},{17,9},{18,10},{19,11},{20,12},{21,13},{22,14},{23,15},{24,... | collective-permute-start | bytes 1622024 | tf_op jit(solution)/shard_map/ppermute | solution.py:40
  19.1 11.1 %collective-permute-start.4 = (bf16[33,64,128]{2,1,0:T(8,128)(2,1)S(1)}, bf16[33,64,128]{2,1,0:T(8,128)(2,1)S(1)}, u32[]{:S(2)}, u32[]{:S(2)}) collective-permute-start(bf16[33,64,128]{2,1,0:T(8,128)(2,1)S(1)} %pad_maximum_fusion), channel_id=1, source_target_pairs={{0,8},{1,9},{2,10},{3,11},{4,12},{5,13},{6,14},{7,15},{8,0},{9,1},... | collective-permute-start | bytes 1622024 | tf_op jit(solution)/shard_map/ppermute | solution.py:40
  20.9 9.3 %copy-start.2 = (bf16[80,64,128]{2,1,0:T(8,128)(2,1)}, bf16[80,64,128]{2,1,0:T(8,128)(2,1)S(1)}, u32[]{:S(2)}) copy-start(bf16[80,64,128]{2,1,0:T(8,128)(2,1)S(1)} %collective-permute-done.1.refs_4_.refs_5_.refs_2_.refs_9_) | copy-start | bytes 3932164
  22.9 14.5 %collective-permute-start.8 = (bf16[32,64,128]{2,1,0:T(8,128)(2,1)S(1)}, bf16[32,64,128]{2,1,0:T(8,128)(2,1)S(1)}, u32[]{:S(2)}, u32[]{:S(2)}) collective-permute-start(bf16[32,64,128]{2,1,0:T(8,128)(2,1)S(1)} %get-tuple-element.25), channel_id=1, source_target_pairs={{0,1},{2,3},{4,5},{6,7},{8,9},{10,11},{12,13},{14,15},{1,0},{3,2},... | collective-permute-start | bytes 1572872 | tf_op jit(solution)/shard_map/ppermute | solution.py:26
  24.9 19.9 %collective-permute-start.9 = (bf16[32,64,128]{2,1,0:T(8,128)(2,1)S(1)}, bf16[32,64,128]{2,1,0:T(8,128)(2,1)}, u32[]{:S(2)}, u32[]{:S(2)}) collective-permute-start(bf16[32,64,128]{2,1,0:T(8,128)(2,1)S(1)} %get-tuple-element.26), channel_id=1, source_target_pairs={{1,2},{3,4},{5,6},{7,8},{9,10},{11,12},{13,14},{15,0},{2,1},{4,3},... | collective-permute-start | bytes 1572872 | tf_op jit(solution)/shard_map/ppermute | solution.py:26
  29.4 0.8 copy-start.12
  30.2 3.1 %copy-start.4 = (bf16[33,64,128]{2,1,0:T(8,128)(2,1)}, bf16[33,64,128]{2,1,0:T(8,128)(2,1)S(1)}, u32[]{:S(2)}) copy-start(bf16[33,64,128]{2,1,0:T(8,128)(2,1)S(1)} %collective-permute-done.4.refs_2_.refs_5_.refs_12_) | copy-start | bytes 1622020
  33.3 4.1 %copy-start.9 = (bf16[48,64,128]{2,1,0:T(8,128)(2,1)}, bf16[48,64,128]{2,1,0:T(8,128)(2,1)S(1)}, u32[]{:S(2)}) copy-start(bf16[48,64,128]{2,1,0:T(8,128)(2,1)S(1)} %get-tuple-element.36) | copy-start | bytes 2359300
  33.4 4.1 %copy-start.10 = (bf16[48,64,128]{2,1,0:T(8,128)(2,1)}, bf16[48,64,128]{2,1,0:T(8,128)(2,1)S(1)}, u32[]{:S(2)}) copy-start(bf16[48,64,128]{2,1,0:T(8,128)(2,1)S(1)} %get-tuple-element.30) | copy-start | bytes 2359300
  33.4 4.0 %copy-start.11 = (bf16[48,64,128]{2,1,0:T(8,128)(2,1)}, bf16[48,64,128]{2,1,0:T(8,128)(2,1)S(1)}, u32[]{:S(2)}) copy-start(bf16[48,64,128]{2,1,0:T(8,128)(2,1)S(1)} %get-tuple-element.29) | copy-start | bytes 2359300
  38.2 51.5 %copy-start.8 = (s32[1,128]{1,0:T(1,128)S(1)}, s32[1,128]{1,0:T(1,128)}, u32[]{:S(2)}) copy-start(s32[1,128]{1,0:T(1,128)} %copy-done.7) | copy-start | bytes 1540
  44.9 44.8 %copy-start.1 = (bf16[80,64,128]{2,1,0:T(8,128)(2,1)S(1)}, bf16[80,64,128]{2,1,0:T(8,128)(2,1)}, u32[]{:S(2)}) copy-start(bf16[80,64,128]{2,1,0:T(8,128)(2,1)} %refs_0_.3) | copy-start | bytes 3932164
  44.9 44.8 %copy-start.3 = (bf16[80,64,128]{2,1,0:T(8,128)(2,1)S(1)}, bf16[80,64,128]{2,1,0:T(8,128)(2,1)}, u32[]{:S(2)}) copy-start(bf16[80,64,128]{2,1,0:T(8,128)(2,1)} %copy-done.2) | copy-start | bytes 3932164
  49.5 40.2 %copy-start.5 = (f32[4,64,128]{2,1,0:T(8,128)S(1)}, f32[4,64,128]{2,1,0:T(8,128)}, u32[]{:S(2)}) copy-start(f32[4,64,128]{2,1,0:T(8,128)} %weights.3) | copy-start | bytes 393220
  49.5 2.4 %collective-permute-start.10 = (f32[40,128]{1,0:T(8,128)}, f32[40,128]{1,0:T(8,128)S(1)}, u32[]{:S(2)}, u32[]{:S(2)}) collective-permute-start(f32[40,128]{1,0:T(8,128)} %get-tuple-element.34), channel_id=1, source_target_pairs={{0,16},{32,48},{64,80},{96,112},{16,0},{48,32},{80,64},{112,96},{1... | collective-permute-start | bytes 61448 | tf_op jit(solution)/shard_map/ppermute | solution.py:26
  50.0 5.3 %collective-permute-start.11 = (f32[40,128]{1,0:T(8,128)}, f32[40,128]{1,0:T(8,128)S(1)}, u32[]{:S(2)}, u32[]{:S(2)}) collective-permute-start(f32[40,128]{1,0:T(8,128)} %get-tuple-element.35), channel_id=1, source_target_pairs={{16,32},{48,64},{80,96},{32,16},{64,48},{96,80},{17,33},{49,65},{8... | collective-permute-start | bytes 61448 | tf_op jit(solution)/shard_map/ppermute | solution.py:26
  51.9 12.7 %copy-start.16 = (f32[40,128]{1,0:T(8,128)}, f32[40,128]{1,0:T(8,128)S(1)}, u32[]{:S(2)}) copy-start(f32[40,128]{1,0:T(8,128)S(1)} %collective-permute-done.10.edge_even) | copy-start | bytes 61444
  55.3 9.3 %copy-start.17 = (f32[40,128]{1,0:T(8,128)}, f32[40,128]{1,0:T(8,128)S(1)}, u32[]{:S(2)}) copy-start(f32[40,128]{1,0:T(8,128)S(1)} %collective-permute-done.11.edge_odd) | copy-start | bytes 61444
  56.0 6.3 %collective-permute-start.13 = (f32[96,128]{1,0:T(8,128)S(1)}, f32[96,128]{1,0:T(8,128)S(1)}, u32[]{:S(2)}, u32[]{:S(2)}) collective-permute-start(f32[96,128]{1,0:T(8,128)S(1)} %pad_maximum_fusion.1), channel_id=1, source_target_pairs={{1,2},{3,4},{5,6},{7,8},{9,10},{11,12},{13,14},{15,0},{2,1},{4,3},... | collective-permute-start | bytes 147464 | tf_op jit(solution)/shard_map/ppermute | solution.py:26
  59.2 3.8 %collective-permute-start.12 = (f32[96,128]{1,0:T(8,128)S(1)}, f32[96,128]{1,0:T(8,128)S(1)}, u32[]{:S(2)}, u32[]{:S(2)}) collective-permute-start(f32[96,128]{1,0:T(8,128)S(1)} %pad_maximum_fusion.1), channel_id=1, source_target_pairs={{0,1},{2,3},{4,5},{6,7},{8,9},{10,11},{12,13},{14,15},{1,0},{3,2},... | collective-permute-start | bytes 147464 | tf_op jit(solution)/shard_map/ppermute | solution.py:26
  59.2 24.7 %collective-permute-start.6 = (bf16[48,64,128]{2,1,0:T(8,128)(2,1)}, bf16[48,64,128]{2,1,0:T(8,128)(2,1)S(1)}, u32[]{:S(2)}, u32[]{:S(2)}) collective-permute-start(bf16[48,64,128]{2,1,0:T(8,128)(2,1)} %copy-done.11), channel_id=1, source_target_pairs={{0,1},{2,3},{4,5},{6,7},{8,9},{10,11},{12,13},{14,15},{1,0},{3,2},... | collective-permute-start | bytes 2359304 | tf_op jit(solution)/shard_map/ppermute | solution.py:26
  60.7 29.0 %collective-permute-start.7 = (bf16[48,64,128]{2,1,0:T(8,128)(2,1)}, bf16[48,64,128]{2,1,0:T(8,128)(2,1)}, u32[]{:S(2)}, u32[]{:S(2)}) collective-permute-start(bf16[48,64,128]{2,1,0:T(8,128)(2,1)} %copy-done.10), channel_id=1, source_target_pairs={{1,2},{3,4},{5,6},{7,8},{9,10},{11,12},{13,14},{15,0},{2,1},{4,3},... | collective-permute-start | bytes 2359304 | tf_op jit(solution)/shard_map/ppermute | solution.py:26
  62.3 2.3 %copy-start.14 = (f32[96,128]{1,0:T(8,128)}, f32[96,128]{1,0:T(8,128)S(1)}, u32[]{:S(2)}) copy-start(f32[96,128]{1,0:T(8,128)S(1)} %collective-permute-done.13.cols_odd) | copy-start | bytes 147460
  63.0 1.6 %copy-start.15 = (f32[96,128]{1,0:T(8,128)}, f32[96,128]{1,0:T(8,128)S(1)}, u32[]{:S(2)}) copy-start(f32[96,128]{1,0:T(8,128)S(1)} %collective-permute-done.12.cols_even) | copy-start | bytes 147460
  63.0 26.6 %collective-permute-start.14 = (bf16[48,64,128]{2,1,0:T(8,128)(2,1)}, bf16[48,64,128]{2,1,0:T(8,128)(2,1)}, u32[]{:S(2)}, u32[]{:S(2)}) collective-permute-start(bf16[48,64,128]{2,1,0:T(8,128)(2,1)} %copy-done.9), channel_id=1, source_target_pairs={{0,8},{1,9},{2,10},{3,11},{4,12},{5,13},{6,14},{7,15},{8,0},{9,1},... | collective-permute-start | bytes 2359304 | tf_op jit(solution)/shard_map/ppermute | solution.py:40
  79.8 15.0 %all-to-all-start.1 = ((f32[16,8,128]{2,1,0:T(8,128)}), f32[16,8,128]{2,1,0:T(8,128)}, u32[]{:S(2)}, u32[]{:S(2)}) async-start(f32[16,8,128]{2,1,0:T(8,128)} %broadcast_in_dim.32), calls=%async_computation.1 | async-start | bytes 131072 | tf_op jit(solution)/shard_map/all_to_all | solution.py:443
  (2 other events, 1.6 us)

commit v3 on v2

--- a/solution.py
+++ b/solution.py
@@ -57,7 +57,7 @@
 def coded(depart_lists, tiles):
     bands, sectors = lax.axis_size("lat"), lax.axis_size("lon")
     band, sector = lax.axis_index("lat"), lax.axis_index("lon")
-    wanted = depart_lists.reshape(1, -1)
+    wanted = depart_lists.transpose(1, 2, 0).reshape(1, -1)
     owner = wanted // tiles
     theirs = owner % sectors
     turn = jnp.where(theirs == (sector ^ 1), 1, 2)
@@ -149,7 +149,7 @@
         across = ((tile & 15) + jnp.where(tile < 16, 80, 96)).astype(F32)
     place = jnp.where(turn == 3, across, place)
     row = iota((LANES, LANES), 0)
-    mine = iota((LANES, LANES), 1) == 2 * (row & 15) + (row >> 6)
+    mine = iota((LANES, LANES), 1) == (row & 15) + 16 * (row >> 6)
     place = jnp.sum(jnp.where(mine, place, 0.0), axis=1, keepdims=True)
     within = ((iota(gather.shape, 0) >> 4) & 3).astype(F32)
     col = iota(gather.shape, 1).astype(F32)
@@ -222,7 +222,7 @@
             rhs[l, every_fourth(q), :] = values[q][1] + 0.5 * values[q][0]
         return carry
 
-    lax.fori_loop(0, 16, level, 0, unroll=8)
+    lax.fori_loop(0, 16, level, 0, unroll=16)
     group = iota((64, LANES), 1) >> 2
     packed = jnp.where(group == 16, pltpu.roll(diag[...], 65, 1), 0.0)
     for l in range(16):
@@ -259,7 +259,7 @@
             jax.ShapeDtypeStruct((64, 64, LANES), BF16), slab, jax.ShapeDtypeStruct((64, LANES), F32)
         ] + [edge] * 4,
         scratch_shapes=scratch(7),
-        compiler_params=pltpu.CompilerParams(vmem_limit_bytes=60 << 20),
+        compiler_params=pltpu.CompilerParams(vmem_limit_bytes=32 << 20),
         cost_estimate=pl.CostEstimate(flops=32 * 2 * 128 * 448 * 128, bytes_accessed=6 << 20, transcendentals=0),
         name="first_levels",
     )(scale, codes, offsets, weights, diag, *pools)
@@ -374,9 +374,7 @@
                 part = part + term[8 * j : 8 * j + 8]
             rowsums[k * 16 + l : k * 16 + l + 1, :] = jnp.sum(part, axis=0, keepdims=True)
     total = jnp.sum(rowsums[...], axis=1, keepdims=True)
-    packed = jnp.zeros((8, LANES), F32)
-    for j in range(8):
-        packed = jnp.where(lane[:8] == j, total[8 * j : 8 * j + 8], packed)
+    packed = jnp.sum(jnp.where(lane == iota((64, LANES), 0), total, 0.0), axis=0, keepdims=True)
     for j in range(sums.shape[0]):
         sums[j] = packed
 
@@ -387,7 +385,7 @@
         sum_kernel,
         in_specs=[SMEM] + [VMEM] * 9,
         out_specs=[VMEM] * 3,
-        out_shape=[slab, slab, jax.ShapeDtypeStruct((lax.axis_size("lat"), 8, LANES), F32)],
+        out_shape=[slab, slab, jax.ShapeDtypeStruct((lax.axis_size("lat"), 1, LANES), F32)],
         scratch_shapes=[pltpu.VMEM((64, LANES), F32)],
         compiler_params=pltpu.CompilerParams(vmem_limit_bytes=60 << 20),
         cost_estimate=pl.CostEstimate(flops=1 << 22, bytes_accessed=2 << 20, transcendentals=0),
@@ -399,10 +397,11 @@
     total = parts[0]
     for j in range(1, parts.shape[0]):
         total = total + parts[j]
-    lane = iota((8, LANES), 1)
+    total = jnp.broadcast_to(total, (8, LANES))
+    lane, row = iota((8, LANES), 1), iota((8, LANES), 0)
 
     def of(k, half):
-        return jnp.sum(jnp.where(lane == 2 * k + half, total, 0.0), axis=1, keepdims=True)
+        return jnp.sum(jnp.where(lane == 16 * k + 8 * half + row, total, 0.0), axis=1, keepdims=True)
 
     for half in range(2):
         s0, s1, s2, s3 = (of(k, half) for k in range(4))
@@ -433,6 +432,7 @@
         in_specs=[SMEM] + [VMEM] * 5,
         out_specs=[VMEM] * 2,
         out_shape=[slab, slab],
+        input_output_aliases={2: 1, 4: 0},
         compiler_params=pltpu.CompilerParams(vmem_limit_bytes=60 << 20),
         cost_estimate=pl.CostEstimate(flops=1 << 21, bytes_accessed=3 << 20, transcendentals=0),
         name="last_step",

time: 98.3 us -> 96 us (0.977)
  waiting for transfers between devices: 22.9 us -> 24.9 us
  other arithmetic: 1.65 us -> 0.14 us
  local copies, waits for them, and re-layouts: 4.97 us -> 3.84 us
    ppermute x12, waiting for transfers between devices: 22.9 us -> 24.9 us  [swap(): return lax.ppermute(block, axis, ends + [(b, a) for a, b in ends])]
    unnamed x37 -> x28, local copies, waits for them, and re-layouts: 3.17 us -> 1.4 us
    pallas_call x1, Pallas kernels: 4.58 us -> 3.19 us  [first_levels(): pl.pallas_call(first_kernel, grid=(1,), in_specs=[SMEM, flat(1), flat(64)...]
  transfers between devices with their start and end apart: 16 -> 16, of which waited for: 7 -> 7; matrix products, arithmetic and copies ran while one was open for 4% -> 3% of each run, Pallas kernels for 14% -> 15%
where the time goes in v3:
time: 96 us; the launch traced here: 95.4 us
  starting transfers between devices  36.3 us (38%)
  waiting for transfers between devices  24.9 us (26%)
  Pallas kernels  20.5 us (21%)
  blocking collectives  8.97 us (9%)
  local copies, waits for them, and re-layouts  3.84 us (4%)
    ppermute x12, starting transfers between devices, swap(): return lax.ppermute(block, axis, ends + [(b, a) for a, b in ends])  26.1 us
    ppermute x12, waiting for transfers between devices, swap(): return lax.ppermute(block, axis, ends + [(b, a) for a, b in ends])  24.9 us
    all_to_all x1, blocking collectives, exchange(): return lax.all_to_all(parts, axis, split_axis=0, concat_axis=0, tiled=True)  8.97 us
    ppermute x3, starting transfers between devices, from_pole(): return lax.ppermute(block, ('lat', 'lon'), pairs)  6.5 us
    pallas_call x2, Pallas kernels, pack(): pl.pallas_call(functools.partial(pack_kernel, count), grid=(blocks,), in_...  5.8 us
    pallas_call x1, Pallas kernels, level_sums(): pl.pallas_call(sum_kernel, in_specs=[SMEM] + [VMEM] * 9, out_specs=[VMEM]...  4.44 us
    pallas_call x1, Pallas kernels, other_levels(): pl.pallas_call(other_kernel, grid=(3,), in_specs=[flat(1), flat(64), WEIG...  4.34 us
    all_to_all x1, starting transfers between devices, exchange(): return lax.all_to_all(parts, axis, split_axis=0, concat_axis=0, tiled=True)  3.71 us
  transfers between devices with their start and end apart: 16, of which 7 were waited for; matrix products, arithmetic and copies ran while one was open for 3% of the time, Pallas kernels for 15%

profile of v3, /device:TPU:1, one launch (start us, length us, event | category | flops | bytes accessed | tf_op | source)
XLA Modules:
  0.0 95.4 jit_solution(4075400382852506589)
XLA Ops:
  0.6 4.7 %collective-permute-start.1 = (bf16[80,64,128]{2,1,0:T(8,128)(2,1)}, bf16[80,64,128]{2,1,0:T(8,128)(2,1)S(1)}, u32[]{:S(2)}, u32[]{:S(2)}) collective-permute-start(bf16[80,64,128]{2,1,0:T(8,128)(2,1)} %refs_0_.3), channel_id=1, source_target_pairs={{16,32},{48,64},{80,96},{32,16},{64,48},{96,80},{17,33},{49,65},{8... | collective-permute-start | bytes 3932168 | tf_op jit(solution)/shard_map/ppermute | solution.py:26
  5.5 0.8 reshape.295
  6.3 6.0 %collective-permute-start.3 = (s32[1,128]{1,0:T(1,128)S(1)}, s32[1,128]{1,0:T(1,128)S(1)}, u32[]{:S(2)}, u32[]{:S(2)}) collective-permute-start(s32[1,128]{1,0:T(1,128)S(1)} %get-tuple-element.50.codes), channel_id=1, source_target_pairs={{1,2},{3,4},{5,6},{7,8},{9,10},{11,12},{13,14},{15,0},{2,1},{4,3},... | collective-permute-start | bytes 1544 | tf_op jit(solution)/shard_map/ppermute | solution.py:26
  12.3 1.1 %fusion.4 = (bf16[16,64,128]{2,1,0:T(8,128)(2,1)S(1)}, bf16[16,64,128]{2,1,0:T(8,128)(2,1)S(1)}) fusion(bf16[80,64,128]{2,1,0:T(8,128)(2,1)} %refs_0_.3), kind=kLoop, calls=%fused_computation.22 | loop fusion | bytes 1048576 | tf_op jit(solution)/shard_map/slice | solution.py:452
  13.5 1.2 %collective-permute-done.2.refs_0_ = s32[1,128]{1,0:T(1,128)S(1)} collective-permute-done((s32[1,128]{1,0:T(1,128)S(1)}, s32[1,128]{1,0:T(1,128)S(1)}, u32[]{:S(2)}, u32[]{:S(2)}) %collective-permute-start.2) | collective-permute-done | bytes 544 | tf_op jit(solution)/shard_map/ppermute | solution.py:26
  14.7 4.2 %collective-permute-start.5 = (bf16[33,64,128]{2,1,0:T(8,128)(2,1)S(1)}, bf16[33,64,128]{2,1,0:T(8,128)(2,1)S(1)}, u32[]{:S(2)}, u32[]{:S(2)}) collective-permute-start(bf16[33,64,128]{2,1,0:T(8,128)(2,1)S(1)} %pad_maximum_fusion), channel_id=1, source_target_pairs={{16,8},{17,9},{18,10},{19,11},{20,12},{21,13},{22,14},{23,15},{24,... | collective-permute-start | bytes 1622024 | tf_op jit(solution)/shard_map/ppermute | solution.py:40
  19.0 0.7 collective-permute-start.4
  19.7 1.2 %collective-permute-done.1.refs_4_.refs_5_.refs_2_.refs_9_ = bf16[80,64,128]{2,1,0:T(8,128)(2,1)S(1)} collective-permute-done((bf16[80,64,128]{2,1,0:T(8,128)(2,1)}, bf16[80,64,128]{2,1,0:T(8,128)(2,1)S(1)}, u32[]{:S(2)}, u32[]{:S(2)}) %collective-permute-start.1) | collective-permute-done | bytes 1310752 | tf_op jit(solution)/shard_map/ppermute | solution.py:26
  20.9 1.8 %pack.2 = (bf16[32,64,128]{2,1,0:T(8,128)(2,1)S(1)}, bf16[32,64,128]{2,1,0:T(8,128)(2,1)S(1)}) custom-call(s32[1,128]{1,0:T(1,128)S(1)} %collective-permute-done.2.refs_0_, s32[1,128]{1,0:T(1,128)S(1)} %collective-permute-done.3.refs_1_, bf16[80,64,128]{2,1,0:T(8,128)(2,1)S(1)} %copy-done, ...), custom_call_target="tpu_custom_call" | custom-call | flops 301989888 | bytes 2621440 | tf_op jit(solution)/shard_map/pack/pallas_call | solution.py:122
  22.7 2.0 %collective-permute-start.8 = (bf16[32,64,128]{2,1,0:T(8,128)(2,1)S(1)}, bf16[32,64,128]{2,1,0:T(8,128)(2,1)S(1)}, u32[]{:S(2)}, u32[]{:S(2)}) collective-permute-start(bf16[32,64,128]{2,1,0:T(8,128)(2,1)S(1)} %get-tuple-element.25), channel_id=1, source_target_pairs={{0,1},{2,3},{4,5},{6,7},{8,9},{10,11},{12,13},{14,15},{1,0},{3,2},... | collective-permute-start | bytes 1572872 | tf_op jit(solution)/shard_map/ppermute | solution.py:26
  24.7 4.5 %collective-permute-start.9 = (bf16[32,64,128]{2,1,0:T(8,128)(2,1)S(1)}, bf16[32,64,128]{2,1,0:T(8,128)(2,1)S(1)}, u32[]{:S(2)}, u32[]{:S(2)}) collective-permute-start(bf16[32,64,128]{2,1,0:T(8,128)(2,1)S(1)} %get-tuple-element.26), channel_id=1, source_target_pairs={{1,2},{3,4},{5,6},{7,8},{9,10},{11,12},{13,14},{15,0},{2,1},{4,3},... | collective-permute-start | bytes 1572872 | tf_op jit(solution)/shard_map/ppermute | solution.py:26
  29.2 4.0 %pack.3 = (bf16[48,64,128]{2,1,0:T(8,128)(2,1)}, bf16[48,64,128]{2,1,0:T(8,128)(2,1)}, bf16[48,64,128]{2,1,0:T(8,128)(2,1)}) custom-call(s32[1,128]{1,0:T(1,128)S(1)} %collective-permute-done.2.refs_0_, s32[1,128]{1,0:T(1,128)S(1)} %collective-permute-done.3.refs_1_, bf16[33,64,128]{2,1,0:T(8,128)(2,1)S(1)} %collective-permute-done.4.refs_2_.refs_5_.refs_12_, ...), custom_call_target="tpu_custom_call" | custom-call | flops 452984832 | bytes 3932160 | tf_op jit(solution)/shard_map/pack/pallas_call | solution.py:122
  33.2 3.7 %collective-permute-done.8.refs_3_.refs_10_ = bf16[32,64,128]{2,1,0:T(8,128)(2,1)S(1)} collective-permute-done((bf16[32,64,128]{2,1,0:T(8,128)(2,1)S(1)}, bf16[32,64,128]{2,1,0:T(8,128)(2,1)S(1)}, u32[]{:S(2)}, u32[]{:S(2)}) %collective-permute-start.8) | collective-permute-done | bytes 524320 | tf_op jit(solution)/shard_map/ppermute | solution.py:26
  37.0 7.7 %collective-permute-done.9.refs_4_.refs_11_ = bf16[32,64,128]{2,1,0:T(8,128)(2,1)S(1)} collective-permute-done((bf16[32,64,128]{2,1,0:T(8,128)(2,1)S(1)}, bf16[32,64,128]{2,1,0:T(8,128)(2,1)S(1)}, u32[]{:S(2)}, u32[]{:S(2)}) %collective-permute-start.9) | collective-permute-done | bytes 524320 | tf_op jit(solution)/shard_map/ppermute | solution.py:26
  44.7 3.2 %first_levels.1 = (bf16[64,64,128]{2,1,0:T(8,128)(2,1)}, f32[16,64,128]{2,1,0:T(8,128)}, f32[64,128]{1,0:T(8,128)S(1)}, f32[40,128]{1,0:T(8,128)S(1)}, f32[40,12...) custom-call(f32[16]{0:T(128)S(1)} %copy-done.8, s32[1,128]{1,0:T(1,128)S(1)} %get-tuple-element.50.codes, ...), custom_call_target="tpu_custom_call" | custom-call | flops 469762048 | bytes 6291456 | tf_op jit(solution)/shard_map/first_levels/pallas_call | solution.py:253
  47.9 0.5 collective-permute-start.10
  48.4 1.9 %collective-permute-start.11 = (f32[40,128]{1,0:T(8,128)S(1)}, f32[40,128]{1,0:T(8,128)S(1)}, u32[]{:S(2)}, u32[]{:S(2)}) collective-permute-start(f32[40,128]{1,0:T(8,128)S(1)} %get-tuple-element.35), channel_id=1, source_target_pairs={{16,32},{48,64},{80,96},{32,16},{64,48},{96,80},{17,33},{49,65},{8... | collective-permute-start | bytes 61448 | tf_op jit(solution)/shard_map/ppermute | solution.py:26
  50.3 3.1 %collective-permute-done.11.edge_odd = f32[40,128]{1,0:T(8,128)S(1)} collective-permute-done((f32[40,128]{1,0:T(8,128)S(1)}, f32[40,128]{1,0:T(8,128)S(1)}, u32[]{:S(2)}, u32[]{:S(2)}) %collective-permute-start.11) | collective-permute-done | bytes 20512 | tf_op jit(solution)/shard_map/ppermute | solution.py:26
  53.5 3.3 %collective-permute-start.13 = (f32[96,128]{1,0:T(8,128)S(1)}, f32[96,128]{1,0:T(8,128)S(1)}, u32[]{:S(2)}, u32[]{:S(2)}) collective-permute-start(f32[96,128]{1,0:T(8,128)S(1)} %pad_maximum_fusion.1), channel_id=1, source_target_pairs={{1,2},{3,4},{5,6},{7,8},{9,10},{11,12},{13,14},{15,0},{2,1},{4,3},... | collective-permute-start | bytes 147464 | tf_op jit(solution)/shard_map/ppermute | solution.py:26
  56.8 1.5 %collective-permute-start.6 = (bf16[48,64,128]{2,1,0:T(8,128)(2,1)}, bf16[48,64,128]{2,1,0:T(8,128)(2,1)S(1)}, u32[]{:S(2)}, u32[]{:S(2)}) collective-permute-start(bf16[48,64,128]{2,1,0:T(8,128)(2,1)} %get-tuple-element.29), channel_id=1, source_target_pairs={{0,1},{2,3},{4,5},{6,7},{8,9},{10,11},{12,13},{14,15},{1,0},{3,2},... | collective-permute-start | bytes 2359304 | tf_op jit(solution)/shard_map/ppermute | solution.py:26
  58.2 1.6 %collective-permute-start.7 = (bf16[48,64,128]{2,1,0:T(8,128)(2,1)}, bf16[48,64,128]{2,1,0:T(8,128)(2,1)}, u32[]{:S(2)}, u32[]{:S(2)}) collective-permute-start(bf16[48,64,128]{2,1,0:T(8,128)(2,1)} %get-tuple-element.30), channel_id=1, source_target_pairs={{1,2},{3,4},{5,6},{7,8},{9,10},{11,12},{13,14},{15,0},{2,1},{4,3},... | collective-permute-start | bytes 2359304 | tf_op jit(solution)/shard_map/ppermute | solution.py:26
  59.8 0.8 collective-permute-done.12.cols_even
  60.6 1.6 %collective-permute-start.14 = (bf16[48,64,128]{2,1,0:T(8,128)(2,1)}, bf16[48,64,128]{2,1,0:T(8,128)(2,1)}, u32[]{:S(2)}, u32[]{:S(2)}) collective-permute-start(bf16[48,64,128]{2,1,0:T(8,128)(2,1)} %get-tuple-element.36), channel_id=1, source_target_pairs={{0,8},{1,9},{2,10},{3,11},{4,12},{5,13},{6,14},{7,15},{8,0},{9,1},... | collective-permute-start | bytes 2359304 | tf_op jit(solution)/shard_map/ppermute | solution.py:40
  62.2 4.4 %level_sums.1 = (f32[16,64,128]{2,1,0:T(8,128)}, f32[16,64,128]{2,1,0:T(8,128)}, f32[8,1,128]{2,1,0:T(1,128)}) custom-call(f32[16]{0:T(128)} %scale.5, f32[16,64,128]{2,1,0:T(8,128)} %get-tuple-element.38.rhs, f32[64,128]{1,0:T(8,128)} %diag.5, f32[64,128]{1,0:T(8,128)} %copy-done.5, f32[40,128]{1,0:T(8,128)} %copy-done.6, f32[40,128]{1,0:T(8,128)} %copy-done.7, ...), custom_call_target="tpu_custom_call" | custom-call | flops 4194304 | bytes 2097152 | tf_op jit(solution)/shard_map/level_sums/pallas_call | solution.py:384
  66.6 9.0 %all_to_all.10 = f32[8,1,128]{2,1,0:T(1,128)S(1)} all-to-all(f32[8,1,128]{2,1,0:T(1,128)} %get-tuple-element.41), channel_id=1, replica_groups=mesh['lat'=8,'lon'=16] {'lat'}, dimensions={0} | all-to-all | bytes 8192 | tf_op jit(solution)/shard_map/all_to_all | solution.py:443
  75.6 0.6 broadcast_in_dim.32
  76.2 3.7 %all-to-all-start.1 = ((f32[16,1,128]{2,1,0:T(1,128)}), f32[16,1,128]{2,1,0:T(1,128)S(1)}, u32[]{:S(2)}, u32[]{:S(2)}) async-start(f32[16,1,128]{2,1,0:T(1,128)} %broadcast_in_dim.32), calls=%async_computation.1 | async-start | bytes 16384 | tf_op jit(solution)/shard_map/all_to_all | solution.py:443
  79.9 7.1 %collective-permute-done.7.refs_4_ = bf16[48,64,128]{2,1,0:T(8,128)(2,1)} collective-permute-done((bf16[48,64,128]{2,1,0:T(8,128)(2,1)}, bf16[48,64,128]{2,1,0:T(8,128)(2,1)}, u32[]{:S(2)}, u32[]{:S(2)}) %collective-permute-start.7) | collective-permute-done | bytes 786464 | tf_op jit(solution)/shard_map/ppermute | solution.py:26
  87.0 0.8 copy-done.4
  87.8 4.3 %other_levels.1 = bf16[64,64,128]{2,1,0:T(8,128)(2,1)} custom-call(s32[1,128]{1,0:T(1,128)S(1)} %get-tuple-element.50.codes, s32[64,128]{1,0:T(8,128)S(1)} %copy-done.4, f32[4,64,128]{2,1,0:T(8,128)S(1)} %copy-done.1, bf16[80,64,128]{2,1,0:T(8,128)(2,1)S(1)} %copy-done, ...), custom_call_target="tpu_custom_call", output_to_operand_aliasing={{}: (9, {})} | custom-call | flops 704643072 | bytes 6291456 | tf_op jit(solution)/shard_map/other_levels/pallas_call | solution.py:289
  92.1 0.6 copy-done.13
  92.7 2.7 %last_step.1 = (f32[16,64,128]{2,1,0:T(8,128)}, f32[16,64,128]{2,1,0:T(8,128)}) custom-call(f32[16]{0:T(128)} %scale.5, f32[16,1,128]{2,1,0:T(1,128)} %copy-done.13, f32[16,64,128]{2,1,0:T(8,128)} %get-tuple-element.38.rhs, f32[64,128]{1,0:T(8,128)} %diag.5, f32[16,64,128]{2,1,0:T(8,128)} %get-tuple-element.43.n0, ...), custom_call_target="tpu_custom_call", output_to_operand_aliasing={{1}: (2, {}), {0}: (4, {})} | custom-call | flops 2097152 | bytes 3145728 | tf_op jit(solution)/shard_map/last_step/pallas_call | solution.py:430
  (46 shorter events, 0.3 us)
Async XLA Ops:
  0.6 20.2 %copy-start = (bf16[80,64,128]{2,1,0:T(8,128)(2,1)S(1)}, bf16[80,64,128]{2,1,0:T(8,128)(2,1)}, u32[]{:S(2)}) copy-start(bf16[80,64,128]{2,1,0:T(8,128)(2,1)} %refs_0_.3) | copy-start | bytes 3932164
  0.6 20.2 %collective-permute-start.1 = (bf16[80,64,128]{2,1,0:T(8,128)(2,1)}, bf16[80,64,128]{2,1,0:T(8,128)(2,1)S(1)}, u32[]{:S(2)}, u32[]{:S(2)}) collective-permute-start(bf16[80,64,128]{2,1,0:T(8,128)(2,1)} %refs_0_.3), channel_id=1, source_target_pairs={{16,32},{48,64},{80,96},{32,16},{64,48},{96,80},{17,33},{49,65},{8... | collective-permute-start | bytes 3932168 | tf_op jit(solution)/shard_map/ppermute | solution.py:26
  5.4 15.5 %collective-permute-start = (bf16[80,64,128]{2,1,0:T(8,128)(2,1)}, bf16[80,64,128]{2,1,0:T(8,128)(2,1)}, u32[]{:S(2)}, u32[]{:S(2)}) collective-permute-start(bf16[80,64,128]{2,1,0:T(8,128)(2,1)} %refs_0_.3), channel_id=1, source_target_pairs={{0,16},{32,48},{64,80},{96,112},{16,0},{48,32},{80,64},{112,96},{1... | collective-permute-start | bytes 3932168 | tf_op jit(solution)/shard_map/ppermute | solution.py:26
  6.3 7.2 %collective-permute-start.3 = (s32[1,128]{1,0:T(1,128)S(1)}, s32[1,128]{1,0:T(1,128)S(1)}, u32[]{:S(2)}, u32[]{:S(2)}) collective-permute-start(s32[1,128]{1,0:T(1,128)S(1)} %get-tuple-element.50.codes), channel_id=1, source_target_pairs={{1,2},{3,4},{5,6},{7,8},{9,10},{11,12},{13,14},{15,0},{2,1},{4,3},... | collective-permute-start | bytes 1544 | tf_op jit(solution)/shard_map/ppermute | solution.py:26
  12.3 2.4 %collective-permute-start.2 = (s32[1,128]{1,0:T(1,128)S(1)}, s32[1,128]{1,0:T(1,128)S(1)}, u32[]{:S(2)}, u32[]{:S(2)}) collective-permute-start(s32[1,128]{1,0:T(1,128)S(1)} %get-tuple-element.50.codes), channel_id=1, source_target_pairs={{0,1},{2,3},{4,5},{6,7},{8,9},{10,11},{12,13},{14,15},{1,0},{3,2},... | collective-permute-start | bytes 1544 | tf_op jit(solution)/shard_map/ppermute | solution.py:26
  14.7 14.5 %collective-permute-start.5 = (bf16[33,64,128]{2,1,0:T(8,128)(2,1)S(1)}, bf16[33,64,128]{2,1,0:T(8,128)(2,1)S(1)}, u32[]{:S(2)}, u32[]{:S(2)}) collective-permute-start(bf16[33,64,128]{2,1,0:T(8,128)(2,1)S(1)} %pad_maximum_fusion), channel_id=1, source_target_pairs={{16,8},{17,9},{18,10},{19,11},{20,12},{21,13},{22,14},{23,15},{24,... | collective-permute-start | bytes 1622024 | tf_op jit(solution)/shard_map/ppermute | solution.py:40
  19.0 10.3 %collective-permute-start.4 = (bf16[33,64,128]{2,1,0:T(8,128)(2,1)S(1)}, bf16[33,64,128]{2,1,0:T(8,128)(2,1)S(1)}, u32[]{:S(2)}, u32[]{:S(2)}) collective-permute-start(bf16[33,64,128]{2,1,0:T(8,128)(2,1)S(1)} %pad_maximum_fusion), channel_id=1, source_target_pairs={{0,8},{1,9},{2,10},{3,11},{4,12},{5,13},{6,14},{7,15},{8,0},{9,1},... | collective-permute-start | bytes 1622024 | tf_op jit(solution)/shard_map/ppermute | solution.py:40
  22.7 14.3 %collective-permute-start.8 = (bf16[32,64,128]{2,1,0:T(8,128)(2,1)S(1)}, bf16[32,64,128]{2,1,0:T(8,128)(2,1)S(1)}, u32[]{:S(2)}, u32[]{:S(2)}) collective-permute-start(bf16[32,64,128]{2,1,0:T(8,128)(2,1)S(1)} %get-tuple-element.25), channel_id=1, source_target_pairs={{0,1},{2,3},{4,5},{6,7},{8,9},{10,11},{12,13},{14,15},{1,0},{3,2},... | collective-permute-start | bytes 1572872 | tf_op jit(solution)/shard_map/ppermute | solution.py:26
  24.7 20.0 %copy-start.1 = (f32[4,64,128]{2,1,0:T(8,128)S(1)}, f32[4,64,128]{2,1,0:T(8,128)}, u32[]{:S(2)}) copy-start(f32[4,64,128]{2,1,0:T(8,128)} %weights.3) | copy-start | bytes 393220
  24.7 20.0 %copy-start.2 = (f32[64,128]{1,0:T(8,128)S(1)}, f32[64,128]{1,0:T(8,128)}, u32[]{:S(2)}) copy-start(f32[64,128]{1,0:T(8,128)} %diag.5) | copy-start | bytes 98308
  24.7 20.0 %copy-start.3 = (s32[64,128]{1,0:T(8,128)S(1)}, s32[64,128]{1,0:T(8,128)}, u32[]{:S(2)}) copy-start(s32[64,128]{1,0:T(8,128)} %offsets.3) | copy-start | bytes 98308
  24.7 20.0 %copy-start.8 = (f32[16]{0:T(128)S(1)}, f32[16]{0:T(128)}, u32[]{:S(2)}) copy-start(f32[16]{0:T(128)} %scale.5) | copy-start | bytes 196
  24.7 20.0 %collective-permute-start.9 = (bf16[32,64,128]{2,1,0:T(8,128)(2,1)S(1)}, bf16[32,64,128]{2,1,0:T(8,128)(2,1)S(1)}, u32[]{:S(2)}, u32[]{:S(2)}) collective-permute-start(bf16[32,64,128]{2,1,0:T(8,128)(2,1)S(1)} %get-tuple-element.26), channel_id=1, source_target_pairs={{1,2},{3,4},{5,6},{7,8},{9,10},{11,12},{13,14},{15,0},{2,1},{4,3},... | collective-permute-start | bytes 1572872 | tf_op jit(solution)/shard_map/ppermute | solution.py:26
  47.9 8.9 %copy-start.6 = (f32[40,128]{1,0:T(8,128)}, f32[40,128]{1,0:T(8,128)S(1)}, u32[]{:S(2)}) copy-start(f32[40,128]{1,0:T(8,128)S(1)} %get-tuple-element.39.own_up) | copy-start | bytes 61444
  47.9 8.9 %copy-start.7 = (f32[40,128]{1,0:T(8,128)}, f32[40,128]{1,0:T(8,128)S(1)}, u32[]{:S(2)}) copy-start(f32[40,128]{1,0:T(8,128)S(1)} %get-tuple-element.40.own_down) | copy-start | bytes 61444
  47.9 14.3 %copy-start.5 = (f32[64,128]{1,0:T(8,128)}, f32[64,128]{1,0:T(8,128)S(1)}, u32[]{:S(2)}) copy-start(f32[64,128]{1,0:T(8,128)S(1)} %get-tuple-element.33.cols) | copy-start | bytes 98308
  47.9 2.4 %collective-permute-start.10 = (f32[40,128]{1,0:T(8,128)S(1)}, f32[40,128]{1,0:T(8,128)S(1)}, u32[]{:S(2)}, u32[]{:S(2)}) collective-permute-start(f32[40,128]{1,0:T(8,128)S(1)} %get-tuple-element.34), channel_id=1, source_target_pairs={{0,16},{32,48},{64,80},{96,112},{16,0},{48,32},{80,64},{112,96},{1... | collective-permute-start | bytes 61448 | tf_op jit(solution)/shard_map/ppermute | solution.py:26
  48.4 5.1 %collective-permute-start.11 = (f32[40,128]{1,0:T(8,128)S(1)}, f32[40,128]{1,0:T(8,128)S(1)}, u32[]{:S(2)}, u32[]{:S(2)}) collective-permute-start(f32[40,128]{1,0:T(8,128)S(1)} %get-tuple-element.35), channel_id=1, source_target_pairs={{16,32},{48,64},{80,96},{32,16},{64,48},{96,80},{17,33},{49,65},{8... | collective-permute-start | bytes 61448 | tf_op jit(solution)/shard_map/ppermute | solution.py:26
  50.3 11.9 %copy-start.11 = (f32[40,128]{1,0:T(8,128)}, f32[40,128]{1,0:T(8,128)S(1)}, u32[]{:S(2)}) copy-start(f32[40,128]{1,0:T(8,128)S(1)} %collective-permute-done.10.edge_even) | copy-start | bytes 61444
  53.5 8.7 %copy-start.12 = (f32[40,128]{1,0:T(8,128)}, f32[40,128]{1,0:T(8,128)S(1)}, u32[]{:S(2)}) copy-start(f32[40,128]{1,0:T(8,128)S(1)} %collective-permute-done.11.edge_odd) | copy-start | bytes 61444
  53.5 6.3 %collective-permute-start.13 = (f32[96,128]{1,0:T(8,128)S(1)}, f32[96,128]{1,0:T(8,128)S(1)}, u32[]{:S(2)}, u32[]{:S(2)}) collective-permute-start(f32[96,128]{1,0:T(8,128)S(1)} %pad_maximum_fusion.1), channel_id=1, source_target_pairs={{1,2},{3,4},{5,6},{7,8},{9,10},{11,12},{13,14},{15,0},{2,1},{4,3},... | collective-permute-start | bytes 147464 | tf_op jit(solution)/shard_map/ppermute | solution.py:26
  56.8 3.8 %collective-permute-start.12 = (f32[96,128]{1,0:T(8,128)S(1)}, f32[96,128]{1,0:T(8,128)S(1)}, u32[]{:S(2)}, u32[]{:S(2)}) collective-permute-start(f32[96,128]{1,0:T(8,128)S(1)} %pad_maximum_fusion.1), channel_id=1, source_target_pairs={{0,1},{2,3},{4,5},{6,7},{8,9},{10,11},{12,13},{14,15},{1,0},{3,2},... | collective-permute-start | bytes 147464 | tf_op jit(solution)/shard_map/ppermute | solution.py:26
  56.8 23.2 %collective-permute-start.6 = (bf16[48,64,128]{2,1,0:T(8,128)(2,1)}, bf16[48,64,128]{2,1,0:T(8,128)(2,1)S(1)}, u32[]{:S(2)}, u32[]{:S(2)}) collective-permute-start(bf16[48,64,128]{2,1,0:T(8,128)(2,1)} %get-tuple-element.29), channel_id=1, source_target_pairs={{0,1},{2,3},{4,5},{6,7},{8,9},{10,11},{12,13},{14,15},{1,0},{3,2},... | collective-permute-start | bytes 2359304 | tf_op jit(solution)/shard_map/ppermute | solution.py:26
  58.2 28.8 %collective-permute-start.7 = (bf16[48,64,128]{2,1,0:T(8,128)(2,1)}, bf16[48,64,128]{2,1,0:T(8,128)(2,1)}, u32[]{:S(2)}, u32[]{:S(2)}) collective-permute-start(bf16[48,64,128]{2,1,0:T(8,128)(2,1)} %get-tuple-element.30), channel_id=1, source_target_pairs={{1,2},{3,4},{5,6},{7,8},{9,10},{11,12},{13,14},{15,0},{2,1},{4,3},... | collective-permute-start | bytes 2359304 | tf_op jit(solution)/shard_map/ppermute | solution.py:26
  59.8 2.3 %copy-start.9 = (f32[96,128]{1,0:T(8,128)}, f32[96,128]{1,0:T(8,128)S(1)}, u32[]{:S(2)}) copy-start(f32[96,128]{1,0:T(8,128)S(1)} %collective-permute-done.13.cols_odd) | copy-start | bytes 147460
  60.6 1.6 %copy-start.10 = (f32[96,128]{1,0:T(8,128)}, f32[96,128]{1,0:T(8,128)S(1)}, u32[]{:S(2)}) copy-start(f32[96,128]{1,0:T(8,128)S(1)} %collective-permute-done.12.cols_even) | copy-start | bytes 147460
  60.6 26.4 %collective-permute-start.14 = (bf16[48,64,128]{2,1,0:T(8,128)(2,1)}, bf16[48,64,128]{2,1,0:T(8,128)(2,1)}, u32[]{:S(2)}, u32[]{:S(2)}) collective-permute-start(bf16[48,64,128]{2,1,0:T(8,128)(2,1)} %get-tuple-element.36), channel_id=1, source_target_pairs={{0,8},{1,9},{2,10},{3,11},{4,12},{5,13},{6,14},{7,15},{8,0},{9,1},... | collective-permute-start | bytes 2359304 | tf_op jit(solution)/shard_map/ppermute | solution.py:40
  76.2 15.9 %all-to-all-start.1 = ((f32[16,1,128]{2,1,0:T(1,128)}), f32[16,1,128]{2,1,0:T(1,128)S(1)}, u32[]{:S(2)}, u32[]{:S(2)}) async-start(f32[16,1,128]{2,1,0:T(1,128)} %broadcast_in_dim.32), calls=%async_computation.1 | async-start | bytes 16384 | tf_op jit(solution)/shard_map/all_to_all | solution.py:443
  87.0 0.8 copy-start.4
  92.1 0.6 copy-start.13

commit v4 on v3

--- a/solution.py
+++ b/solution.py
@@ -160,15 +160,14 @@
     return pl.ds(q, 16, stride=4)
 
 
-def set_weights(offsets, weights, coef):
+def set_weights(table, coef):
     for q in range(4):
-        offset = offsets[every_fourth(q), :]
-        points = [weights[m, every_fourth(q), :] for m in range(4)]
+        *points, offset = (table[m, every_fourth(q), :] for m in range(5))
         for r in range(8):
             value = jnp.zeros((16, LANES), F32)
             for m in range(4):
                 if 0 <= r - m <= 4:
-                    value = jnp.where(offset == r - m, points[m], value)
+                    value = jnp.where(offset == float(r - m), points[m], value)
             coef[q * 8 + r] = value
 
 
@@ -200,7 +199,7 @@
 
 SMEM = pl.BlockSpec(memory_space=pltpu.SMEM)
 VMEM = pl.BlockSpec(memory_space=pltpu.VMEM)
-WEIGHTS = pl.BlockSpec((4, 64, LANES), lambda g: (0, 0, 0))
+TABLE = pl.BlockSpec((5, 64, LANES), lambda g: (0, 0, 0))
 
 
 def scratch(pool):
@@ -209,11 +208,11 @@
     ]
 
 
-def first_kernel(scale, codes, offsets, weights, diag, *refs):
+def first_kernel(scale, codes, table, diag, *refs):
     middle, top = refs[0:7], refs[7:14]
-    adv, rhs, cols, edge_even, edge_odd, own_up, own_down, gather, coef, tmp = refs[14:]
+    adv, rhs, cols, edge_even, edge_odd, gather, coef, tmp, own_up, own_down = refs[14:]
     set_gather(codes, gather, False)
-    set_weights(offsets, weights, coef)
+    set_weights(table, coef)
 
     def level(l, carry):
         values = interpolate(gather, coef, middle, top, l)
@@ -242,7 +241,7 @@
     edge_odd[...] = jnp.where(even_band, up, down)
 
 
-def first_levels(scale, codes, offsets, weights, diag, bands, slots, far):
+def first_levels(scale, codes, table, diag, bands, slots, far):
     slab = jax.ShapeDtypeStruct((16, 64, LANES), F32)
     edge = jax.ShapeDtypeStruct((40, LANES), F32)
     whole = levels_block(lambda g: 0)
@@ -253,25 +252,25 @@
     return pl.pallas_call(
         first_kernel,
         grid=(1,),
-        in_specs=[SMEM, flat(1), flat(64), WEIGHTS, flat(64)] + specs,
-        out_specs=[levels_block(lambda g: 2), whole, flat(64)] + [flat(40)] * 4,
+        in_specs=[SMEM, flat(1), TABLE, flat(64)] + specs,
+        out_specs=[levels_block(lambda g: 2), whole, flat(64)] + [flat(40)] * 2,
         out_shape=[
             jax.ShapeDtypeStruct((64, 64, LANES), BF16), slab, jax.ShapeDtypeStruct((64, LANES), F32)
-        ] + [edge] * 4,
-        scratch_shapes=scratch(7),
+        ] + [edge] * 2,
+        scratch_shapes=scratch(7) + [pltpu.VMEM((40, LANES), F32)] * 2,
         compiler_params=pltpu.CompilerParams(vmem_limit_bytes=32 << 20),
         cost_estimate=pl.CostEstimate(flops=32 * 2 * 128 * 448 * 128, bytes_accessed=6 << 20, transcendentals=0),
         name="first_levels",
-    )(scale, codes, offsets, weights, diag, *pools)
-
-
-def other_kernel(codes, offsets, weights, *refs):
+    )(scale, codes, table, diag, *pools)
+
+
+def other_kernel(codes, table, *refs):
     pools, (start, adv, gather, coef, tmp) = refs[:6], refs[6:]
 
     @pl.when(pl.program_id(0) == 0)
     def _():
         set_gather(codes, gather, True)
-        set_weights(offsets, weights, coef)
+        set_weights(table, coef)
 
     def pair(g, carry):
         values = interpolate(gather, coef, pools, pools, 2 * g, 2 * g + 1)
@@ -285,25 +284,25 @@
         adv[f] = tmp[f].astype(BF16)
 
 
-def other_levels(codes, offsets, weights, bands, slots, start):
+def other_levels(codes, table, bands, slots, start):
     return pl.pallas_call(
         other_kernel,
         grid=(3,),
-        in_specs=[flat(1), flat(64), WEIGHTS]
+        in_specs=[flat(1), TABLE]
         + [levels_block(lambda g: g + g // 2)] * 3
         + [levels_block(lambda g: g)] * 3
         + [pl.BlockSpec(memory_space=pl.ANY)],
         out_specs=levels_block(lambda g: g + g // 2),
         out_shape=jax.ShapeDtypeStruct(start.shape, start.dtype),
         scratch_shapes=scratch(6),
-        input_output_aliases={9: 0},
+        input_output_aliases={8: 0},
         compiler_params=pltpu.CompilerParams(vmem_limit_bytes=32 << 20),
         cost_estimate=pl.CostEstimate(flops=48 * 2 * 128 * 448 * 128, bytes_accessed=6 << 20, transcendentals=0),
         name="other_levels",
-    )(codes, offsets, weights, *bands, *slots, start)
-
-
-def sum_kernel(scale, rhs, diag, cols, own_up, own_down, cols_even, cols_odd, edge_even, edge_odd, n0, n1, sums, rowsums):
+    )(codes, table, *bands, *slots, start)
+
+
+def sum_kernel(scale, rhs, diag, cols, cols_even, cols_odd, edge_even, edge_odd, n0, n1, sums, rowsums):
     lane = iota((64, LANES), 1)
     even_band = lax.rem(lax.axis_index("lat"), 2) == 0
     even_sector = lax.rem(lax.axis_index("lon"), 2) == 0
@@ -334,7 +333,11 @@
         beside = beside + jnp.where(lane16 == LANES - 1, east, pltpu.roll(near, LANES - 1, 1))
         return flag * (second + inner + beside) / (4.0 + edge[32:33, :] * column)
 
-    top, bottom = rim_row(above, own_up[0:16, :], *corners[0]), rim_row(below, own_down[0:16, :], *corners[1])
+    def own_row(r):
+        rows = jnp.concatenate([rhs[l, r : r + 1, :] for l in range(16)], axis=0)
+        return rows / (4.0 + diag[r : r + 1, :] * column)
+
+    top, bottom = rim_row(above, own_row(0), *corners[0]), rim_row(below, own_row(63), *corners[1])
 
     def rim_col(edge, side, which, toward, diag_lane):
         values = edge[0:64]
@@ -379,18 +382,18 @@
         sums[j] = packed
 
 
-def level_sums(scale, rhs, diag, cols, own, cols_rim, edges):
+def level_sums(scale, rhs, diag, cols, cols_rim, edges):
     slab = jax.ShapeDtypeStruct((16, 64, LANES), F32)
     return pl.pallas_call(
         sum_kernel,
-        in_specs=[SMEM] + [VMEM] * 9,
+        in_specs=[SMEM] + [VMEM] * 7,
         out_specs=[VMEM] * 3,
         out_shape=[slab, slab, jax.ShapeDtypeStruct((lax.axis_size("lat"), 1, LANES), F32)],
         scratch_shapes=[pltpu.VMEM((64, LANES), F32)],
         compiler_params=pltpu.CompilerParams(vmem_limit_bytes=60 << 20),
         cost_estimate=pl.CostEstimate(flops=1 << 22, bytes_accessed=2 << 20, transcendentals=0),
         name="level_sums",
-    )(scale, rhs, diag, cols, *own, *cols_rim, *edges)
+    )(scale, rhs, diag, cols, *cols_rim, *edges)
 
 
 def last_kernel(scale, parts, rhs, diag, n0, n1, pressure, residual):
@@ -403,34 +406,35 @@
     def of(k, half):
         return jnp.sum(jnp.where(lane == 16 * k + 8 * half + row, total, 0.0), axis=1, keepdims=True)
 
-    for half in range(2):
-        s0, s1, s2, s3 = (of(k, half) for k in range(4))
-        curve = s0 - s1
-        step = s0 / curve
-        keep = -s1 / curve
-        norm = keep * keep * s0 + 2.0 * keep * step * s1 + step * step * s2
-        ratio = norm / s0
-        bend = norm - (keep * keep * s1 + 2.0 * keep * step * s2 + step * step * s3)
-        other = norm / (bend - ratio * ratio * curve)
-        along = other * (keep + ratio)
-        across = other * step
-        fit_z, fit_p = step + along, across
-        fit_r, fit_n0, fit_n1 = keep - along, step + along - across, across
-        for s in range(8):
-            l = 8 * half + s
-            at = lambda column: column[s : s + 1]
-            inverse = 1.0 / (4.0 + diag[...] * scale[l])
-            start, around = rhs[l], n0[l]
-            pressure[l] = (at(fit_z) * start + at(fit_p) * around) * inverse
-            residual[l] = at(fit_r) * start + at(fit_n0) * around + at(fit_n1) * n1[l]
+    half = pl.program_id(0)
+    s0, s1, s2, s3 = (of(k, half) for k in range(4))
+    curve = s0 - s1
+    step = s0 / curve
+    keep = -s1 / curve
+    norm = keep * keep * s0 + 2.0 * keep * step * s1 + step * step * s2
+    ratio = norm / s0
+    bend = norm - (keep * keep * s1 + 2.0 * keep * step * s2 + step * step * s3)
+    other = norm / (bend - ratio * ratio * curve)
+    along = other * (keep + ratio)
+    across = other * step
+    fit_z, fit_p = step + along, across
+    fit_r, fit_n0, fit_n1 = keep - along, step + along - across, across
+    for s in range(8):
+        at = lambda column: column[s : s + 1]
+        inverse = 1.0 / (4.0 + diag[...] * scale[8 * half + s])
+        start, around = rhs[s], n0[s]
+        pressure[s] = (at(fit_z) * start + at(fit_p) * around) * inverse
+        residual[s] = at(fit_r) * start + at(fit_n0) * around + at(fit_n1) * n1[s]
 
 
 def last_step(scale, parts, rhs, diag, n0, n1):
     slab = jax.ShapeDtypeStruct((16, 64, LANES), F32)
+    block = pl.BlockSpec((8, 64, LANES), lambda g: (g, 0, 0))
     return pl.pallas_call(
         last_kernel,
-        in_specs=[SMEM] + [VMEM] * 5,
-        out_specs=[VMEM] * 2,
+        grid=(2,),
+        in_specs=[SMEM, pl.BlockSpec(parts.shape, lambda g: (0, 0, 0)), block, flat(64), block, block],
+        out_specs=[block] * 2,
         out_shape=[slab, slab],
         input_output_aliases={2: 1, 4: 0},
         compiler_params=pltpu.CompilerParams(vmem_limit_bytes=60 << 20),
@@ -454,20 +458,22 @@
     first_out = pack(lists, bands, 2, lambda g: 2 + 2 * g)
     first_slots = swaps(*first_out, "lon")
     later = after(lists[0], *first_out, *first_far)
+    offsets = after(stencil_offsets, *first_out)
+    table = jnp.concatenate([interp_weights, offsets.astype(F32)[None]], axis=0)
     *other_out, other_far = pack((later, lists[1], first_far[0]), bands, 3, lambda g: g + g // 2)
     other_slots = swaps(*other_out, "lon")
     first_slots = (after(first_slots[0], *other_out), first_slots[1])
     adv, rhs, cols, *edges = first_levels(
-        level_scale, codes, stencil_offsets, interp_weights, diag_coef, bands, first_slots, first_far
+        level_scale, codes, table, diag_coef, bands, first_slots, first_far
     )
-    own, edges = edges[2:], swaps(*edges[:2], "lat")
+    edges = swaps(*edges, "lat")
     rim = jnp.concatenate([cols, edges[0][:16], edges[1][:16]], axis=0)
     cols_rim = swaps(rim, rim, "lon")
     other_far = from_far(after(other_far, *cols_rim))
-    n0, n1, parts = level_sums(level_scale, rhs, diag_coef, cols, own, cols_rim, edges)
+    n0, n1, parts = level_sums(level_scale, rhs, diag_coef, cols, cols_rim, edges)
     parts = jnp.sum(exchange(parts, "lat"), axis=0)
     parts = exchange(jnp.broadcast_to(parts[None], (lax.axis_size("lon"),) + parts.shape), "lon")
-    adv = other_levels(codes, stencil_offsets, interp_weights, bands, other_slots + (other_far,), adv)
+    adv = other_levels(codes, table, bands, other_slots + (other_far,), adv)
     parts = after(parts, adv)
     pressure, residual = last_step(level_scale, parts, rhs, diag_coef, n0, n1)
     return (adv, pressure, residual)

time: 96 us -> 95.1 us (level)
  transfers between devices with their start and end apart: 16 -> 16, of which waited for: 7 -> 7; matrix products, arithmetic and copies ran while one was open for 3% -> 3% of each run, Pallas kernels for 15% -> 16%
where the time goes in v4:
time: 95.1 us; the launch traced here: 94.6 us
  starting transfers between devices  36.2 us (38%)
  waiting for transfers between devices  25.1 us (26%)
  Pallas kernels  20.4 us (21%)
  blocking collectives  8.85 us (9%)
  local copies, waits for them, and re-layouts  3.07 us (3%)
    ppermute x12, starting transfers between devices, swap(): return lax.ppermute(block, axis, ends + [(b, a) for a, b in ends])  26 us
    ppermute x12, waiting for transfers between devices, swap(): return lax.ppermute(block, axis, ends + [(b, a) for a, b in ends])  25.1 us
    all_to_all x1, blocking collectives, exchange(): return lax.all_to_all(parts, axis, split_axis=0, concat_axis=0, tiled=True)  8.85 us
    ppermute x3, starting transfers between devices, from_pole(): return lax.ppermute(block, ('lat', 'lon'), pairs)  6.49 us
    pallas_call x2, Pallas kernels, pack(): pl.pallas_call(functools.partial(pack_kernel, count), grid=(blocks,), in_...  5.84 us
    pallas_call x1, Pallas kernels, other_levels(): pl.pallas_call(other_kernel, grid=(3,), in_specs=[flat(1), TABLE] + [leve...  4.51 us
    pallas_call x1, Pallas kernels, level_sums(): pl.pallas_call(sum_kernel, in_specs=[SMEM] + [VMEM] * 7, out_specs=[VMEM]...  4.44 us
    all_to_all x1, starting transfers between devices, exchange(): return lax.all_to_all(parts, axis, split_axis=0, concat_axis=0, tiled=True)  3.72 us
  transfers between devices with their start and end apart: 16, of which 7 were waited for; matrix products, arithmetic and copies ran while one was open for 3% of the time, Pallas kernels for 16%

profile of v4, /device:TPU:1, one launch (start us, length us, event | category | flops | bytes accessed | tf_op | source)
XLA Modules:
  0.0 94.6 jit_solution(3492310146712736524)
XLA Ops:
  0.6 4.7 %collective-permute-start.3 = (bf16[80,64,128]{2,1,0:T(8,128)(2,1)}, bf16[80,64,128]{2,1,0:T(8,128)(2,1)S(1)}, u32[]{:S(2)}, u32[]{:S(2)}) collective-permute-start(bf16[80,64,128]{2,1,0:T(8,128)(2,1)} %refs_0_.3), channel_id=1, source_target_pairs={{16,32},{48,64},{80,96},{32,16},{64,48},{96,80},{17,33},{49,65},{8... | collective-permute-start | bytes 3932168 | tf_op jit(solution)/shard_map/ppermute | solution.py:26
  5.4 0.1 collective-permute-start.2
  5.5 0.8 reshape.295
  6.3 6.0 %collective-permute-start.1 = (s32[1,128]{1,0:T(1,128)S(1)}, s32[1,128]{1,0:T(1,128)S(1)}, u32[]{:S(2)}, u32[]{:S(2)}) collective-permute-start(s32[1,128]{1,0:T(1,128)S(1)} %get-tuple-element.48.codes), channel_id=1, source_target_pairs={{1,2},{3,4},{5,6},{7,8},{9,10},{11,12},{13,14},{15,0},{2,1},{4,3},... | collective-permute-start | bytes 1544 | tf_op jit(solution)/shard_map/ppermute | solution.py:26
  12.3 1.1 %fusion.4 = (bf16[16,64,128]{2,1,0:T(8,128)(2,1)S(1)}, bf16[16,64,128]{2,1,0:T(8,128)(2,1)S(1)}) fusion(bf16[80,64,128]{2,1,0:T(8,128)(2,1)} %refs_0_.3), kind=kLoop, calls=%fused_computation.24 | loop fusion | bytes 1048576 | tf_op jit(solution)/shard_map/slice | solution.py:456
  13.5 1.2 %collective-permute-done.refs_0_ = s32[1,128]{1,0:T(1,128)S(1)} collective-permute-done((s32[1,128]{1,0:T(1,128)S(1)}, s32[1,128]{1,0:T(1,128)S(1)}, u32[]{:S(2)}, u32[]{:S(2)}) %collective-permute-start) | collective-permute-done | bytes 544 | tf_op jit(solution)/shard_map/ppermute | solution.py:26
  14.7 4.2 %collective-permute-start.5 = (bf16[33,64,128]{2,1,0:T(8,128)(2,1)S(1)}, bf16[33,64,128]{2,1,0:T(8,128)(2,1)S(1)}, u32[]{:S(2)}, u32[]{:S(2)}) collective-permute-start(bf16[33,64,128]{2,1,0:T(8,128)(2,1)S(1)} %pad_maximum_fusion), channel_id=1, source_target_pairs={{16,8},{17,9},{18,10},{19,11},{20,12},{21,13},{22,14},{23,15},{24,... | collective-permute-start | bytes 1622024 | tf_op jit(solution)/shard_map/ppermute | solution.py:40
  19.0 0.7 collective-permute-start.4
  19.7 1.2 %collective-permute-done.3.refs_4_.refs_5_.refs_2_.refs_9_ = bf16[80,64,128]{2,1,0:T(8,128)(2,1)S(1)} collective-permute-done((bf16[80,64,128]{2,1,0:T(8,128)(2,1)}, bf16[80,64,128]{2,1,0:T(8,128)(2,1)S(1)}, u32[]{:S(2)}, u32[]{:S(2)}) %collective-permute-start.3) | collective-permute-done | bytes 1310752 | tf_op jit(solution)/shard_map/ppermute | solution.py:26
  20.9 1.8 %pack.2 = (bf16[32,64,128]{2,1,0:T(8,128)(2,1)S(1)}, bf16[32,64,128]{2,1,0:T(8,128)(2,1)S(1)}) custom-call(s32[1,128]{1,0:T(1,128)S(1)} %collective-permute-done.refs_0_, s32[1,128]{1,0:T(1,128)S(1)} %collective-permute-done.1.refs_1_, bf16[80,64,128]{2,1,0:T(8,128)(2,1)S(1)} %copy-done, ...), custom_call_target="tpu_custom_call" | custom-call | flops 301989888 | bytes 2621440 | tf_op jit(solution)/shard_map/pack/pallas_call | solution.py:122
  22.7 2.0 %collective-permute-start.8 = (bf16[32,64,128]{2,1,0:T(8,128)(2,1)S(1)}, bf16[32,64,128]{2,1,0:T(8,128)(2,1)S(1)}, u32[]{:S(2)}, u32[]{:S(2)}) collective-permute-start(bf16[32,64,128]{2,1,0:T(8,128)(2,1)S(1)} %get-tuple-element.24), channel_id=1, source_target_pairs={{0,1},{2,3},{4,5},{6,7},{8,9},{10,11},{12,13},{14,15},{1,0},{3,2},... | collective-permute-start | bytes 1572872 | tf_op jit(solution)/shard_map/ppermute | solution.py:26
  24.7 4.5 %collective-permute-start.9 = (bf16[32,64,128]{2,1,0:T(8,128)(2,1)S(1)}, bf16[32,64,128]{2,1,0:T(8,128)(2,1)S(1)}, u32[]{:S(2)}, u32[]{:S(2)}) collective-permute-start(bf16[32,64,128]{2,1,0:T(8,128)(2,1)S(1)} %get-tuple-element.25), channel_id=1, source_target_pairs={{1,2},{3,4},{5,6},{7,8},{9,10},{11,12},{13,14},{15,0},{2,1},{4,3},... | collective-permute-start | bytes 1572872 | tf_op jit(solution)/shard_map/ppermute | solution.py:26
  29.2 4.0 %pack.3 = (bf16[48,64,128]{2,1,0:T(8,128)(2,1)}, bf16[48,64,128]{2,1,0:T(8,128)(2,1)}, bf16[48,64,128]{2,1,0:T(8,128)(2,1)}) custom-call(s32[1,128]{1,0:T(1,128)S(1)} %collective-permute-done.refs_0_, s32[1,128]{1,0:T(1,128)S(1)} %collective-permute-done.1.refs_1_, bf16[33,64,128]{2,1,0:T(8,128)(2,1)S(1)} %collective-permute-done.4.refs_2_.refs_5_.refs_12_, ...), custom_call_target="tpu_custom_call" | custom-call | flops 452984832 | bytes 3932160 | tf_op jit(solution)/shard_map/pack/pallas_call | solution.py:122
  33.3 3.7 %collective-permute-done.8.refs_3_.refs_10_ = bf16[32,64,128]{2,1,0:T(8,128)(2,1)S(1)} collective-permute-done((bf16[32,64,128]{2,1,0:T(8,128)(2,1)S(1)}, bf16[32,64,128]{2,1,0:T(8,128)(2,1)S(1)}, u32[]{:S(2)}, u32[]{:S(2)}) %collective-permute-start.8) | collective-permute-done | bytes 524320 | tf_op jit(solution)/shard_map/ppermute | solution.py:26
  37.0 7.7 %collective-permute-done.9.refs_4_.refs_11_ = bf16[32,64,128]{2,1,0:T(8,128)(2,1)S(1)} collective-permute-done((bf16[32,64,128]{2,1,0:T(8,128)(2,1)S(1)}, bf16[32,64,128]{2,1,0:T(8,128)(2,1)S(1)}, u32[]{:S(2)}, u32[]{:S(2)}) %collective-permute-start.9) | collective-permute-done | bytes 524320 | tf_op jit(solution)/shard_map/ppermute | solution.py:26
  44.7 3.2 %first_levels.1 = (bf16[64,64,128]{2,1,0:T(8,128)(2,1)}, f32[16,64,128]{2,1,0:T(8,128)}, f32[64,128]{1,0:T(8,128)S(1)}, f32[40,128]{1,0:T(8,128)S(1)}, f32[40,128]{1,0:T(8,128)S(1)}) custom-call(f32[16]{0:T(128)S(1)} %copy-done.3, s32[1,128]{1,0:T(1,128)S(1)} %get-tuple-element.48.codes, f32[5,64,128]{2,1,0:T(8,128)S(1)} %pad_maximum_fusion.1.table, ...), custom_call_target="tpu_custom_call" | custom-call | flops 469762048 | bytes 6291456 | tf_op jit(solution)/shard_map/first_levels/pallas_call | solution.py:252
  47.9 0.4 collective-permute-start.10
  48.3 1.9 %collective-permute-start.11 = (f32[40,128]{1,0:T(8,128)S(1)}, f32[40,128]{1,0:T(8,128)S(1)}, u32[]{:S(2)}, u32[]{:S(2)}) collective-permute-start(f32[40,128]{1,0:T(8,128)S(1)} %get-tuple-element.35), channel_id=1, source_target_pairs={{16,32},{48,64},{80,96},{32,16},{64,48},{96,80},{17,33},{49,65},{8... | collective-permute-start | bytes 61448 | tf_op jit(solution)/shard_map/ppermute | solution.py:26
  50.2 3.1 %collective-permute-done.11.edge_odd = f32[40,128]{1,0:T(8,128)S(1)} collective-permute-done((f32[40,128]{1,0:T(8,128)S(1)}, f32[40,128]{1,0:T(8,128)S(1)}, u32[]{:S(2)}, u32[]{:S(2)}) %collective-permute-start.11) | collective-permute-done | bytes 20512 | tf_op jit(solution)/shard_map/ppermute | solution.py:26
  53.4 3.3 %collective-permute-start.13 = (f32[96,128]{1,0:T(8,128)S(1)}, f32[96,128]{1,0:T(8,128)S(1)}, u32[]{:S(2)}, u32[]{:S(2)}) collective-permute-start(f32[96,128]{1,0:T(8,128)S(1)} %pad_maximum_fusion.2), channel_id=1, source_target_pairs={{1,2},{3,4},{5,6},{7,8},{9,10},{11,12},{13,14},{15,0},{2,1},{4,3},... | collective-permute-start | bytes 147464 | tf_op jit(solution)/shard_map/ppermute | solution.py:26
  56.6 1.5 %collective-permute-start.6 = (bf16[48,64,128]{2,1,0:T(8,128)(2,1)}, bf16[48,64,128]{2,1,0:T(8,128)(2,1)}, u32[]{:S(2)}, u32[]{:S(2)}) collective-permute-start(bf16[48,64,128]{2,1,0:T(8,128)(2,1)} %get-tuple-element.29), channel_id=1, source_target_pairs={{0,1},{2,3},{4,5},{6,7},{8,9},{10,11},{12,13},{14,15},{1,0},{3,2},... | collective-permute-start | bytes 2359304 | tf_op jit(solution)/shard_map/ppermute | solution.py:26
  58.1 1.6 %collective-permute-start.7 = (bf16[48,64,128]{2,1,0:T(8,128)(2,1)}, bf16[48,64,128]{2,1,0:T(8,128)(2,1)}, u32[]{:S(2)}, u32[]{:S(2)}) collective-permute-start(bf16[48,64,128]{2,1,0:T(8,128)(2,1)} %get-tuple-element.30), channel_id=1, source_target_pairs={{1,2},{3,4},{5,6},{7,8},{9,10},{11,12},{13,14},{15,0},{2,1},{4,3},... | collective-permute-start | bytes 2359304 | tf_op jit(solution)/shard_map/ppermute | solution.py:26
  59.7 0.9 collective-permute-done.12.cols_even
  60.6 1.6 %collective-permute-start.14 = (bf16[48,64,128]{2,1,0:T(8,128)(2,1)}, bf16[48,64,128]{2,1,0:T(8,128)(2,1)}, u32[]{:S(2)}, u32[]{:S(2)}) collective-permute-start(bf16[48,64,128]{2,1,0:T(8,128)(2,1)} %get-tuple-element.36), channel_id=1, source_target_pairs={{0,8},{1,9},{2,10},{3,11},{4,12},{5,13},{6,14},{7,15},{8,0},{9,1},... | collective-permute-start | bytes 2359304 | tf_op jit(solution)/shard_map/ppermute | solution.py:40
  62.1 4.4 %level_sums.1 = (f32[16,64,128]{2,1,0:T(8,128)}, f32[16,64,128]{2,1,0:T(8,128)}, f32[8,1,128]{2,1,0:T(1,128)}) custom-call(f32[16]{0:T(128)} %scale.5, f32[16,64,128]{2,1,0:T(8,128)} %get-tuple-element.38.rhs, f32[64,128]{1,0:T(8,128)} %diag.5, f32[64,128]{1,0:T(8,128)} %copy-done.2, f32[96,128]{1,0:T(8,128)} %copy-done.6, f32[96,128]{1,0:T(8,128)} %copy-done.5, ...), custom_call_target="tpu_custom_call" | custom-call | flops 4194304 | bytes 2097152 | tf_op jit(solution)/shard_map/level_sums/pallas_call | solution.py:387
  66.6 8.9 %all_to_all.10 = f32[8,1,128]{2,1,0:T(1,128)S(1)} all-to-all(f32[8,1,128]{2,1,0:T(1,128)} %get-tuple-element.39), channel_id=1, replica_groups=mesh['lat'=8,'lon'=16] {'lat'}, dimensions={0} | all-to-all | bytes 8192 | tf_op jit(solution)/shard_map/all_to_all | solution.py:447
  75.5 0.6 broadcast_in_dim.36
  76.1 3.7 %all-to-all-start.1 = ((f32[16,1,128]{2,1,0:T(1,128)}), f32[16,1,128]{2,1,0:T(1,128)S(1)}, u32[]{:S(2)}, u32[]{:S(2)}) async-start(f32[16,1,128]{2,1,0:T(1,128)} %broadcast_in_dim.36), calls=%async_computation.1 | async-start | bytes 16384 | tf_op jit(solution)/shard_map/all_to_all | solution.py:447
  79.8 7.3 %collective-permute-done.7.refs_4_ = bf16[48,64,128]{2,1,0:T(8,128)(2,1)} collective-permute-done((bf16[48,64,128]{2,1,0:T(8,128)(2,1)}, bf16[48,64,128]{2,1,0:T(8,128)(2,1)}, u32[]{:S(2)}, u32[]{:S(2)}) %collective-permute-start.7) | collective-permute-done | bytes 786464 | tf_op jit(solution)/shard_map/ppermute | solution.py:26
  87.1 4.5 %other_levels.1 = bf16[64,64,128]{2,1,0:T(8,128)(2,1)} custom-call(s32[1,128]{1,0:T(1,128)S(1)} %get-tuple-element.48.codes, f32[5,64,128]{2,1,0:T(8,128)S(1)} %pad_maximum_fusion.1.table, bf16[80,64,128]{2,1,0:T(8,128)(2,1)S(1)} %copy-done, ...), custom_call_target="tpu_custom_call", output_to_operand_aliasing={{}: (8, {})} | custom-call | flops 704643072 | bytes 6291456 | tf_op jit(solution)/shard_map/other_levels/pallas_call | solution.py:288
  91.6 0.6 copy-done.9
  92.2 2.4 %last_step.1 = (f32[16,64,128]{2,1,0:T(8,128)}, f32[16,64,128]{2,1,0:T(8,128)}) custom-call(f32[16]{0:T(128)} %scale.5, f32[16,1,128]{2,1,0:T(1,128)} %copy-done.9, f32[16,64,128]{2,1,0:T(8,128)} %get-tuple-element.38.rhs, f32[64,128]{1,0:T(8,128)} %diag.5, f32[16,64,128]{2,1,0:T(8,128)} %get-tuple-element.41.n0, ...), custom_call_target="tpu_custom_call", output_to_operand_aliasing={{1}: (2, {}), {0}: (4, {})} | custom-call | flops 2097152 | bytes 3145728 | tf_op jit(solution)/shard_map/last_step/pallas_call | solution.py:433
  (42 shorter events, 0.2 us)
Async XLA Ops:
  0.6 20.2 %copy-start = (bf16[80,64,128]{2,1,0:T(8,128)(2,1)S(1)}, bf16[80,64,128]{2,1,0:T(8,128)(2,1)}, u32[]{:S(2)}) copy-start(bf16[80,64,128]{2,1,0:T(8,128)(2,1)} %refs_0_.3) | copy-start | bytes 3932164
  0.6 20.2 %collective-permute-start.3 = (bf16[80,64,128]{2,1,0:T(8,128)(2,1)}, bf16[80,64,128]{2,1,0:T(8,128)(2,1)S(1)}, u32[]{:S(2)}, u32[]{:S(2)}) collective-permute-start(bf16[80,64,128]{2,1,0:T(8,128)(2,1)} %refs_0_.3), channel_id=1, source_target_pairs={{16,32},{48,64},{80,96},{32,16},{64,48},{96,80},{17,33},{49,65},{8... | collective-permute-start | bytes 3932168 | tf_op jit(solution)/shard_map/ppermute | solution.py:26
  5.4 15.5 %collective-permute-start.2 = (bf16[80,64,128]{2,1,0:T(8,128)(2,1)}, bf16[80,64,128]{2,1,0:T(8,128)(2,1)}, u32[]{:S(2)}, u32[]{:S(2)}) collective-permute-start(bf16[80,64,128]{2,1,0:T(8,128)(2,1)} %refs_0_.3), channel_id=1, source_target_pairs={{0,16},{32,48},{64,80},{96,112},{16,0},{48,32},{80,64},{112,96},{1... | collective-permute-start | bytes 3932168 | tf_op jit(solution)/shard_map/ppermute | solution.py:26
  6.3 7.2 %collective-permute-start.1 = (s32[1,128]{1,0:T(1,128)S(1)}, s32[1,128]{1,0:T(1,128)S(1)}, u32[]{:S(2)}, u32[]{:S(2)}) collective-permute-start(s32[1,128]{1,0:T(1,128)S(1)} %get-tuple-element.48.codes), channel_id=1, source_target_pairs={{1,2},{3,4},{5,6},{7,8},{9,10},{11,12},{13,14},{15,0},{2,1},{4,3},... | collective-permute-start | bytes 1544 | tf_op jit(solution)/shard_map/ppermute | solution.py:26
  12.3 2.4 %collective-permute-start = (s32[1,128]{1,0:T(1,128)S(1)}, s32[1,128]{1,0:T(1,128)S(1)}, u32[]{:S(2)}, u32[]{:S(2)}) collective-permute-start(s32[1,128]{1,0:T(1,128)S(1)} %get-tuple-element.48.codes), channel_id=1, source_target_pairs={{0,1},{2,3},{4,5},{6,7},{8,9},{10,11},{12,13},{14,15},{1,0},{3,2},... | collective-permute-start | bytes 1544 | tf_op jit(solution)/shard_map/ppermute | solution.py:26
  14.7 14.5 %collective-permute-start.5 = (bf16[33,64,128]{2,1,0:T(8,128)(2,1)S(1)}, bf16[33,64,128]{2,1,0:T(8,128)(2,1)S(1)}, u32[]{:S(2)}, u32[]{:S(2)}) collective-permute-start(bf16[33,64,128]{2,1,0:T(8,128)(2,1)S(1)} %pad_maximum_fusion), channel_id=1, source_target_pairs={{16,8},{17,9},{18,10},{19,11},{20,12},{21,13},{22,14},{23,15},{24,... | collective-permute-start | bytes 1622024 | tf_op jit(solution)/shard_map/ppermute | solution.py:40
  19.0 10.3 %collective-permute-start.4 = (bf16[33,64,128]{2,1,0:T(8,128)(2,1)S(1)}, bf16[33,64,128]{2,1,0:T(8,128)(2,1)S(1)}, u32[]{:S(2)}, u32[]{:S(2)}) collective-permute-start(bf16[33,64,128]{2,1,0:T(8,128)(2,1)S(1)} %pad_maximum_fusion), channel_id=1, source_target_pairs={{0,8},{1,9},{2,10},{3,11},{4,12},{5,13},{6,14},{7,15},{8,0},{9,1},... | collective-permute-start | bytes 1622024 | tf_op jit(solution)/shard_map/ppermute | solution.py:40
  22.7 14.3 %collective-permute-start.8 = (bf16[32,64,128]{2,1,0:T(8,128)(2,1)S(1)}, bf16[32,64,128]{2,1,0:T(8,128)(2,1)S(1)}, u32[]{:S(2)}, u32[]{:S(2)}) collective-permute-start(bf16[32,64,128]{2,1,0:T(8,128)(2,1)S(1)} %get-tuple-element.24), channel_id=1, source_target_pairs={{0,1},{2,3},{4,5},{6,7},{8,9},{10,11},{12,13},{14,15},{1,0},{3,2},... | collective-permute-start | bytes 1572872 | tf_op jit(solution)/shard_map/ppermute | solution.py:26
  24.7 8.6 %copy-start.10 = (s32[64,128]{1,0:T(8,128)S(1)}, s32[64,128]{1,0:T(8,128)}, u32[]{:S(2)}) copy-start(s32[64,128]{1,0:T(8,128)} %param.8) | copy-start | bytes 98308
  24.7 8.6 %copy-start.4 = (f32[4,64,128]{2,1,0:T(8,128)S(1)}, f32[4,64,128]{2,1,0:T(8,128)}, u32[]{:S(2)}) copy-start(f32[4,64,128]{2,1,0:T(8,128)} %param.9) | copy-start | bytes 393220
  24.7 20.0 %copy-start.1 = (f32[64,128]{1,0:T(8,128)S(1)}, f32[64,128]{1,0:T(8,128)}, u32[]{:S(2)}) copy-start(f32[64,128]{1,0:T(8,128)} %diag.5) | copy-start | bytes 98308
  24.7 20.0 %copy-start.3 = (f32[16]{0:T(128)S(1)}, f32[16]{0:T(128)}, u32[]{:S(2)}) copy-start(f32[16]{0:T(128)} %scale.5) | copy-start | bytes 196
  24.7 20.0 %collective-permute-start.9 = (bf16[32,64,128]{2,1,0:T(8,128)(2,1)S(1)}, bf16[32,64,128]{2,1,0:T(8,128)(2,1)S(1)}, u32[]{:S(2)}, u32[]{:S(2)}) collective-permute-start(bf16[32,64,128]{2,1,0:T(8,128)(2,1)S(1)} %get-tuple-element.25), channel_id=1, source_target_pairs={{1,2},{3,4},{5,6},{7,8},{9,10},{11,12},{13,14},{15,0},{2,1},{4,3},... | collective-permute-start | bytes 1572872 | tf_op jit(solution)/shard_map/ppermute | solution.py:26
  47.9 14.3 %copy-start.2 = (f32[64,128]{1,0:T(8,128)}, f32[64,128]{1,0:T(8,128)S(1)}, u32[]{:S(2)}) copy-start(f32[64,128]{1,0:T(8,128)S(1)} %get-tuple-element.33.cols) | copy-start | bytes 98308
  47.9 2.3 %collective-permute-start.10 = (f32[40,128]{1,0:T(8,128)S(1)}, f32[40,128]{1,0:T(8,128)S(1)}, u32[]{:S(2)}, u32[]{:S(2)}) collective-permute-start(f32[40,128]{1,0:T(8,128)S(1)} %get-tuple-element.34), channel_id=1, source_target_pairs={{0,16},{32,48},{64,80},{96,112},{16,0},{48,32},{80,64},{112,96},{1... | collective-permute-start | bytes 61448 | tf_op jit(solution)/shard_map/ppermute | solution.py:26
  48.3 5.1 %collective-permute-start.11 = (f32[40,128]{1,0:T(8,128)S(1)}, f32[40,128]{1,0:T(8,128)S(1)}, u32[]{:S(2)}, u32[]{:S(2)}) collective-permute-start(f32[40,128]{1,0:T(8,128)S(1)} %get-tuple-element.35), channel_id=1, source_target_pairs={{16,32},{48,64},{80,96},{32,16},{64,48},{96,80},{17,33},{49,65},{8... | collective-permute-start | bytes 61448 | tf_op jit(solution)/shard_map/ppermute | solution.py:26
  50.2 11.9 %copy-start.7 = (f32[40,128]{1,0:T(8,128)}, f32[40,128]{1,0:T(8,128)S(1)}, u32[]{:S(2)}) copy-start(f32[40,128]{1,0:T(8,128)S(1)} %collective-permute-done.10.edge_even) | copy-start | bytes 61444
  53.3 8.8 %copy-start.8 = (f32[40,128]{1,0:T(8,128)}, f32[40,128]{1,0:T(8,128)S(1)}, u32[]{:S(2)}) copy-start(f32[40,128]{1,0:T(8,128)S(1)} %collective-permute-done.11.edge_odd) | copy-start | bytes 61444
  53.4 6.3 %collective-permute-start.13 = (f32[96,128]{1,0:T(8,128)S(1)}, f32[96,128]{1,0:T(8,128)S(1)}, u32[]{:S(2)}, u32[]{:S(2)}) collective-permute-start(f32[96,128]{1,0:T(8,128)S(1)} %pad_maximum_fusion.2), channel_id=1, source_target_pairs={{1,2},{3,4},{5,6},{7,8},{9,10},{11,12},{13,14},{15,0},{2,1},{4,3},... | collective-permute-start | bytes 147464 | tf_op jit(solution)/shard_map/ppermute | solution.py:26
  56.6 3.9 %collective-permute-start.12 = (f32[96,128]{1,0:T(8,128)S(1)}, f32[96,128]{1,0:T(8,128)S(1)}, u32[]{:S(2)}, u32[]{:S(2)}) collective-permute-start(f32[96,128]{1,0:T(8,128)S(1)} %pad_maximum_fusion.2), channel_id=1, source_target_pairs={{0,1},{2,3},{4,5},{6,7},{8,9},{10,11},{12,13},{14,15},{1,0},{3,2},... | collective-permute-start | bytes 147464 | tf_op jit(solution)/shard_map/ppermute | solution.py:26
  56.6 23.2 %collective-permute-start.6 = (bf16[48,64,128]{2,1,0:T(8,128)(2,1)}, bf16[48,64,128]{2,1,0:T(8,128)(2,1)}, u32[]{:S(2)}, u32[]{:S(2)}) collective-permute-start(bf16[48,64,128]{2,1,0:T(8,128)(2,1)} %get-tuple-element.29), channel_id=1, source_target_pairs={{0,1},{2,3},{4,5},{6,7},{8,9},{10,11},{12,13},{14,15},{1,0},{3,2},... | collective-permute-start | bytes 2359304 | tf_op jit(solution)/shard_map/ppermute | solution.py:26
  58.1 29.0 %collective-permute-start.7 = (bf16[48,64,128]{2,1,0:T(8,128)(2,1)}, bf16[48,64,128]{2,1,0:T(8,128)(2,1)}, u32[]{:S(2)}, u32[]{:S(2)}) collective-permute-start(bf16[48,64,128]{2,1,0:T(8,128)(2,1)} %get-tuple-element.30), channel_id=1, source_target_pairs={{1,2},{3,4},{5,6},{7,8},{9,10},{11,12},{13,14},{15,0},{2,1},{4,3},... | collective-permute-start | bytes 2359304 | tf_op jit(solution)/shard_map/ppermute | solution.py:26
  59.7 2.4 %copy-start.5 = (f32[96,128]{1,0:T(8,128)}, f32[96,128]{1,0:T(8,128)S(1)}, u32[]{:S(2)}) copy-start(f32[96,128]{1,0:T(8,128)S(1)} %collective-permute-done.13.cols_odd) | copy-start | bytes 147460
  60.6 1.6 %copy-start.6 = (f32[96,128]{1,0:T(8,128)}, f32[96,128]{1,0:T(8,128)S(1)}, u32[]{:S(2)}) copy-start(f32[96,128]{1,0:T(8,128)S(1)} %collective-permute-done.12.cols_even) | copy-start | bytes 147460
  60.6 26.5 %collective-permute-start.14 = (bf16[48,64,128]{2,1,0:T(8,128)(2,1)}, bf16[48,64,128]{2,1,0:T(8,128)(2,1)}, u32[]{:S(2)}, u32[]{:S(2)}) collective-permute-start(bf16[48,64,128]{2,1,0:T(8,128)(2,1)} %get-tuple-element.36), channel_id=1, source_target_pairs={{0,8},{1,9},{2,10},{3,11},{4,12},{5,13},{6,14},{7,15},{8,0},{9,1},... | collective-permute-start | bytes 2359304 | tf_op jit(solution)/shard_map/ppermute | solution.py:40
  76.1 15.5 %all-to-all-start.1 = ((f32[16,1,128]{2,1,0:T(1,128)}), f32[16,1,128]{2,1,0:T(1,128)S(1)}, u32[]{:S(2)}, u32[]{:S(2)}) async-start(f32[16,1,128]{2,1,0:T(1,128)} %broadcast_in_dim.36), calls=%async_computation.1 | async-start | bytes 16384 | tf_op jit(solution)/shard_map/all_to_all | solution.py:447
  91.6 0.6 copy-start.9

commit v5 on v4

--- a/solution.py
+++ b/solution.py
@@ -141,8 +141,9 @@
     rank = ranks(turn == sub)
     turn, tile = turn[:1], codes[:1] & (SPAN - 1)
     place = jnp.where(turn == 0, tile.astype(F32), -1.0)
-    place = jnp.where(turn == 1, 48.0 + rank[1:2], place)
-    place = jnp.where(turn == 2, 64.0 + rank[2:3], place)
+    even_at, odd_at = (64.0, 48.0) if far_slots else (48.0, 64.0)
+    place = jnp.where(turn == 1, even_at + rank[1:2], place)
+    place = jnp.where(turn == 2, odd_at + rank[2:3], place)
     if far_slots:
         across = 80.0 + rank[3:4]
     else:
@@ -473,7 +474,7 @@
     n0, n1, parts = level_sums(level_scale, rhs, diag_coef, cols, cols_rim, edges)
     parts = jnp.sum(exchange(parts, "lat"), axis=0)
     parts = exchange(jnp.broadcast_to(parts[None], (lax.axis_size("lon"),) + parts.shape), "lon")
-    adv = other_levels(codes, table, bands, other_slots + (other_far,), adv)
+    adv = other_levels(codes, table, bands, (other_slots[1], other_slots[0], other_far), adv)
     parts = after(parts, adv)
     pressure, residual = last_step(level_scale, parts, rhs, diag_coef, n0, n1)
     return (adv, pressure, residual)

time: 95.1 us -> 93.1 us (0.979)
  starting transfers between devices: 36.2 us -> 35.1 us
    ppermute x12, starting transfers between devices: 26 us -> 24.6 us  [swap(): return lax.ppermute(block, axis, ends + [(b, a) for a, b in ends])]
  transfers between devices with their start and end apart: 16 -> 16, of which waited for: 7 -> 8; matrix products, arithmetic and copies ran while one was open for 3% -> 3% of each run, Pallas kernels for 16% -> 16%
where the time goes in v5:
time: 93.1 us; the launch traced here: 92.6 us
  starting transfers between devices  35.1 us (38%)
  waiting for transfers between devices  24.2 us (26%)
  Pallas kernels  20.4 us (22%)
  blocking collectives  8.83 us (9%)
  local copies, waits for them, and re-layouts  3.07 us (3%)
    ppermute x12, starting transfers between devices, swap(): return lax.ppermute(block, axis, ends + [(b, a) for a, b in ends])  24.6 us
    ppermute x12, waiting for transfers between devices, swap(): return lax.ppermute(block, axis, ends + [(b, a) for a, b in ends])  24.2 us
    all_to_all x1, blocking collectives, exchange(): return lax.all_to_all(parts, axis, split_axis=0, concat_axis=0, tiled=True)  8.83 us
    ppermute x3, starting transfers between devices, from_pole(): return lax.ppermute(block, ('lat', 'lon'), pairs)  6.49 us
    pallas_call x2, Pallas kernels, pack(): pl.pallas_call(functools.partial(pack_kernel, count), grid=(blocks,), in_...  5.84 us
    pallas_call x1, Pallas kernels, other_levels(): pl.pallas_call(other_kernel, grid=(3,), in_specs=[flat(1), TABLE] + [leve...  4.51 us
    pallas_call x1, Pallas kernels, level_sums(): pl.pallas_call(sum_kernel, in_specs=[SMEM] + [VMEM] * 7, out_specs=[VMEM]...  4.44 us
    all_to_all x1, starting transfers between devices, exchange(): return lax.all_to_all(parts, axis, split_axis=0, concat_axis=0, tiled=True)  4.07 us
  transfers between devices with their start and end apart: 16, of which 8 were waited for; matrix products, arithmetic and copies ran while one was open for 3% of the time, Pallas kernels for 16%

profile of v5, /device:TPU:1, one launch (start us, length us, event | category | flops | bytes accessed | tf_op | source)
XLA Modules:
  0.0 92.6 jit_solution(1410046128002418953)
XLA Ops:
  0.6 4.7 %collective-permute-start.3 = (bf16[80,64,128]{2,1,0:T(8,128)(2,1)}, bf16[80,64,128]{2,1,0:T(8,128)(2,1)S(1)}, u32[]{:S(2)}, u32[]{:S(2)}) collective-permute-start(bf16[80,64,128]{2,1,0:T(8,128)(2,1)} %refs_0_.3), channel_id=1, source_target_pairs={{16,32},{48,64},{80,96},{32,16},{64,48},{96,80},{17,33},{49,65},{8... | collective-permute-start | bytes 3932168 | tf_op jit(solution)/shard_map/ppermute | solution.py:26
  5.4 0.1 collective-permute-start.2
  5.5 0.8 reshape.295
  6.3 6.0 %collective-permute-start.1 = (s32[1,128]{1,0:T(1,128)S(1)}, s32[1,128]{1,0:T(1,128)S(1)}, u32[]{:S(2)}, u32[]{:S(2)}) collective-permute-start(s32[1,128]{1,0:T(1,128)S(1)} %get-tuple-element.48.codes), channel_id=1, source_target_pairs={{1,2},{3,4},{5,6},{7,8},{9,10},{11,12},{13,14},{15,0},{2,1},{4,3},... | collective-permute-start | bytes 1544 | tf_op jit(solution)/shard_map/ppermute | solution.py:26
  12.3 1.1 %fusion.4 = (bf16[16,64,128]{2,1,0:T(8,128)(2,1)S(1)}, bf16[16,64,128]{2,1,0:T(8,128)(2,1)S(1)}) fusion(bf16[80,64,128]{2,1,0:T(8,128)(2,1)} %refs_0_.3), kind=kLoop, calls=%fused_computation.24 | loop fusion | bytes 1048576 | tf_op jit(solution)/shard_map/slice | solution.py:457
  13.5 1.2 %collective-permute-done.refs_0_ = s32[1,128]{1,0:T(1,128)S(1)} collective-permute-done((s32[1,128]{1,0:T(1,128)S(1)}, s32[1,128]{1,0:T(1,128)S(1)}, u32[]{:S(2)}, u32[]{:S(2)}) %collective-permute-start) | collective-permute-done | bytes 544 | tf_op jit(solution)/shard_map/ppermute | solution.py:26
  14.7 4.2 %collective-permute-start.5 = (bf16[33,64,128]{2,1,0:T(8,128)(2,1)S(1)}, bf16[33,64,128]{2,1,0:T(8,128)(2,1)S(1)}, u32[]{:S(2)}, u32[]{:S(2)}) collective-permute-start(bf16[33,64,128]{2,1,0:T(8,128)(2,1)S(1)} %pad_maximum_fusion), channel_id=1, source_target_pairs={{16,8},{17,9},{18,10},{19,11},{20,12},{21,13},{22,14},{23,15},{24,... | collective-permute-start | bytes 1622024 | tf_op jit(solution)/shard_map/ppermute | solution.py:40
  19.0 0.7 collective-permute-start.4
  19.7 1.2 %collective-permute-done.3.refs_4_.refs_5_.refs_2_.refs_9_ = bf16[80,64,128]{2,1,0:T(8,128)(2,1)S(1)} collective-permute-done((bf16[80,64,128]{2,1,0:T(8,128)(2,1)}, bf16[80,64,128]{2,1,0:T(8,128)(2,1)S(1)}, u32[]{:S(2)}, u32[]{:S(2)}) %collective-permute-start.3) | collective-permute-done | bytes 1310752 | tf_op jit(solution)/shard_map/ppermute | solution.py:26
  20.9 1.8 %pack.2 = (bf16[32,64,128]{2,1,0:T(8,128)(2,1)S(1)}, bf16[32,64,128]{2,1,0:T(8,128)(2,1)S(1)}) custom-call(s32[1,128]{1,0:T(1,128)S(1)} %collective-permute-done.refs_0_, s32[1,128]{1,0:T(1,128)S(1)} %collective-permute-done.1.refs_1_, bf16[80,64,128]{2,1,0:T(8,128)(2,1)S(1)} %copy-done, ...), custom_call_target="tpu_custom_call" | custom-call | flops 301989888 | bytes 2621440 | tf_op jit(solution)/shard_map/pack/pallas_call | solution.py:122
  22.7 2.0 %collective-permute-start.8 = (bf16[32,64,128]{2,1,0:T(8,128)(2,1)S(1)}, bf16[32,64,128]{2,1,0:T(8,128)(2,1)S(1)}, u32[]{:S(2)}, u32[]{:S(2)}) collective-permute-start(bf16[32,64,128]{2,1,0:T(8,128)(2,1)S(1)} %get-tuple-element.24), channel_id=1, source_target_pairs={{0,1},{2,3},{4,5},{6,7},{8,9},{10,11},{12,13},{14,15},{1,0},{3,2},... | collective-permute-start | bytes 1572872 | tf_op jit(solution)/shard_map/ppermute | solution.py:26
  24.7 4.5 %collective-permute-start.9 = (bf16[32,64,128]{2,1,0:T(8,128)(2,1)S(1)}, bf16[32,64,128]{2,1,0:T(8,128)(2,1)S(1)}, u32[]{:S(2)}, u32[]{:S(2)}) collective-permute-start(bf16[32,64,128]{2,1,0:T(8,128)(2,1)S(1)} %get-tuple-element.25), channel_id=1, source_target_pairs={{1,2},{3,4},{5,6},{7,8},{9,10},{11,12},{13,14},{15,0},{2,1},{4,3},... | collective-permute-start | bytes 1572872 | tf_op jit(solution)/shard_map/ppermute | solution.py:26
  29.2 4.0 %pack.3 = (bf16[48,64,128]{2,1,0:T(8,128)(2,1)}, bf16[48,64,128]{2,1,0:T(8,128)(2,1)}, bf16[48,64,128]{2,1,0:T(8,128)(2,1)}) custom-call(s32[1,128]{1,0:T(1,128)S(1)} %collective-permute-done.refs_0_, s32[1,128]{1,0:T(1,128)S(1)} %collective-permute-done.1.refs_1_, bf16[33,64,128]{2,1,0:T(8,128)(2,1)S(1)} %collective-permute-done.4.refs_2_.refs_5_.refs_12_, ...), custom_call_target="tpu_custom_call" | custom-call | flops 452984832 | bytes 3932160 | tf_op jit(solution)/shard_map/pack/pallas_call | solution.py:122
  33.3 3.7 %collective-permute-done.8.refs_3_.refs_10_ = bf16[32,64,128]{2,1,0:T(8,128)(2,1)S(1)} collective-permute-done((bf16[32,64,128]{2,1,0:T(8,128)(2,1)S(1)}, bf16[32,64,128]{2,1,0:T(8,128)(2,1)S(1)}, u32[]{:S(2)}, u32[]{:S(2)}) %collective-permute-start.8) | collective-permute-done | bytes 524320 | tf_op jit(solution)/shard_map/ppermute | solution.py:26
  37.0 7.7 %collective-permute-done.9.refs_4_.refs_11_ = bf16[32,64,128]{2,1,0:T(8,128)(2,1)S(1)} collective-permute-done((bf16[32,64,128]{2,1,0:T(8,128)(2,1)S(1)}, bf16[32,64,128]{2,1,0:T(8,128)(2,1)S(1)}, u32[]{:S(2)}, u32[]{:S(2)}) %collective-permute-start.9) | collective-permute-done | bytes 524320 | tf_op jit(solution)/shard_map/ppermute | solution.py:26
  44.7 3.2 %first_levels.1 = (bf16[64,64,128]{2,1,0:T(8,128)(2,1)}, f32[16,64,128]{2,1,0:T(8,128)}, f32[64,128]{1,0:T(8,128)S(1)}, f32[40,128]{1,0:T(8,128)S(1)}, f32[40,128]{1,0:T(8,128)S(1)}) custom-call(f32[16]{0:T(128)S(1)} %copy-done.3, s32[1,128]{1,0:T(1,128)S(1)} %get-tuple-element.48.codes, f32[5,64,128]{2,1,0:T(8,128)S(1)} %pad_maximum_fusion.1.table, ...), custom_call_target="tpu_custom_call" | custom-call | flops 469762048 | bytes 6291456 | tf_op jit(solution)/shard_map/first_levels/pallas_call | solution.py:253
  47.9 0.4 collective-permute-start.10
  48.3 1.9 %collective-permute-start.11 = (f32[40,128]{1,0:T(8,128)S(1)}, f32[40,128]{1,0:T(8,128)S(1)}, u32[]{:S(2)}, u32[]{:S(2)}) collective-permute-start(f32[40,128]{1,0:T(8,128)S(1)} %get-tuple-element.35), channel_id=1, source_target_pairs={{16,32},{48,64},{80,96},{32,16},{64,48},{96,80},{17,33},{49,65},{8... | collective-permute-start | bytes 61448 | tf_op jit(solution)/shard_map/ppermute | solution.py:26
  50.2 3.1 %collective-permute-done.11.edge_odd = f32[40,128]{1,0:T(8,128)S(1)} collective-permute-done((f32[40,128]{1,0:T(8,128)S(1)}, f32[40,128]{1,0:T(8,128)S(1)}, u32[]{:S(2)}, u32[]{:S(2)}) %collective-permute-start.11) | collective-permute-done | bytes 20512 | tf_op jit(solution)/shard_map/ppermute | solution.py:26
  53.4 3.3 %collective-permute-start.13 = (f32[96,128]{1,0:T(8,128)S(1)}, f32[96,128]{1,0:T(8,128)S(1)}, u32[]{:S(2)}, u32[]{:S(2)}) collective-permute-start(f32[96,128]{1,0:T(8,128)S(1)} %pad_maximum_fusion.2), channel_id=1, source_target_pairs={{1,2},{3,4},{5,6},{7,8},{9,10},{11,12},{13,14},{15,0},{2,1},{4,3},... | collective-permute-start | bytes 147464 | tf_op jit(solution)/shard_map/ppermute | solution.py:26
  56.6 1.6 %collective-permute-start.6 = (bf16[48,64,128]{2,1,0:T(8,128)(2,1)}, bf16[48,64,128]{2,1,0:T(8,128)(2,1)}, u32[]{:S(2)}, u32[]{:S(2)}) collective-permute-start(bf16[48,64,128]{2,1,0:T(8,128)(2,1)} %get-tuple-element.29), channel_id=1, source_target_pairs={{1,2},{3,4},{5,6},{7,8},{9,10},{11,12},{13,14},{15,0},{2,1},{4,3},... | collective-permute-start | bytes 2359304 | tf_op jit(solution)/shard_map/ppermute | solution.py:26
  58.2 2.1 %collective-permute-done.13.cols_odd = f32[96,128]{1,0:T(8,128)S(1)} collective-permute-done((f32[96,128]{1,0:T(8,128)S(1)}, f32[96,128]{1,0:T(8,128)S(1)}, u32[]{:S(2)}, u32[]{:S(2)}) %collective-permute-start.13) | collective-permute-done | bytes 49184 | tf_op jit(solution)/shard_map/ppermute | solution.py:26
  60.3 0.2 collective-permute-done.12.cols_even
  60.5 1.6 %collective-permute-start.14 = (bf16[48,64,128]{2,1,0:T(8,128)(2,1)}, bf16[48,64,128]{2,1,0:T(8,128)(2,1)}, u32[]{:S(2)}, u32[]{:S(2)}) collective-permute-start(bf16[48,64,128]{2,1,0:T(8,128)(2,1)} %get-tuple-element.36), channel_id=1, source_target_pairs={{0,8},{1,9},{2,10},{3,11},{4,12},{5,13},{6,14},{7,15},{8,0},{9,1},... | collective-permute-start | bytes 2359304 | tf_op jit(solution)/shard_map/ppermute | solution.py:40
  62.1 4.4 %level_sums.1 = (f32[16,64,128]{2,1,0:T(8,128)}, f32[16,64,128]{2,1,0:T(8,128)}, f32[8,1,128]{2,1,0:T(1,128)}) custom-call(f32[16]{0:T(128)} %scale.5, f32[16,64,128]{2,1,0:T(8,128)} %get-tuple-element.38.rhs, f32[64,128]{1,0:T(8,128)} %diag.5, f32[64,128]{1,0:T(8,128)} %copy-done.2, f32[96,128]{1,0:T(8,128)} %copy-done.6, f32[96,128]{1,0:T(8,128)} %copy-done.5, ...), custom_call_target="tpu_custom_call" | custom-call | flops 4194304 | bytes 2097152 | tf_op jit(solution)/shard_map/level_sums/pallas_call | solution.py:388
  66.5 8.8 %all_to_all.10 = f32[8,1,128]{2,1,0:T(1,128)S(1)} all-to-all(f32[8,1,128]{2,1,0:T(1,128)} %get-tuple-element.39), channel_id=1, replica_groups=mesh['lat'=8,'lon'=16] {'lat'}, dimensions={0} | all-to-all | bytes 8192 | tf_op jit(solution)/shard_map/all_to_all | solution.py:448
  75.4 0.6 broadcast_in_dim.36
  76.0 4.1 %all-to-all-start.1 = ((f32[16,1,128]{2,1,0:T(1,128)}), f32[16,1,128]{2,1,0:T(1,128)S(1)}, u32[]{:S(2)}, u32[]{:S(2)}) async-start(f32[16,1,128]{2,1,0:T(1,128)} %broadcast_in_dim.36), calls=%async_computation.1 | async-start | bytes 16384 | tf_op jit(solution)/shard_map/all_to_all | solution.py:448
  80.1 5.0 %collective-permute-done.6.refs_3_ = bf16[48,64,128]{2,1,0:T(8,128)(2,1)} collective-permute-done((bf16[48,64,128]{2,1,0:T(8,128)(2,1)}, bf16[48,64,128]{2,1,0:T(8,128)(2,1)}, u32[]{:S(2)}, u32[]{:S(2)}) %collective-permute-start.6) | collective-permute-done | bytes 786464 | tf_op jit(solution)/shard_map/ppermute | solution.py:26
  85.1 4.5 %other_levels.1 = bf16[64,64,128]{2,1,0:T(8,128)(2,1)} custom-call(s32[1,128]{1,0:T(1,128)S(1)} %get-tuple-element.48.codes, f32[5,64,128]{2,1,0:T(8,128)S(1)} %pad_maximum_fusion.1.table, bf16[80,64,128]{2,1,0:T(8,128)(2,1)S(1)} %copy-done, ...), custom_call_target="tpu_custom_call", output_to_operand_aliasing={{}: (8, {})} | custom-call | flops 704643072 | bytes 6291456 | tf_op jit(solution)/shard_map/other_levels/pallas_call | solution.py:289
  89.6 0.6 copy-done.9
  90.2 2.4 %last_step.1 = (f32[16,64,128]{2,1,0:T(8,128)}, f32[16,64,128]{2,1,0:T(8,128)}) custom-call(f32[16]{0:T(128)} %scale.5, f32[16,1,128]{2,1,0:T(1,128)} %copy-done.9, f32[16,64,128]{2,1,0:T(8,128)} %get-tuple-element.38.rhs, f32[64,128]{1,0:T(8,128)} %diag.5, f32[16,64,128]{2,1,0:T(8,128)} %get-tuple-element.41.n0, ...), custom_call_target="tpu_custom_call", output_to_operand_aliasing={{1}: (2, {}), {0}: (4, {})} | custom-call | flops 2097152 | bytes 3145728 | tf_op jit(solution)/shard_map/last_step/pallas_call | solution.py:434
  (42 shorter events, 0.2 us)
Async XLA Ops:
  0.6 20.2 %copy-start = (bf16[80,64,128]{2,1,0:T(8,128)(2,1)S(1)}, bf16[80,64,128]{2,1,0:T(8,128)(2,1)}, u32[]{:S(2)}) copy-start(bf16[80,64,128]{2,1,0:T(8,128)(2,1)} %refs_0_.3) | copy-start | bytes 3932164
  0.6 20.2 %collective-permute-start.3 = (bf16[80,64,128]{2,1,0:T(8,128)(2,1)}, bf16[80,64,128]{2,1,0:T(8,128)(2,1)S(1)}, u32[]{:S(2)}, u32[]{:S(2)}) collective-permute-start(bf16[80,64,128]{2,1,0:T(8,128)(2,1)} %refs_0_.3), channel_id=1, source_target_pairs={{16,32},{48,64},{80,96},{32,16},{64,48},{96,80},{17,33},{49,65},{8... | collective-permute-start | bytes 3932168 | tf_op jit(solution)/shard_map/ppermute | solution.py:26
  5.4 15.5 %collective-permute-start.2 = (bf16[80,64,128]{2,1,0:T(8,128)(2,1)}, bf16[80,64,128]{2,1,0:T(8,128)(2,1)}, u32[]{:S(2)}, u32[]{:S(2)}) collective-permute-start(bf16[80,64,128]{2,1,0:T(8,128)(2,1)} %refs_0_.3), channel_id=1, source_target_pairs={{0,16},{32,48},{64,80},{96,112},{16,0},{48,32},{80,64},{112,96},{1... | collective-permute-start | bytes 3932168 | tf_op jit(solution)/shard_map/ppermute | solution.py:26
  6.3 7.2 %collective-permute-start.1 = (s32[1,128]{1,0:T(1,128)S(1)}, s32[1,128]{1,0:T(1,128)S(1)}, u32[]{:S(2)}, u32[]{:S(2)}) collective-permute-start(s32[1,128]{1,0:T(1,128)S(1)} %get-tuple-element.48.codes), channel_id=1, source_target_pairs={{1,2},{3,4},{5,6},{7,8},{9,10},{11,12},{13,14},{15,0},{2,1},{4,3},... | collective-permute-start | bytes 1544 | tf_op jit(solution)/shard_map/ppermute | solution.py:26
  12.3 2.4 %collective-permute-start = (s32[1,128]{1,0:T(1,128)S(1)}, s32[1,128]{1,0:T(1,128)S(1)}, u32[]{:S(2)}, u32[]{:S(2)}) collective-permute-start(s32[1,128]{1,0:T(1,128)S(1)} %get-tuple-element.48.codes), channel_id=1, source_target_pairs={{0,1},{2,3},{4,5},{6,7},{8,9},{10,11},{12,13},{14,15},{1,0},{3,2},... | collective-permute-start | bytes 1544 | tf_op jit(solution)/shard_map/ppermute | solution.py:26
  14.7 14.5 %collective-permute-start.5 = (bf16[33,64,128]{2,1,0:T(8,128)(2,1)S(1)}, bf16[33,64,128]{2,1,0:T(8,128)(2,1)S(1)}, u32[]{:S(2)}, u32[]{:S(2)}) collective-permute-start(bf16[33,64,128]{2,1,0:T(8,128)(2,1)S(1)} %pad_maximum_fusion), channel_id=1, source_target_pairs={{16,8},{17,9},{18,10},{19,11},{20,12},{21,13},{22,14},{23,15},{24,... | collective-permute-start | bytes 1622024 | tf_op jit(solution)/shard_map/ppermute | solution.py:40
  19.0 10.3 %collective-permute-start.4 = (bf16[33,64,128]{2,1,0:T(8,128)(2,1)S(1)}, bf16[33,64,128]{2,1,0:T(8,128)(2,1)S(1)}, u32[]{:S(2)}, u32[]{:S(2)}) collective-permute-start(bf16[33,64,128]{2,1,0:T(8,128)(2,1)S(1)} %pad_maximum_fusion), channel_id=1, source_target_pairs={{0,8},{1,9},{2,10},{3,11},{4,12},{5,13},{6,14},{7,15},{8,0},{9,1},... | collective-permute-start | bytes 1622024 | tf_op jit(solution)/shard_map/ppermute | solution.py:40
  22.7 14.3 %collective-permute-start.8 = (bf16[32,64,128]{2,1,0:T(8,128)(2,1)S(1)}, bf16[32,64,128]{2,1,0:T(8,128)(2,1)S(1)}, u32[]{:S(2)}, u32[]{:S(2)}) collective-permute-start(bf16[32,64,128]{2,1,0:T(8,128)(2,1)S(1)} %get-tuple-element.24), channel_id=1, source_target_pairs={{0,1},{2,3},{4,5},{6,7},{8,9},{10,11},{12,13},{14,15},{1,0},{3,2},... | collective-permute-start | bytes 1572872 | tf_op jit(solution)/shard_map/ppermute | solution.py:26
  24.7 8.6 %copy-start.10 = (s32[64,128]{1,0:T(8,128)S(1)}, s32[64,128]{1,0:T(8,128)}, u32[]{:S(2)}) copy-start(s32[64,128]{1,0:T(8,128)} %param.8) | copy-start | bytes 98308
  24.7 8.6 %copy-start.4 = (f32[4,64,128]{2,1,0:T(8,128)S(1)}, f32[4,64,128]{2,1,0:T(8,128)}, u32[]{:S(2)}) copy-start(f32[4,64,128]{2,1,0:T(8,128)} %param.9) | copy-start | bytes 393220
  24.7 20.0 %copy-start.1 = (f32[64,128]{1,0:T(8,128)S(1)}, f32[64,128]{1,0:T(8,128)}, u32[]{:S(2)}) copy-start(f32[64,128]{1,0:T(8,128)} %diag.5) | copy-start | bytes 98308
  24.7 20.0 %copy-start.3 = (f32[16]{0:T(128)S(1)}, f32[16]{0:T(128)}, u32[]{:S(2)}) copy-start(f32[16]{0:T(128)} %scale.5) | copy-start | bytes 196
  24.7 20.0 %collective-permute-start.9 = (bf16[32,64,128]{2,1,0:T(8,128)(2,1)S(1)}, bf16[32,64,128]{2,1,0:T(8,128)(2,1)S(1)}, u32[]{:S(2)}, u32[]{:S(2)}) collective-permute-start(bf16[32,64,128]{2,1,0:T(8,128)(2,1)S(1)} %get-tuple-element.25), channel_id=1, source_target_pairs={{1,2},{3,4},{5,6},{7,8},{9,10},{11,12},{13,14},{15,0},{2,1},{4,3},... | collective-permute-start | bytes 1572872 | tf_op jit(solution)/shard_map/ppermute | solution.py:26
  47.9 14.2 %copy-start.2 = (f32[64,128]{1,0:T(8,128)}, f32[64,128]{1,0:T(8,128)S(1)}, u32[]{:S(2)}) copy-start(f32[64,128]{1,0:T(8,128)S(1)} %get-tuple-element.33.cols) | copy-start | bytes 98308
  47.9 2.3 %collective-permute-start.10 = (f32[40,128]{1,0:T(8,128)S(1)}, f32[40,128]{1,0:T(8,128)S(1)}, u32[]{:S(2)}, u32[]{:S(2)}) collective-permute-start(f32[40,128]{1,0:T(8,128)S(1)} %get-tuple-element.34), channel_id=1, source_target_pairs={{0,16},{32,48},{64,80},{96,112},{16,0},{48,32},{80,64},{112,96},{1... | collective-permute-start | bytes 61448 | tf_op jit(solution)/shard_map/ppermute | solution.py:26
  48.3 5.1 %collective-permute-start.11 = (f32[40,128]{1,0:T(8,128)S(1)}, f32[40,128]{1,0:T(8,128)S(1)}, u32[]{:S(2)}, u32[]{:S(2)}) collective-permute-start(f32[40,128]{1,0:T(8,128)S(1)} %get-tuple-element.35), channel_id=1, source_target_pairs={{16,32},{48,64},{80,96},{32,16},{64,48},{96,80},{17,33},{49,65},{8... | collective-permute-start | bytes 61448 | tf_op jit(solution)/shard_map/ppermute | solution.py:26
  50.2 11.9 %copy-start.7 = (f32[40,128]{1,0:T(8,128)}, f32[40,128]{1,0:T(8,128)S(1)}, u32[]{:S(2)}) copy-start(f32[40,128]{1,0:T(8,128)S(1)} %collective-permute-done.10.edge_even) | copy-start | bytes 61444
  53.3 8.7 %copy-start.8 = (f32[40,128]{1,0:T(8,128)}, f32[40,128]{1,0:T(8,128)S(1)}, u32[]{:S(2)}) copy-start(f32[40,128]{1,0:T(8,128)S(1)} %collective-permute-done.11.edge_odd) | copy-start | bytes 61444
  53.4 7.0 %collective-permute-start.13 = (f32[96,128]{1,0:T(8,128)S(1)}, f32[96,128]{1,0:T(8,128)S(1)}, u32[]{:S(2)}, u32[]{:S(2)}) collective-permute-start(f32[96,128]{1,0:T(8,128)S(1)} %pad_maximum_fusion.2), channel_id=1, source_target_pairs={{1,2},{3,4},{5,6},{7,8},{9,10},{11,12},{13,14},{15,0},{2,1},{4,3},... | collective-permute-start | bytes 147464 | tf_op jit(solution)/shard_map/ppermute | solution.py:26
  56.6 3.9 %collective-permute-start.12 = (f32[96,128]{1,0:T(8,128)S(1)}, f32[96,128]{1,0:T(8,128)S(1)}, u32[]{:S(2)}, u32[]{:S(2)}) collective-permute-start(f32[96,128]{1,0:T(8,128)S(1)} %pad_maximum_fusion.2), channel_id=1, source_target_pairs={{0,1},{2,3},{4,5},{6,7},{8,9},{10,11},{12,13},{14,15},{1,0},{3,2},... | collective-permute-start | bytes 147464 | tf_op jit(solution)/shard_map/ppermute | solution.py:26
  56.6 28.5 %collective-permute-start.6 = (bf16[48,64,128]{2,1,0:T(8,128)(2,1)}, bf16[48,64,128]{2,1,0:T(8,128)(2,1)}, u32[]{:S(2)}, u32[]{:S(2)}) collective-permute-start(bf16[48,64,128]{2,1,0:T(8,128)(2,1)} %get-tuple-element.29), channel_id=1, source_target_pairs={{1,2},{3,4},{5,6},{7,8},{9,10},{11,12},{13,14},{15,0},{2,1},{4,3},... | collective-permute-start | bytes 2359304 | tf_op jit(solution)/shard_map/ppermute | solution.py:26
  58.2 26.9 %collective-permute-start.7 = (bf16[48,64,128]{2,1,0:T(8,128)(2,1)}, bf16[48,64,128]{2,1,0:T(8,128)(2,1)}, u32[]{:S(2)}, u32[]{:S(2)}) collective-permute-start(bf16[48,64,128]{2,1,0:T(8,128)(2,1)} %get-tuple-element.30), channel_id=1, source_target_pairs={{0,1},{2,3},{4,5},{6,7},{8,9},{10,11},{12,13},{14,15},{1,0},{3,2},... | collective-permute-start | bytes 2359304 | tf_op jit(solution)/shard_map/ppermute | solution.py:26
  60.3 1.7 %copy-start.5 = (f32[96,128]{1,0:T(8,128)}, f32[96,128]{1,0:T(8,128)S(1)}, u32[]{:S(2)}) copy-start(f32[96,128]{1,0:T(8,128)S(1)} %collective-permute-done.13.cols_odd) | copy-start | bytes 147460
  60.5 1.6 %copy-start.6 = (f32[96,128]{1,0:T(8,128)}, f32[96,128]{1,0:T(8,128)S(1)}, u32[]{:S(2)}) copy-start(f32[96,128]{1,0:T(8,128)S(1)} %collective-permute-done.12.cols_even) | copy-start | bytes 147460
  60.5 24.6 %collective-permute-start.14 = (bf16[48,64,128]{2,1,0:T(8,128)(2,1)}, bf16[48,64,128]{2,1,0:T(8,128)(2,1)}, u32[]{:S(2)}, u32[]{:S(2)}) collective-permute-start(bf16[48,64,128]{2,1,0:T(8,128)(2,1)} %get-tuple-element.36), channel_id=1, source_target_pairs={{0,8},{1,9},{2,10},{3,11},{4,12},{5,13},{6,14},{7,15},{8,0},{9,1},... | collective-permute-start | bytes 2359304 | tf_op jit(solution)/shard_map/ppermute | solution.py:40
  76.0 13.6 %all-to-all-start.1 = ((f32[16,1,128]{2,1,0:T(1,128)}), f32[16,1,128]{2,1,0:T(1,128)S(1)}, u32[]{:S(2)}, u32[]{:S(2)}) async-start(f32[16,1,128]{2,1,0:T(1,128)} %broadcast_in_dim.36), calls=%async_computation.1 | async-start | bytes 16384 | tf_op jit(solution)/shard_map/all_to_all | solution.py:448
  89.6 0.6 copy-start.9

commit v6 on v5

--- a/solution.py
+++ b/solution.py
@@ -454,7 +454,7 @@
     bands = (fields,) + swaps(fields, fields, "lat")
     lists = swaps(codes, codes, "lon")
     rows = jnp.broadcast_to(codes.astype(BF16)[None], (1, 64, LANES))
-    first = after(jnp.concatenate([fields[32:48], fields[64:80], rows], axis=0), *lists)
+    first = after(jnp.concatenate([fields[32:48], fields[64:80], rows], axis=0), lists[0])
     first_far = (from_far(first), from_far_next(first))
     first_out = pack(lists, bands, 2, lambda g: 2 + 2 * g)
     first_slots = swaps(*first_out, "lon")

time: 93.1 us -> 92.5 us (level)
  waiting for transfers between devices: 24.2 us -> 14.7 us
  starting transfers between devices: 35.1 us -> 42.4 us
  blocking collectives: 8.83 us -> 10.1 us
    ppermute x12, waiting for transfers between devices: 24.2 us -> 12.8 us  [swap(): return lax.ppermute(block, axis, ends + [(b, a) for a, b in ends])]
    ppermute x12, starting transfers between devices: 24.6 us -> 29.7 us  [swap(): return lax.ppermute(block, axis, ends + [(b, a) for a, b in ends])]
    all_to_all x1, waiting for transfers between devices: 0.01 us -> 1.85 us  [exchange(): return lax.all_to_all(parts, axis, split_axis=0, concat_axis=0, tiled=True)]
    ppermute x3, starting transfers between devices: 6.49 us -> 8.03 us  [from_pole(): return lax.ppermute(block, ('lat', 'lon'), pairs)]
    all_to_all x1, blocking collectives: 8.83 us -> 10.1 us  [exchange(): return lax.all_to_all(parts, axis, split_axis=0, concat_axis=0, tiled=True)]
  transfers between devices with their start and end apart: 16 -> 16, of which waited for: 8 -> 5; matrix products, arithmetic and copies ran while one was open for 3% -> 3% of each run, Pallas kernels for 16% -> 16%
where the time goes in v6:
time: 92.5 us; the launch traced here: 91.6 us
  starting transfers between devices  42.4 us (46%)
  Pallas kernels  20.4 us (22%)
  waiting for transfers between devices  14.7 us (16%)
  blocking collectives  10.1 us (11%)
  local copies, waits for them, and re-layouts  3.07 us (3%)
    ppermute x12, starting transfers between devices, swap(): return lax.ppermute(block, axis, ends + [(b, a) for a, b in ends])  29.7 us
    ppermute x12, waiting for transfers between devices, swap(): return lax.ppermute(block, axis, ends + [(b, a) for a, b in ends])  12.8 us
    all_to_all x1, blocking collectives, exchange(): return lax.all_to_all(parts, axis, split_axis=0, concat_axis=0, tiled=True)  10.1 us
    ppermute x3, starting transfers between devices, from_pole(): return lax.ppermute(block, ('lat', 'lon'), pairs)  8.03 us
    pallas_call x2, Pallas kernels, pack(): pl.pallas_call(functools.partial(pack_kernel, count), grid=(blocks,), in_...  5.85 us
    all_to_all x1, starting transfers between devices, exchange(): return lax.all_to_all(parts, axis, split_axis=0, concat_axis=0, tiled=True)  4.73 us
    pallas_call x1, Pallas kernels, other_levels(): pl.pallas_call(other_kernel, grid=(3,), in_specs=[flat(1), TABLE] + [leve...  4.52 us
    pallas_call x1, Pallas kernels, level_sums(): pl.pallas_call(sum_kernel, in_specs=[SMEM] + [VMEM] * 7, out_specs=[VMEM]...  4.44 us
  transfers between devices with their start and end apart: 16, of which 5 were waited for; matrix products, arithmetic and copies ran while one was open for 3% of the time, Pallas kernels for 16%

profile of v6, /device:TPU:1, one launch (start us, length us, event | category | flops | bytes accessed | tf_op | source)
XLA Modules:
  0.0 91.6 jit_solution(17458231721013354221)
XLA Ops:
  0.6 4.7 %collective-permute-start.3 = (bf16[80,64,128]{2,1,0:T(8,128)(2,1)}, bf16[80,64,128]{2,1,0:T(8,128)(2,1)S(1)}, u32[]{:S(2)}, u32[]{:S(2)}) collective-permute-start(bf16[80,64,128]{2,1,0:T(8,128)(2,1)} %refs_0_.3), channel_id=1, source_target_pairs={{16,32},{48,64},{80,96},{32,16},{64,48},{96,80},{17,33},{49,65},{8... | collective-permute-start | bytes 3932168 | tf_op jit(solution)/shard_map/ppermute | solution.py:26
  5.4 0.1 collective-permute-start.2
  5.5 0.8 reshape.295
  6.3 1.7 %collective-permute-start = (s32[1,128]{1,0:T(1,128)S(1)}, s32[1,128]{1,0:T(1,128)S(1)}, u32[]{:S(2)}, u32[]{:S(2)}) collective-permute-start(s32[1,128]{1,0:T(1,128)S(1)} %get-tuple-element.48.codes), channel_id=1, source_target_pairs={{0,1},{2,3},{4,5},{6,7},{8,9},{10,11},{12,13},{14,15},{1,0},{3,2},... | collective-permute-start | bytes 1544 | tf_op jit(solution)/shard_map/ppermute | solution.py:26
  8.0 1.1 %fusion.4 = (bf16[16,64,128]{2,1,0:T(8,128)(2,1)S(1)}, bf16[16,64,128]{2,1,0:T(8,128)(2,1)S(1)}) fusion(bf16[80,64,128]{2,1,0:T(8,128)(2,1)} %refs_0_.3), kind=kLoop, calls=%fused_computation.24 | loop fusion | bytes 1048576 | tf_op jit(solution)/shard_map/slice | solution.py:457
  9.1 0.1 pad_maximum_fusion
  9.2 5.8 %collective-permute-start.5 = (bf16[33,64,128]{2,1,0:T(8,128)(2,1)S(1)}, bf16[33,64,128]{2,1,0:T(8,128)(2,1)S(1)}, u32[]{:S(2)}, u32[]{:S(2)}) collective-permute-start(bf16[33,64,128]{2,1,0:T(8,128)(2,1)S(1)} %pad_maximum_fusion), channel_id=1, source_target_pairs={{16,8},{17,9},{18,10},{19,11},{20,12},{21,13},{22,14},{23,15},{24,... | collective-permute-start | bytes 1622024 | tf_op jit(solution)/shard_map/ppermute | solution.py:40
  15.0 0.7 collective-permute-start.4
  15.7 4.4 %collective-permute-start.1 = (s32[1,128]{1,0:T(1,128)S(1)}, s32[1,128]{1,0:T(1,128)S(1)}, u32[]{:S(2)}, u32[]{:S(2)}) collective-permute-start(s32[1,128]{1,0:T(1,128)S(1)} %get-tuple-element.48.codes), channel_id=1, source_target_pairs={{1,2},{3,4},{5,6},{7,8},{9,10},{11,12},{13,14},{15,0},{2,1},{4,3},... | collective-permute-start | bytes 1544 | tf_op jit(solution)/shard_map/ppermute | solution.py:26
  20.1 1.4 %collective-permute-done.1.refs_1_ = s32[1,128]{1,0:T(1,128)S(1)} collective-permute-done((s32[1,128]{1,0:T(1,128)S(1)}, s32[1,128]{1,0:T(1,128)S(1)}, u32[]{:S(2)}, u32[]{:S(2)}) %collective-permute-start.1) | collective-permute-done | bytes 544 | tf_op jit(solution)/shard_map/ppermute | solution.py:26
  21.5 1.8 %pack.2 = (bf16[32,64,128]{2,1,0:T(8,128)(2,1)S(1)}, bf16[32,64,128]{2,1,0:T(8,128)(2,1)S(1)}) custom-call(s32[1,128]{1,0:T(1,128)S(1)} %collective-permute-done.refs_0_, s32[1,128]{1,0:T(1,128)S(1)} %collective-permute-done.1.refs_1_, bf16[80,64,128]{2,1,0:T(8,128)(2,1)S(1)} %copy-done, ...), custom_call_target="tpu_custom_call" | custom-call | flops 301989888 | bytes 2621440 | tf_op jit(solution)/shard_map/pack/pallas_call | solution.py:122
  23.4 1.4 %collective-permute-start.8 = (bf16[32,64,128]{2,1,0:T(8,128)(2,1)S(1)}, bf16[32,64,128]{2,1,0:T(8,128)(2,1)S(1)}, u32[]{:S(2)}, u32[]{:S(2)}) collective-permute-start(bf16[32,64,128]{2,1,0:T(8,128)(2,1)S(1)} %get-tuple-element.24), channel_id=1, source_target_pairs={{0,1},{2,3},{4,5},{6,7},{8,9},{10,11},{12,13},{14,15},{1,0},{3,2},... | collective-permute-start | bytes 1572872 | tf_op jit(solution)/shard_map/ppermute | solution.py:26
  24.7 4.5 %collective-permute-start.9 = (bf16[32,64,128]{2,1,0:T(8,128)(2,1)S(1)}, bf16[32,64,128]{2,1,0:T(8,128)(2,1)S(1)}, u32[]{:S(2)}, u32[]{:S(2)}) collective-permute-start(bf16[32,64,128]{2,1,0:T(8,128)(2,1)S(1)} %get-tuple-element.25), channel_id=1, source_target_pairs={{1,2},{3,4},{5,6},{7,8},{9,10},{11,12},{13,14},{15,0},{2,1},{4,3},... | collective-permute-start | bytes 1572872 | tf_op jit(solution)/shard_map/ppermute | solution.py:26
  29.2 4.0 %pack.3 = (bf16[48,64,128]{2,1,0:T(8,128)(2,1)}, bf16[48,64,128]{2,1,0:T(8,128)(2,1)}, bf16[48,64,128]{2,1,0:T(8,128)(2,1)}) custom-call(s32[1,128]{1,0:T(1,128)S(1)} %collective-permute-done.refs_0_, s32[1,128]{1,0:T(1,128)S(1)} %collective-permute-done.1.refs_1_, bf16[33,64,128]{2,1,0:T(8,128)(2,1)S(1)} %collective-permute-done.4.refs_2_.refs_5_.refs_12_, ...), custom_call_target="tpu_custom_call" | custom-call | flops 452984832 | bytes 3932160 | tf_op jit(solution)/shard_map/pack/pallas_call | solution.py:122
  33.3 2.2 %collective-permute-done.8.refs_3_.refs_10_ = bf16[32,64,128]{2,1,0:T(8,128)(2,1)S(1)} collective-permute-done((bf16[32,64,128]{2,1,0:T(8,128)(2,1)S(1)}, bf16[32,64,128]{2,1,0:T(8,128)(2,1)S(1)}, u32[]{:S(2)}, u32[]{:S(2)}) %collective-permute-start.8) | collective-permute-done | bytes 524320 | tf_op jit(solution)/shard_map/ppermute | solution.py:26
  35.5 6.5 %collective-permute-done.9.refs_4_.refs_11_ = bf16[32,64,128]{2,1,0:T(8,128)(2,1)S(1)} collective-permute-done((bf16[32,64,128]{2,1,0:T(8,128)(2,1)S(1)}, bf16[32,64,128]{2,1,0:T(8,128)(2,1)S(1)}, u32[]{:S(2)}, u32[]{:S(2)}) %collective-permute-start.9) | collective-permute-done | bytes 524320 | tf_op jit(solution)/shard_map/ppermute | solution.py:26
  42.0 3.2 %first_levels.1 = (bf16[64,64,128]{2,1,0:T(8,128)(2,1)}, f32[16,64,128]{2,1,0:T(8,128)}, f32[64,128]{1,0:T(8,128)S(1)}, f32[40,128]{1,0:T(8,128)S(1)}, f32[40,128]{1,0:T(8,128)S(1)}) custom-call(f32[16]{0:T(128)S(1)} %copy-done.3, s32[1,128]{1,0:T(1,128)S(1)} %get-tuple-element.48.codes, f32[5,64,128]{2,1,0:T(8,128)S(1)} %pad_maximum_fusion.1.table, ...), custom_call_target="tpu_custom_call" | custom-call | flops 469762048 | bytes 6291456 | tf_op jit(solution)/shard_map/first_levels/pallas_call | solution.py:253
  45.1 1.1 %collective-permute-start.10 = (f32[40,128]{1,0:T(8,128)S(1)}, f32[40,128]{1,0:T(8,128)S(1)}, u32[]{:S(2)}, u32[]{:S(2)}) collective-permute-start(f32[40,128]{1,0:T(8,128)S(1)} %get-tuple-element.34), channel_id=1, source_target_pairs={{0,16},{32,48},{64,80},{96,112},{16,0},{48,32},{80,64},{112,96},{1... | collective-permute-start | bytes 61448 | tf_op jit(solution)/shard_map/ppermute | solution.py:26
  46.3 2.3 %collective-permute-start.11 = (f32[40,128]{1,0:T(8,128)S(1)}, f32[40,128]{1,0:T(8,128)S(1)}, u32[]{:S(2)}, u32[]{:S(2)}) collective-permute-start(f32[40,128]{1,0:T(8,128)S(1)} %get-tuple-element.35), channel_id=1, source_target_pairs={{16,32},{48,64},{80,96},{32,16},{64,48},{96,80},{17,33},{49,65},{8... | collective-permute-start | bytes 61448 | tf_op jit(solution)/shard_map/ppermute | solution.py:26
  48.6 2.7 %collective-permute-done.11.edge_odd = f32[40,128]{1,0:T(8,128)S(1)} collective-permute-done((f32[40,128]{1,0:T(8,128)S(1)}, f32[40,128]{1,0:T(8,128)S(1)}, u32[]{:S(2)}, u32[]{:S(2)}) %collective-permute-start.11) | collective-permute-done | bytes 20512 | tf_op jit(solution)/shard_map/ppermute | solution.py:26
  51.4 3.9 %collective-permute-start.13 = (f32[96,128]{1,0:T(8,128)S(1)}, f32[96,128]{1,0:T(8,128)S(1)}, u32[]{:S(2)}, u32[]{:S(2)}) collective-permute-start(f32[96,128]{1,0:T(8,128)S(1)} %pad_maximum_fusion.2), channel_id=1, source_target_pairs={{1,2},{3,4},{5,6},{7,8},{9,10},{11,12},{13,14},{15,0},{2,1},{4,3},... | collective-permute-start | bytes 147464 | tf_op jit(solution)/shard_map/ppermute | solution.py:26
  55.3 2.8 %collective-permute-start.6 = (bf16[48,64,128]{2,1,0:T(8,128)(2,1)}, bf16[48,64,128]{2,1,0:T(8,128)(2,1)}, u32[]{:S(2)}, u32[]{:S(2)}) collective-permute-start(bf16[48,64,128]{2,1,0:T(8,128)(2,1)} %get-tuple-element.29), channel_id=1, source_target_pairs={{1,2},{3,4},{5,6},{7,8},{9,10},{11,12},{13,14},{15,0},{2,1},{4,3},... | collective-permute-start | bytes 2359304 | tf_op jit(solution)/shard_map/ppermute | solution.py:26
  58.0 2.7 %collective-permute-start.7 = (bf16[48,64,128]{2,1,0:T(8,128)(2,1)}, bf16[48,64,128]{2,1,0:T(8,128)(2,1)}, u32[]{:S(2)}, u32[]{:S(2)}) collective-permute-start(bf16[48,64,128]{2,1,0:T(8,128)(2,1)} %get-tuple-element.30), channel_id=1, source_target_pairs={{0,1},{2,3},{4,5},{6,7},{8,9},{10,11},{12,13},{14,15},{1,0},{3,2},... | collective-permute-start | bytes 2359304 | tf_op jit(solution)/shard_map/ppermute | solution.py:26
  60.8 1.6 %collective-permute-start.14 = (bf16[48,64,128]{2,1,0:T(8,128)(2,1)}, bf16[48,64,128]{2,1,0:T(8,128)(2,1)}, u32[]{:S(2)}, u32[]{:S(2)}) collective-permute-start(bf16[48,64,128]{2,1,0:T(8,128)(2,1)} %get-tuple-element.36), channel_id=1, source_target_pairs={{0,8},{1,9},{2,10},{3,11},{4,12},{5,13},{6,14},{7,15},{8,0},{9,1},... | collective-permute-start | bytes 2359304 | tf_op jit(solution)/shard_map/ppermute | solution.py:40
  62.4 4.4 %level_sums.1 = (f32[16,64,128]{2,1,0:T(8,128)}, f32[16,64,128]{2,1,0:T(8,128)}, f32[8,1,128]{2,1,0:T(1,128)}) custom-call(f32[16]{0:T(128)} %scale.5, f32[16,64,128]{2,1,0:T(8,128)} %get-tuple-element.38.rhs, f32[64,128]{1,0:T(8,128)} %diag.5, f32[64,128]{1,0:T(8,128)} %copy-done.2, f32[96,128]{1,0:T(8,128)} %copy-done.6, f32[96,128]{1,0:T(8,128)} %copy-done.5, ...), custom_call_target="tpu_custom_call" | custom-call | flops 4194304 | bytes 2097152 | tf_op jit(solution)/shard_map/level_sums/pallas_call | solution.py:388
  66.8 10.1 %all_to_all.10 = f32[8,1,128]{2,1,0:T(1,128)S(1)} all-to-all(f32[8,1,128]{2,1,0:T(1,128)} %get-tuple-element.39), channel_id=1, replica_groups=mesh['lat'=8,'lon'=16] {'lat'}, dimensions={0} | all-to-all | bytes 8192 | tf_op jit(solution)/shard_map/all_to_all | solution.py:448
  76.9 0.6 broadcast_in_dim.36
  77.5 4.7 %all-to-all-start.1 = ((f32[16,1,128]{2,1,0:T(1,128)}), f32[16,1,128]{2,1,0:T(1,128)S(1)}, u32[]{:S(2)}, u32[]{:S(2)}) async-start(f32[16,1,128]{2,1,0:T(1,128)} %broadcast_in_dim.36), calls=%async_computation.1 | async-start | bytes 16384 | tf_op jit(solution)/shard_map/all_to_all | solution.py:448
  82.3 4.5 %other_levels.1 = bf16[64,64,128]{2,1,0:T(8,128)(2,1)} custom-call(s32[1,128]{1,0:T(1,128)S(1)} %get-tuple-element.48.codes, f32[5,64,128]{2,1,0:T(8,128)S(1)} %pad_maximum_fusion.1.table, bf16[80,64,128]{2,1,0:T(8,128)(2,1)S(1)} %copy-done, ...), custom_call_target="tpu_custom_call", output_to_operand_aliasing={{}: (8, {})} | custom-call | flops 704643072 | bytes 6291456 | tf_op jit(solution)/shard_map/other_levels/pallas_call | solution.py:289
  86.8 1.8 %all-to-all-done.1.parts = f32[16,1,128]{2,1,0:T(1,128)S(1)} async-done(((f32[16,1,128]{2,1,0:T(1,128)}), f32[16,1,128]{2,1,0:T(1,128)S(1)}, u32[]{:S(2)}, u32[]{:S(2)}) %all-to-all-start.1) | async-done | bytes 8224 | tf_op jit(solution)/shard_map/all_to_all | solution.py:448
  88.7 0.6 copy-done.9
  89.3 2.4 %last_step.1 = (f32[16,64,128]{2,1,0:T(8,128)}, f32[16,64,128]{2,1,0:T(8,128)}) custom-call(f32[16]{0:T(128)} %scale.5, f32[16,1,128]{2,1,0:T(1,128)} %copy-done.9, f32[16,64,128]{2,1,0:T(8,128)} %get-tuple-element.38.rhs, f32[64,128]{1,0:T(8,128)} %diag.5, f32[16,64,128]{2,1,0:T(8,128)} %get-tuple-element.41.n0, ...), custom_call_target="tpu_custom_call", output_to_operand_aliasing={{1}: (2, {}), {0}: (4, {})} | custom-call | flops 2097152 | bytes 3145728 | tf_op jit(solution)/shard_map/last_step/pallas_call | solution.py:434
  (42 shorter events, 0.2 us)
Async XLA Ops:
  0.6 20.9 %copy-start = (bf16[80,64,128]{2,1,0:T(8,128)(2,1)S(1)}, bf16[80,64,128]{2,1,0:T(8,128)(2,1)}, u32[]{:S(2)}) copy-start(bf16[80,64,128]{2,1,0:T(8,128)(2,1)} %refs_0_.3) | copy-start | bytes 3932164
  0.6 20.9 %collective-permute-start.3 = (bf16[80,64,128]{2,1,0:T(8,128)(2,1)}, bf16[80,64,128]{2,1,0:T(8,128)(2,1)S(1)}, u32[]{:S(2)}, u32[]{:S(2)}) collective-permute-start(bf16[80,64,128]{2,1,0:T(8,128)(2,1)} %refs_0_.3), channel_id=1, source_target_pairs={{16,32},{48,64},{80,96},{32,16},{64,48},{96,80},{17,33},{49,65},{8... | collective-permute-start | bytes 3932168 | tf_op jit(solution)/shard_map/ppermute | solution.py:26
  5.4 16.1 %collective-permute-start.2 = (bf16[80,64,128]{2,1,0:T(8,128)(2,1)}, bf16[80,64,128]{2,1,0:T(8,128)(2,1)}, u32[]{:S(2)}, u32[]{:S(2)}) collective-permute-start(bf16[80,64,128]{2,1,0:T(8,128)(2,1)} %refs_0_.3), channel_id=1, source_target_pairs={{0,16},{32,48},{64,80},{96,112},{16,0},{48,32},{80,64},{112,96},{1... | collective-permute-start | bytes 3932168 | tf_op jit(solution)/shard_map/ppermute | solution.py:26
  6.3 2.9 %collective-permute-start = (s32[1,128]{1,0:T(1,128)S(1)}, s32[1,128]{1,0:T(1,128)S(1)}, u32[]{:S(2)}, u32[]{:S(2)}) collective-permute-start(s32[1,128]{1,0:T(1,128)S(1)} %get-tuple-element.48.codes), channel_id=1, source_target_pairs={{0,1},{2,3},{4,5},{6,7},{8,9},{10,11},{12,13},{14,15},{1,0},{3,2},... | collective-permute-start | bytes 1544 | tf_op jit(solution)/shard_map/ppermute | solution.py:26
  9.2 20.1 %collective-permute-start.5 = (bf16[33,64,128]{2,1,0:T(8,128)(2,1)S(1)}, bf16[33,64,128]{2,1,0:T(8,128)(2,1)S(1)}, u32[]{:S(2)}, u32[]{:S(2)}) collective-permute-start(bf16[33,64,128]{2,1,0:T(8,128)(2,1)S(1)} %pad_maximum_fusion), channel_id=1, source_target_pairs={{16,8},{17,9},{18,10},{19,11},{20,12},{21,13},{22,14},{23,15},{24,... | collective-permute-start | bytes 1622024 | tf_op jit(solution)/shard_map/ppermute | solution.py:40
  15.0 14.3 %collective-permute-start.4 = (bf16[33,64,128]{2,1,0:T(8,128)(2,1)S(1)}, bf16[33,64,128]{2,1,0:T(8,128)(2,1)S(1)}, u32[]{:S(2)}, u32[]{:S(2)}) collective-permute-start(bf16[33,64,128]{2,1,0:T(8,128)(2,1)S(1)} %pad_maximum_fusion), channel_id=1, source_target_pairs={{0,8},{1,9},{2,10},{3,11},{4,12},{5,13},{6,14},{7,15},{8,0},{9,1},... | collective-permute-start | bytes 1622024 | tf_op jit(solution)/shard_map/ppermute | solution.py:40
  15.7 5.8 %collective-permute-start.1 = (s32[1,128]{1,0:T(1,128)S(1)}, s32[1,128]{1,0:T(1,128)S(1)}, u32[]{:S(2)}, u32[]{:S(2)}) collective-permute-start(s32[1,128]{1,0:T(1,128)S(1)} %get-tuple-element.48.codes), channel_id=1, source_target_pairs={{1,2},{3,4},{5,6},{7,8},{9,10},{11,12},{13,14},{15,0},{2,1},{4,3},... | collective-permute-start | bytes 1544 | tf_op jit(solution)/shard_map/ppermute | solution.py:26
  23.4 12.1 %collective-permute-start.8 = (bf16[32,64,128]{2,1,0:T(8,128)(2,1)S(1)}, bf16[32,64,128]{2,1,0:T(8,128)(2,1)S(1)}, u32[]{:S(2)}, u32[]{:S(2)}) collective-permute-start(bf16[32,64,128]{2,1,0:T(8,128)(2,1)S(1)} %get-tuple-element.24), channel_id=1, source_target_pairs={{0,1},{2,3},{4,5},{6,7},{8,9},{10,11},{12,13},{14,15},{1,0},{3,2},... | collective-permute-start | bytes 1572872 | tf_op jit(solution)/shard_map/ppermute | solution.py:26
  24.7 8.6 %copy-start.10 = (s32[64,128]{1,0:T(8,128)S(1)}, s32[64,128]{1,0:T(8,128)}, u32[]{:S(2)}) copy-start(s32[64,128]{1,0:T(8,128)} %param.8) | copy-start | bytes 98308
  24.7 8.6 %copy-start.4 = (f32[4,64,128]{2,1,0:T(8,128)S(1)}, f32[4,64,128]{2,1,0:T(8,128)}, u32[]{:S(2)}) copy-start(f32[4,64,128]{2,1,0:T(8,128)} %param.9) | copy-start | bytes 393220
  24.7 17.2 %copy-start.1 = (f32[64,128]{1,0:T(8,128)S(1)}, f32[64,128]{1,0:T(8,128)}, u32[]{:S(2)}) copy-start(f32[64,128]{1,0:T(8,128)} %diag.5) | copy-start | bytes 98308
  24.7 17.2 %copy-start.3 = (f32[16]{0:T(128)S(1)}, f32[16]{0:T(128)}, u32[]{:S(2)}) copy-start(f32[16]{0:T(128)} %scale.5) | copy-start | bytes 196
  24.7 17.2 %collective-permute-start.9 = (bf16[32,64,128]{2,1,0:T(8,128)(2,1)S(1)}, bf16[32,64,128]{2,1,0:T(8,128)(2,1)S(1)}, u32[]{:S(2)}, u32[]{:S(2)}) collective-permute-start(bf16[32,64,128]{2,1,0:T(8,128)(2,1)S(1)} %get-tuple-element.25), channel_id=1, source_target_pairs={{1,2},{3,4},{5,6},{7,8},{9,10},{11,12},{13,14},{15,0},{2,1},{4,3},... | collective-permute-start | bytes 1572872 | tf_op jit(solution)/shard_map/ppermute | solution.py:26
  45.1 17.2 %copy-start.2 = (f32[64,128]{1,0:T(8,128)}, f32[64,128]{1,0:T(8,128)S(1)}, u32[]{:S(2)}) copy-start(f32[64,128]{1,0:T(8,128)S(1)} %get-tuple-element.33.cols) | copy-start | bytes 98308
  45.1 3.5 %collective-permute-start.10 = (f32[40,128]{1,0:T(8,128)S(1)}, f32[40,128]{1,0:T(8,128)S(1)}, u32[]{:S(2)}, u32[]{:S(2)}) collective-permute-start(f32[40,128]{1,0:T(8,128)S(1)} %get-tuple-element.34), channel_id=1, source_target_pairs={{0,16},{32,48},{64,80},{96,112},{16,0},{48,32},{80,64},{112,96},{1... | collective-permute-start | bytes 61448 | tf_op jit(solution)/shard_map/ppermute | solution.py:26
  46.3 5.1 %collective-permute-start.11 = (f32[40,128]{1,0:T(8,128)S(1)}, f32[40,128]{1,0:T(8,128)S(1)}, u32[]{:S(2)}, u32[]{:S(2)}) collective-permute-start(f32[40,128]{1,0:T(8,128)S(1)} %get-tuple-element.35), channel_id=1, source_target_pairs={{16,32},{48,64},{80,96},{32,16},{64,48},{96,80},{17,33},{49,65},{8... | collective-permute-start | bytes 61448 | tf_op jit(solution)/shard_map/ppermute | solution.py:26
  48.6 13.7 %copy-start.7 = (f32[40,128]{1,0:T(8,128)}, f32[40,128]{1,0:T(8,128)S(1)}, u32[]{:S(2)}) copy-start(f32[40,128]{1,0:T(8,128)S(1)} %collective-permute-done.10.edge_even) | copy-start | bytes 61444
  51.3 11.0 %copy-start.8 = (f32[40,128]{1,0:T(8,128)}, f32[40,128]{1,0:T(8,128)S(1)}, u32[]{:S(2)}) copy-start(f32[40,128]{1,0:T(8,128)S(1)} %collective-permute-done.11.edge_odd) | copy-start | bytes 61444
  51.4 9.4 %collective-permute-start.13 = (f32[96,128]{1,0:T(8,128)S(1)}, f32[96,128]{1,0:T(8,128)S(1)}, u32[]{:S(2)}, u32[]{:S(2)}) collective-permute-start(f32[96,128]{1,0:T(8,128)S(1)} %pad_maximum_fusion.2), channel_id=1, source_target_pairs={{1,2},{3,4},{5,6},{7,8},{9,10},{11,12},{13,14},{15,0},{2,1},{4,3},... | collective-permute-start | bytes 147464 | tf_op jit(solution)/shard_map/ppermute | solution.py:26
  55.2 5.5 %collective-permute-start.12 = (f32[96,128]{1,0:T(8,128)S(1)}, f32[96,128]{1,0:T(8,128)S(1)}, u32[]{:S(2)}, u32[]{:S(2)}) collective-permute-start(f32[96,128]{1,0:T(8,128)S(1)} %pad_maximum_fusion.2), channel_id=1, source_target_pairs={{0,1},{2,3},{4,5},{6,7},{8,9},{10,11},{12,13},{14,15},{1,0},{3,2},... | collective-permute-start | bytes 147464 | tf_op jit(solution)/shard_map/ppermute | solution.py:26
  55.3 27.0 %collective-permute-start.6 = (bf16[48,64,128]{2,1,0:T(8,128)(2,1)}, bf16[48,64,128]{2,1,0:T(8,128)(2,1)}, u32[]{:S(2)}, u32[]{:S(2)}) collective-permute-start(bf16[48,64,128]{2,1,0:T(8,128)(2,1)} %get-tuple-element.29), channel_id=1, source_target_pairs={{1,2},{3,4},{5,6},{7,8},{9,10},{11,12},{13,14},{15,0},{2,1},{4,3},... | collective-permute-start | bytes 2359304 | tf_op jit(solution)/shard_map/ppermute | solution.py:26
  58.0 24.3 %collective-permute-start.7 = (bf16[48,64,128]{2,1,0:T(8,128)(2,1)}, bf16[48,64,128]{2,1,0:T(8,128)(2,1)}, u32[]{:S(2)}, u32[]{:S(2)}) collective-permute-start(bf16[48,64,128]{2,1,0:T(8,128)(2,1)} %get-tuple-element.30), channel_id=1, source_target_pairs={{0,1},{2,3},{4,5},{6,7},{8,9},{10,11},{12,13},{14,15},{1,0},{3,2},... | collective-permute-start | bytes 2359304 | tf_op jit(solution)/shard_map/ppermute | solution.py:26
  60.8 1.6 %copy-start.5 = (f32[96,128]{1,0:T(8,128)}, f32[96,128]{1,0:T(8,128)S(1)}, u32[]{:S(2)}) copy-start(f32[96,128]{1,0:T(8,128)S(1)} %collective-permute-done.13.cols_odd) | copy-start | bytes 147460
  60.8 1.6 %copy-start.6 = (f32[96,128]{1,0:T(8,128)}, f32[96,128]{1,0:T(8,128)S(1)}, u32[]{:S(2)}) copy-start(f32[96,128]{1,0:T(8,128)S(1)} %collective-permute-done.12.cols_even) | copy-start | bytes 147460
  60.8 21.5 %collective-permute-start.14 = (bf16[48,64,128]{2,1,0:T(8,128)(2,1)}, bf16[48,64,128]{2,1,0:T(8,128)(2,1)}, u32[]{:S(2)}, u32[]{:S(2)}) collective-permute-start(bf16[48,64,128]{2,1,0:T(8,128)(2,1)} %get-tuple-element.36), channel_id=1, source_target_pairs={{0,8},{1,9},{2,10},{3,11},{4,12},{5,13},{6,14},{7,15},{8,0},{9,1},... | collective-permute-start | bytes 2359304 | tf_op jit(solution)/shard_map/ppermute | solution.py:40
  77.5 11.1 %all-to-all-start.1 = ((f32[16,1,128]{2,1,0:T(1,128)}), f32[16,1,128]{2,1,0:T(1,128)S(1)}, u32[]{:S(2)}, u32[]{:S(2)}) async-start(f32[16,1,128]{2,1,0:T(1,128)} %broadcast_in_dim.36), calls=%async_computation.1 | async-start | bytes 16384 | tf_op jit(solution)/shard_map/all_to_all | solution.py:448
  88.7 0.6 copy-start.9
